TPU v7x, 32 devices: a whole 2x2x4 slice. The times are simulated.
32 devices in a mesh: map: 8 (over z, core), layer: 4 (over y, x).
Axes of the slice: x: 2, y: 2, z: 4, core: 2. Of those that a mesh axis runs over, the one named last changes fastest.
Arguments:
- velocity_init: float32 [2, 16, 16, 1024], P(None, 'layer', 'map'), may hold values from -4 to 4
- driving: float32 [2, 16, 1024], P(None, 'map', 'layer'), may hold values from -80 to 80
- observed: float32 [2, 16, 1024], P(None, 'map', 'layer'), may hold values from -4 to 4
- log_friction: float32 [16, 1024], P('map', 'layer'), may hold values from -1 to 1.5
- ice_mask: int32 [16, 1024], P('map', 'layer'), may hold values from 0 to 2
Outputs:
- velocity: float32 [2, 16, 16, 1024], P(None, 'layer', 'map')
- friction_new: float32 [16, 1024], P('map', 'layer')
- misfit: float32 [], replicated
All inputs are finite; a program needn't handle non-finite values.
Results may differ from a plain program's by a relative error of at most 0.0003.
Values sent between devices are 32-bit elements; how exact they have to be, the bound alone decides.
No kernel may reach another device: no remote copies, remote signals or barrier semaphores. Data moves between devices by JAX's collectives and lax.ppermute only.
A program may use at most 64 MiB of HBM per device.

v0:
```python
import jax
import jax.numpy as jnp
from jax import lax
from jax.sharding import PartitionSpec as P

strain_floor = 0.1
step_size = 0.5


def with_halo(block, sides, width):
    for axis, dim in sides:
        count = lax.axis_size(axis)
        forward = [(i, i + 1) for i in range(count - 1)]
        backward = [(target, source) for source, target in forward]
        low = lax.ppermute(
            lax.slice_in_dim(block, block.shape[dim] - width, None, axis=dim), axis, forward
        )
        high = lax.ppermute(lax.slice_in_dim(block, 0, width, axis=dim), axis, backward)
        block = jnp.concatenate([low, block, high], axis=dim)
    return block


def viscosity_of(extended):
    along_x = extended[0]
    along_y = extended[1]
    stretch_x = (along_x[:, 2:, 1:-1] - along_x[:, :-2, 1:-1]) * 0.5
    shear_uy = (along_x[:, 1:-1, 2:] - along_x[:, 1:-1, :-2]) * 0.5
    shear_vx = (along_y[:, 2:, 1:-1] - along_y[:, :-2, 1:-1]) * 0.5
    stretch_y = (along_y[:, 1:-1, 2:] - along_y[:, 1:-1, :-2]) * 0.5
    shearing = shear_uy + shear_vx
    strain_rate = (
        stretch_x * stretch_x
        + stretch_y * stretch_y
        + stretch_x * stretch_y
        + 0.25 * shearing * shearing
    )
    return jnp.power(strain_floor + strain_rate, -1.0 / 3.0)


def face_terms(viscous):
    centre = viscous[:, 1:-1, 1:-1]
    east_face = 0.5 * (centre + viscous[:, 2:, 1:-1])
    west_face = 0.5 * (centre + viscous[:, :-2, 1:-1])
    north_face = 0.5 * (centre + viscous[:, 1:-1, 2:])
    south_face = 0.5 * (centre + viscous[:, 1:-1, :-2])
    return (east_face, west_face, north_face, south_face)


def horizontal_diag(face_list):
    east_face, west_face, north_face, south_face = face_list
    first = 4.0 * (east_face + west_face) + (north_face + south_face)
    second = east_face + west_face + 4.0 * (north_face + south_face)
    return jnp.stack([first, second], 0)


def neighbour_sum(face_list, extended):
    east_face, west_face, north_face, south_face = face_list
    comp_u = extended[0]
    comp_v = extended[1]
    first = (
        4.0 * (east_face * comp_u[:, 2:, 1:-1] + west_face * comp_u[:, :-2, 1:-1])
        + north_face * comp_u[:, 1:-1, 2:]
        + south_face * comp_u[:, 1:-1, :-2]
    )
    second = (
        east_face * comp_v[:, 2:, 1:-1]
        + west_face * comp_v[:, :-2, 1:-1]
        + 4.0 * (north_face * comp_v[:, 1:-1, 2:] + south_face * comp_v[:, 1:-1, :-2])
    )
    return jnp.stack([first, second], 0)


def column_solve(centre, side_diag, right_hand, friction):
    layer_total = centre.shape[0]
    vertical_gain = 2.0 * float(layer_total * layer_total)
    coupling = vertical_gain * 0.5 * (centre[:-1] + centre[1:])
    zero_layer = jnp.zeros_like(centre[:1])
    lower_link = jnp.concatenate([zero_layer, coupling], 0)
    upper_link = jnp.concatenate([coupling, zero_layer], 0)
    bed_term = jnp.concatenate([friction[None], jnp.zeros_like(centre[1:])], 0)
    diagonal = (lower_link + upper_link + bed_term)[None] + side_diag
    diagonal = jnp.moveaxis(diagonal, 1, 0)
    right_side = jnp.moveaxis(right_hand, 1, 0)

    def forward(carried, layer_item):
        ratio_prev, value_prev = carried
        diag_layer, lower_layer, upper_layer, right_layer = layer_item
        pivots = diag_layer + lower_layer * ratio_prev
        ratio = -upper_layer / pivots
        value = (right_layer + lower_layer * value_prev) / pivots
        return ((ratio, value), (ratio, value))

    start = (jnp.zeros_like(right_side[0]), jnp.zeros_like(right_side[0]))
    final_pair, (ratios, values) = lax.scan(
        forward, start, (diagonal, lower_link, upper_link, right_side), unroll=8
    )

    def backward(following, layer_item):
        ratio, value = layer_item
        current = value - ratio * following
        return (current, current)

    final_row, solved = lax.scan(
        backward, jnp.zeros_like(right_side[0]), (ratios, values), reverse=True, unroll=8
    )
    return jnp.moveaxis(solved, 0, 1)


def top_source(mismatch, layer_count):
    zero_part = jnp.zeros((2, layer_count - 1) + mismatch.shape[1:], jnp.float32)
    return jnp.concatenate([zero_part, (float(layer_count) * mismatch)[:, None]], 1)


def to_layers(columns):
    return lax.all_to_all(columns, "layer", split_axis=1, concat_axis=3, tiled=True)


def on_device(velocity_init, driving, observed, log_friction, ice_mask):
    ice_cols = ice_mask != 0
    friction = jnp.exp(log_friction) * (ice_mask == 1).astype(jnp.float32)
    forcing = driving[:, None]
    column_count = (
        log_friction.shape[0]
        * log_friction.shape[1]
        * lax.axis_size("map")
        * lax.axis_size("layer")
    )
    layers = velocity_init
    for iteration in range(2):
        padded = with_halo(layers, (("map", 2),), 2)
        padded = jnp.pad(padded, ((0, 0), (0, 0), (0, 0), (2, 2)))
        viscous = viscosity_of(padded)
        face_list = face_terms(viscous)
        column_pack = jnp.concatenate(
            [
                viscous[None, :, 1:-1, 1:-1],
                horizontal_diag(face_list),
                neighbour_sum(face_list, padded[:, :, 1:-1, 1:-1]),
            ],
            0,
        )
        columns = lax.all_to_all(column_pack, "layer", split_axis=3, concat_axis=1, tiled=True)
        centre = columns[0]
        side_diag = columns[1:3]
        velocity_cols = jnp.where(
            ice_cols, column_solve(centre, side_diag, forcing + columns[3:5], friction), 0.0
        )
        layers = to_layers(velocity_cols)
    mismatch = jnp.where(ice_cols, velocity_cols[:, -1] - observed, 0.0)
    source = top_source(mismatch, velocity_cols.shape[1])
    adjoint = jnp.where(ice_cols, column_solve(centre, side_diag, source, friction), 0.0)
    adjoint_layers = to_layers(adjoint)
    adjoint_rim = with_halo(adjoint_layers, (("map", 2),), 1)
    adjoint_rim = jnp.pad(adjoint_rim, ((0, 0), (0, 0), (0, 0), (1, 1)))
    side_terms = lax.all_to_all(
        neighbour_sum(face_list, adjoint_rim), "layer", split_axis=3, concat_axis=1, tiled=True
    )
    adjoint = jnp.where(
        ice_cols, column_solve(centre, side_diag, source + side_terms, friction), 0.0
    )
    gradient = -friction * (
        velocity_cols[0, 0] * adjoint[0, 0] + velocity_cols[1, 0] * adjoint[1, 0]
    )
    misfit_sum, grad_sum = lax.psum(
        (0.5 * jnp.sum(mismatch * mismatch), jnp.sum(gradient * gradient)), ("map", "layer")
    )
    grad_scale = jnp.sqrt(grad_sum / column_count + 1e-06)
    return (layers, log_friction - step_size * gradient / grad_scale, misfit_sum / column_count)


def solution(mesh):
    in_specs = (
        P(None, "layer", "map", None),
        P(None, "map", "layer"),
        P(None, "map", "layer"),
        P("map", "layer"),
        P("map", "layer"),
    )
    out_specs = (P(None, "layer", "map", None), P("map", "layer"), P())
    return jax.shard_map(
        on_device, mesh=mesh, in_specs=in_specs, out_specs=out_specs, check_vma=False
    )
```

profile of v0, /device:TPU:0, one launch (start us, length us, event | category | flops | bytes accessed | tf_op | source)
XLA Modules:
  0.0 177.3 jit_solution(18236260642446603400)
XLA Ops:
  1.5 2.4 %collective-permute-start = (f32[2,4,2,1024]{3,1,2,0:T(4,128)S(1)}, f32[2,4,2,1024]{3,1,2,0:T(4,128)S(1)}, u32[]{:S(2)}, u32[]{:S(2)}) collective-permute-start(f32[2,4,2,1024]{3,1,2,0:T(4,128)S(1)} %copy.78), channel_id=1, source_target_pairs={{0,4},{4,8},{8,12},{12,16},{16,20},{20,24},{24,28},{1,5},{5,9},{9,... | collective-permute-start | bytes 196616 | tf_op jit(solution)/shard_map/ppermute | solution.py:15
  3.9 1.3 collective-permute-start.1
  5.9 3.3 %collective-permute-done.1 = f32[2,4,2,1024]{3,1,2,0:T(4,128)S(1)} collective-permute-done((f32[2,4,2,1024]{3,1,2,0:T(4,128)S(1)}, f32[2,4,2,1024]{3,1,2,0:T(4,128)S(1)}, u32[]{:S(2)}, u32[]{:S(2)}) %collective-permute-start.1) | collective-permute-done | bytes 65568 | tf_op jit(solution)/shard_map/ppermute | solution.py:18
  10.5 3.1 %copy.81 = f32[5,4,2,1024]{0,1,2,3:T(4,128)} copy(f32[5,4,2,1024]{3,1,2,0:T(4,128)S(1)} %fusion.422) | data formatting | bytes 327680 | tf_op jit(solution)/shard_map/concatenate | solution.py:134
  13.6 6.6 %reshape.658 = f32[4,1,10240]{2,1,0:T(1,128)} reshape(f32[1024,2,4,5]{3,2,1,0:T(4,128)} %bitcast.1638) | data formatting | bytes 327680
  20.3 3.7 %all-to-all-start = ((f32[4,1,10240]{2,1,0:T(1,128)}), f32[4,1,10240]{2,1,0:T(1,128)S(1)}, u32[]{:S(2)}, u32[]{:S(2)}) async-start(f32[4,1,10240]{2,1,0:T(1,128)} %reshape.658), calls=%async_computation | async-start | bytes 327680 | tf_op jit(solution)/shard_map/all_to_all | solution.py:142
  24.0 5.1 %all-to-all-done = f32[4,1,10240]{2,1,0:T(1,128)S(1)} async-done(((f32[4,1,10240]{2,1,0:T(1,128)}), f32[4,1,10240]{2,1,0:T(1,128)S(1)}, u32[]{:S(2)}, u32[]{:S(2)}) %all-to-all-start) | async-done | bytes 163872 | tf_op jit(solution)/shard_map/all_to_all | solution.py:142
  30.7 7.3 %reshape.659 = f32[1024,2,4,5]{3,2,1,0:T(4,128)} reshape(f32[4,10240]{1,0:T(4,128)S(1)} %reduce) | data formatting | bytes 327680
  38.0 3.5 %copy.82 = f32[5,4,2,4,256]{4,2,1,3,0:T(2,128)S(1)} copy(f32[5,4,2,4,256]{0,1,2,4,3:T(4,128)} %bitcast.1639) | data formatting | bytes 327680 | tf_op jit(solution)/shard_map/all_to_all | solution.py:142
  43.1 7.2 %all_to_all.102 = f32[2,16,2,256]{3,2,0,1:T(2,128)S(1)} all-to-all(f32[2,16,2,256]{3,2,0,1:T(2,128)S(1)} %bitcast.1661), channel_id=1, replica_groups=mesh['map'=8,'layer'=4] {'layer'}, dimensions={1} | all-to-all | bytes 131072 | tf_op jit(solution)/shard_map/all_to_all | solution.py:115
  50.4 2.3 %collective-permute-start.2 = (f32[2,4,2,1024]{3,1,2,0:T(4,128)S(1)}, f32[2,4,2,1024]{3,1,2,0:T(4,128)S(1)}, u32[]{:S(2)}, u32[]{:S(2)}) collective-permute-start(f32[2,4,2,1024]{3,1,2,0:T(4,128)S(1)} %all_to_all.80), channel_id=1, source_target_pairs={{0,4},{4,8},{8,12},{12,16},{16,20},{20,24},{24,28},{1,5},{5,9},{9,... | collective-permute-start | bytes 196616 | tf_op jit(solution)/shard_map/ppermute | solution.py:15
  52.7 1.3 collective-permute-start.3
  54.0 4.2 %collective-permute-done.3 = f32[2,4,2,1024]{3,1,2,0:T(4,128)S(1)} collective-permute-done((f32[2,4,2,1024]{3,1,2,0:T(4,128)S(1)}, f32[2,4,2,1024]{3,1,2,0:T(4,128)S(1)}, u32[]{:S(2)}, u32[]{:S(2)}) %collective-permute-start.3) | collective-permute-done | bytes 65568 | tf_op jit(solution)/shard_map/ppermute | solution.py:18
  59.4 3.1 %copy.86 = f32[5,4,2,1024]{0,1,2,3:T(4,128)} copy(f32[5,4,2,1024]{3,1,2,0:T(4,128)S(1)} %fusion.406) | data formatting | bytes 327680 | tf_op jit(solution)/shard_map/concatenate | solution.py:134
  62.6 6.6 %reshape.660 = f32[4,1,10240]{2,1,0:T(1,128)} reshape(f32[1024,2,4,5]{3,2,1,0:T(4,128)} %bitcast.1640) | data formatting | bytes 327680
  69.2 3.5 %all-to-all-start.2 = ((f32[4,1,10240]{2,1,0:T(1,128)}), f32[4,1,10240]{2,1,0:T(1,128)S(1)}, u32[]{:S(2)}, u32[]{:S(2)}) async-start(f32[4,1,10240]{2,1,0:T(1,128)} %reshape.660), calls=%async_computation.2 | async-start | bytes 327680 | tf_op jit(solution)/shard_map/all_to_all | solution.py:142
  72.8 4.8 %all-to-all-done.2 = f32[4,1,10240]{2,1,0:T(1,128)S(1)} async-done(((f32[4,1,10240]{2,1,0:T(1,128)}), f32[4,1,10240]{2,1,0:T(1,128)S(1)}, u32[]{:S(2)}, u32[]{:S(2)}) %all-to-all-start.2) | async-done | bytes 163872 | tf_op jit(solution)/shard_map/all_to_all | solution.py:142
  77.6 1.1 reduce.1
  78.7 7.3 %reshape.661 = f32[1024,2,4,5]{3,2,1,0:T(4,128)} reshape(f32[4,10240]{1,0:T(4,128)S(1)} %reduce.1) | data formatting | bytes 327680
  86.0 3.5 %copy.87 = f32[5,4,2,4,256]{4,2,1,3,0:T(2,128)S(1)} copy(f32[5,4,2,4,256]{0,1,2,4,3:T(4,128)} %bitcast.1641) | data formatting | bytes 327680 | tf_op jit(solution)/shard_map/all_to_all | solution.py:142
  91.8 1.4 multiply_reduce_fusion
  94.6 7.3 %all_to_all.103 = f32[2,16,2,256]{3,2,0,1:T(2,128)S(1)} all-to-all(f32[2,16,2,256]{3,2,0,1:T(2,128)S(1)} %bitcast.1663), channel_id=1, replica_groups=mesh['map'=8,'layer'=4] {'layer'}, dimensions={1} | all-to-all | bytes 131072 | tf_op jit(solution)/shard_map/all_to_all | solution.py:115
  102.0 2.5 %collective-permute-start.4 = (f32[2,4,1,1024]{3,1,2,0:T(4,128)S(1)}, f32[2,4,1,1024]{3,1,2,0:T(4,128)S(1)}, u32[]{:S(2)}, u32[]{:S(2)}) collective-permute-start(f32[2,4,1,1024]{3,1,2,0:T(4,128)S(1)} %get-tuple-element.1241), channel_id=1, source_target_pairs={{0,4},{4,8},{8,12},{12,16},{16,20},{20,24},{24,28},{1,5},{5,9},{9,... | collective-permute-start | bytes 98312 | tf_op jit(solution)/shard_map/ppermute | solution.py:15
  104.5 1.3 collective-permute-start.5
  105.8 3.3 %all-to-all-start.3 = ((f32[2,16,2,256]{3,2,0,1:T(2,128)}), f32[2,16,2,256]{3,2,0,1:T(2,128)S(1)}, u32[]{:S(2)}, u32[]{:S(2)}) async-start(f32[2,16,2,256]{3,2,0,1:T(2,128)} %bitcast.46), calls=%async_computation.3 | async-start | bytes 131072 | tf_op jit(solution)/shard_map/all_to_all | solution.py:115
  109.8 1.4 copy.92
  111.2 3.8 %reshape.662 = f32[4,1,4096]{2,1,0:T(1,128)} reshape(f32[1024,2,2,4]{3,2,1,0:T(2,128)S(1)} %bitcast.1643) | data formatting | bytes 131072
  115.0 3.8 %all-to-all-start.5 = ((f32[4,1,4096]{2,1,0:T(1,128)}), f32[4,1,4096]{2,1,0:T(1,128)S(1)}, u32[]{:S(2)}, u32[]{:S(2)}) async-start(f32[4,1,4096]{2,1,0:T(1,128)} %reshape.662), calls=%async_computation.5 | async-start | bytes 131072 | tf_op jit(solution)/shard_map/all_to_all | solution.py:155
  120.2 3.5 %all-to-all-done.5 = f32[4,1,4096]{2,1,0:T(1,128)S(1)} async-done(((f32[4,1,4096]{2,1,0:T(1,128)}), f32[4,1,4096]{2,1,0:T(1,128)S(1)}, u32[]{:S(2)}, u32[]{:S(2)}) %all-to-all-start.5) | async-done | bytes 65568 | tf_op jit(solution)/shard_map/all_to_all | solution.py:155
  124.4 3.2 %reshape.663 = f32[1024,2,2,4]{3,2,1,0:T(2,128)S(1)} reshape(f32[4,4096]{1,0:T(4,128)S(1)} %reduce.2) | data formatting | bytes 131072
  130.0 1.3 multiply_reduce_fusion.1
  131.2 43.0 %all-reduce.9 = (f32[]{:T(128)}, f32[]{:T(128)}) all-reduce(f32[]{:T(128)} %get-tuple-element.1115, f32[]{:T(128)S(6)} %mul.1092), channel_id=1, replica_groups=mesh['map'=8,'layer'=4] {'map','layer'}, use_global_device_ids=true, to_apply=%region_17.18 | all-reduce | flops 2 | bytes 16 | tf_op jit(solution)/shard_map/psum | solution.py:164
  (276 shorter events, 20.1 us)
Async XLA Ops:
  1.5 4.4 %collective-permute-start = (f32[2,4,2,1024]{3,1,2,0:T(4,128)S(1)}, f32[2,4,2,1024]{3,1,2,0:T(4,128)S(1)}, u32[]{:S(2)}, u32[]{:S(2)}) collective-permute-start(f32[2,4,2,1024]{3,1,2,0:T(4,128)S(1)} %copy.78), channel_id=1, source_target_pairs={{0,4},{4,8},{8,12},{12,16},{16,20},{20,24},{24,28},{1,5},{5,9},{9,... | collective-permute-start | bytes 196616 | tf_op jit(solution)/shard_map/ppermute | solution.py:15
  3.9 5.3 %collective-permute-start.1 = (f32[2,4,2,1024]{3,1,2,0:T(4,128)S(1)}, f32[2,4,2,1024]{3,1,2,0:T(4,128)S(1)}, u32[]{:S(2)}, u32[]{:S(2)}) collective-permute-start(f32[2,4,2,1024]{3,1,2,0:T(4,128)S(1)} %copy.78), channel_id=1, source_target_pairs={{4,0},{8,4},{12,8},{16,12},{20,16},{24,20},{28,24},{5,1},{9,5},{13... | collective-permute-start | bytes 196616 | tf_op jit(solution)/shard_map/ppermute | solution.py:18
  10.5 13.5 %copy-start = (s32[2,256]{1,0:T(2,128)S(1)}, s32[2,256]{1,0:T(2,128)}, u32[]{:S(2)}) copy-start(s32[2,256]{1,0:T(2,128)} %param.25) | copy-start | bytes 6148
  20.3 8.8 %all-to-all-start = ((f32[4,1,10240]{2,1,0:T(1,128)}), f32[4,1,10240]{2,1,0:T(1,128)S(1)}, u32[]{:S(2)}, u32[]{:S(2)}) async-start(f32[4,1,10240]{2,1,0:T(1,128)} %reshape.658), calls=%async_computation | async-start | bytes 327680 | tf_op jit(solution)/shard_map/all_to_all | solution.py:142
  30.7 11.0 %copy-start.2 = (f32[2,2,256]{2,1,0:T(2,128)S(1)}, f32[2,2,256]{2,1,0:T(2,128)}, u32[]{:S(2)}) copy-start(f32[2,2,256]{2,1,0:T(2,128)} %param.22) | copy-start | bytes 12292
  50.4 3.6 %collective-permute-start.2 = (f32[2,4,2,1024]{3,1,2,0:T(4,128)S(1)}, f32[2,4,2,1024]{3,1,2,0:T(4,128)S(1)}, u32[]{:S(2)}, u32[]{:S(2)}) collective-permute-start(f32[2,4,2,1024]{3,1,2,0:T(4,128)S(1)} %all_to_all.80), channel_id=1, source_target_pairs={{0,4},{4,8},{8,12},{12,16},{16,20},{20,24},{24,28},{1,5},{5,9},{9,... | collective-permute-start | bytes 196616 | tf_op jit(solution)/shard_map/ppermute | solution.py:15
  52.7 5.5 %collective-permute-start.3 = (f32[2,4,2,1024]{3,1,2,0:T(4,128)S(1)}, f32[2,4,2,1024]{3,1,2,0:T(4,128)S(1)}, u32[]{:S(2)}, u32[]{:S(2)}) collective-permute-start(f32[2,4,2,1024]{3,1,2,0:T(4,128)S(1)} %all_to_all.80), channel_id=1, source_target_pairs={{4,0},{8,4},{12,8},{16,12},{20,16},{24,20},{28,24},{5,1},{9,5},{13... | collective-permute-start | bytes 196616 | tf_op jit(solution)/shard_map/ppermute | solution.py:18
  69.2 8.4 %all-to-all-start.2 = ((f32[4,1,10240]{2,1,0:T(1,128)}), f32[4,1,10240]{2,1,0:T(1,128)S(1)}, u32[]{:S(2)}, u32[]{:S(2)}) async-start(f32[4,1,10240]{2,1,0:T(1,128)} %reshape.660), calls=%async_computation.2 | async-start | bytes 327680 | tf_op jit(solution)/shard_map/all_to_all | solution.py:142
  89.6 2.2 %copy-start.3 = (f32[2,2,256]{2,1,0:T(2,128)S(1)}, f32[2,2,256]{2,1,0:T(2,128)}, u32[]{:S(2)}) copy-start(f32[2,2,256]{2,1,0:T(2,128)} %param.23) | copy-start | bytes 12292
  102.0 7.1 %collective-permute-start.4 = (f32[2,4,1,1024]{3,1,2,0:T(4,128)S(1)}, f32[2,4,1,1024]{3,1,2,0:T(4,128)S(1)}, u32[]{:S(2)}, u32[]{:S(2)}) collective-permute-start(f32[2,4,1,1024]{3,1,2,0:T(4,128)S(1)} %get-tuple-element.1241), channel_id=1, source_target_pairs={{0,4},{4,8},{8,12},{12,16},{16,20},{20,24},{24,28},{1,5},{5,9},{9,... | collective-permute-start | bytes 98312 | tf_op jit(solution)/shard_map/ppermute | solution.py:15
  104.5 5.0 %collective-permute-start.5 = (f32[2,4,1,1024]{3,1,2,0:T(4,128)S(1)}, f32[2,4,1,1024]{3,1,2,0:T(4,128)S(1)}, u32[]{:S(2)}, u32[]{:S(2)}) collective-permute-start(f32[2,4,1,1024]{3,1,2,0:T(4,128)S(1)} %get-tuple-element.1242), channel_id=1, source_target_pairs={{4,0},{8,4},{12,8},{16,12},{20,16},{24,20},{28,24},{5,1},{9,5},{13... | collective-permute-start | bytes 98312 | tf_op jit(solution)/shard_map/ppermute | solution.py:18
  105.8 9.2 %all-to-all-start.3 = ((f32[2,16,2,256]{3,2,0,1:T(2,128)}), f32[2,16,2,256]{3,2,0,1:T(2,128)S(1)}, u32[]{:S(2)}, u32[]{:S(2)}) async-start(f32[2,16,2,256]{3,2,0,1:T(2,128)} %bitcast.46), calls=%async_computation.3 | async-start | bytes 131072 | tf_op jit(solution)/shard_map/all_to_all | solution.py:115
  115.0 8.6 %all-to-all-start.5 = ((f32[4,1,4096]{2,1,0:T(1,128)}), f32[4,1,4096]{2,1,0:T(1,128)S(1)}, u32[]{:S(2)}, u32[]{:S(2)}) async-start(f32[4,1,4096]{2,1,0:T(1,128)} %reshape.662), calls=%async_computation.5 | async-start | bytes 131072 | tf_op jit(solution)/shard_map/all_to_all | solution.py:155
  127.6 2.4 %copy-start.1 = (f32[2,256]{1,0:T(2,128)S(1)}, f32[2,256]{1,0:T(2,128)}, u32[]{:S(2)}) copy-start(f32[2,256]{1,0:T(2,128)} %param.24) | copy-start | bytes 6148
where the time goes:
time: 178 us; the launch traced here: 177 us
  blocking collectives  57.5 us (32%)
  local copies, waits for them, and re-layouts  54.7 us (31%)
  starting transfers between devices  25.3 us (14%)
  waiting for transfers between devices  21.3 us (12%)
  other arithmetic  13.2 us (7%)
  between operations  4.38 us (2%)
    psum x1, blocking collectives, on_device(): lax.psum((0.5 * jnp.sum(mismatch * mismatch), jnp.sum(gradient * gradient...  43 us
    unnamed x17, local copies, waits for them, and re-layouts  35.9 us
    all_to_all x2, blocking collectives, to_layers(): lax.all_to_all(columns, 'layer', split_axis=1, concat_axis=3, tiled=True)  14.5 us
    all_to_all x2, waiting for transfers between devices, on_device(): lax.all_to_all(column_pack, 'layer', split_axis=3, concat_axis=1, tiled=T...  9.94 us
    ppermute x3, waiting for transfers between devices, with_halo(): lax.ppermute(lax.slice_in_dim(block, 0, width, axis=dim), axis, backward)  7.87 us
    all_to_all x3, local copies, waits for them, and re-layouts, on_device(): lax.all_to_all(column_pack, 'layer', split_axis=3, concat_axis=1, tiled=T...  7.61 us
    all_to_all x2, starting transfers between devices, on_device(): lax.all_to_all(column_pack, 'layer', split_axis=3, concat_axis=1, tiled=T...  7.24 us
    ppermute x3, starting transfers between devices, with_halo(): lax.ppermute(lax.slice_in_dim(block, block.shape[dim] - width, None, axis...  7.07 us
  transfers between devices with their start and end apart: 10, of which 6 were waited for; matrix products, arithmetic and copies ran while one was open for 4% of the time, Pallas kernels for 0%

commit v1 on v0

v1 whole, which is shorter than its diff:
```python
import functools
import math

import jax
import jax.numpy as jnp
from jax import lax
from jax.experimental import pallas as pl
from jax.experimental.pallas import tpu as pltpu
from jax.sharding import PartitionSpec as P

strain_floor = 0.1
step_size = 0.5
LANES = 128
REACH = 5
MIB = 1 << 20


def rows_of_eight(count):
    return -(-count // 8) * 8


class Plan:
    def __init__(self, mesh_shape, velocity_shape):
        self.map_size = mesh_shape["map"]
        self.layer_size = mesh_shape["layer"]
        self.devices = self.map_size * self.layer_size
        self.layers_here = velocity_shape[1]
        self.rows = velocity_shape[2]
        self.ny = velocity_shape[3]
        self.layers = self.layers_here * self.layer_size
        self.cols = self.ny // self.devices
        self.width = LANES // self.rows
        self.halo = (self.width - self.cols) // 2
        self.local_cols = self.ny // self.layer_size
        self.per_chunk = LANES // self.cols
        self.chunks = self.ny // LANES
        self.column_count = self.rows * self.map_size * self.ny
        self.vel_rows = 2 * self.layers_here
        self.in_rows = rows_of_eight(self.vel_rows + 6)
        self.out_rows = rows_of_eight(self.layers_here + 3)
        self.unrolled = self.map_size <= 8
        assert self.width * self.rows == LANES and self.cols * self.per_chunk == LANES
        assert self.halo >= REACH and 2 * self.cols <= self.width and self.local_cols % LANES == 0


def repeat(plan, count, body, carry=0):
    if plan.unrolled:
        for index in range(count):
            carry = body(index, carry)
        return carry
    return lax.fori_loop(0, count, body, carry)


def lane_roll(value, shift):
    shift = shift % LANES
    return value if shift == 0 else pltpu.roll(value, shift, 1)


def pack_kernel(plan, vel_ref, driving_ref, observed_ref, log_ref, mask_ref, out_ref, held):
    width, rows = plan.width, plan.rows
    held[...] = jnp.zeros_like(held)
    for r in range(rows):
        for c in range(2):
            for k in range(plan.layers_here):
                held[r, c * plan.layers_here + k : c * plan.layers_here + k + 1, LANES : LANES + plan.ny] = vel_ref[
                    c, k, r : r + 1, :
                ]
    first = pl.multiple_of(LANES + lax.axis_index("layer") * plan.local_cols, LANES)
    here = pl.ds(first, plan.local_cols)
    base = plan.vel_rows
    for r in range(rows):
        for c in range(2):
            held[r, base + c : base + c + 1, here] = driving_ref[c, r : r + 1, :]
            held[r, base + 2 + c : base + 3 + c, here] = observed_ref[c, r : r + 1, :]
        held[r, base + 4 : base + 5, here] = log_ref[r : r + 1, :]
        held[r, base + 5 : base + 6, here] = mask_ref[r : r + 1, :].astype(jnp.float32)

    lane = lax.broadcasted_iota(jnp.int32, (plan.in_rows, LANES), 1)

    def chunk_windows(i, carry):
        def part(r, step):
            return held[r, :, pl.ds(pl.multiple_of((i + 1 + step) * LANES, LANES), LANES)]

        for t in range(plan.per_chunk):
            relative = plan.cols * t - plan.halo
            step, offset = relative // LANES, relative % LANES
            block = None
            for r in range(rows):
                window = part(r, step)
                if offset + width > LANES:
                    window = jnp.where(lane >= offset, window, part(r, step + 1))
                window = lane_roll(window, r * width - offset)
                block = window if block is None else jnp.where(lane >= r * width, window, block)
            out_ref[i * plan.per_chunk + t] = block
        return carry

    repeat(plan, plan.chunks, chunk_windows)


def solve_kernel(plan, in_ref, out_ref, field, eta_ref, side, rhs, faces, ratio, inverse):
    size, width, rows = plan.map_size, plan.width, plan.rows
    layers, here = plan.layers, plan.layers_here
    shape = (size, LANES)
    lane = lax.broadcasted_iota(jnp.int32, shape, 1)
    sub = lax.broadcasted_iota(jnp.int32, shape, 0)
    last_group = lane >= LANES - width
    first_group = lane < width
    x_end = jnp.logical_and(last_group, sub == size - 1)
    x_start = jnp.logical_and(first_group, sub == 0)

    def arrived(part, row):
        return in_ref[pl.ds(part * plan.in_rows + row, size, stride=plan.layer_size * plan.in_rows), :]

    def column_input(index):
        total = arrived(0, plan.vel_rows + index)
        for part in range(1, plan.layer_size):
            total = total + arrived(part, plan.vel_rows + index)
        return total

    def x_pair(value, edge):
        after = lane_roll(value, -width)
        before = after if 2 * width == LANES else lane_roll(value, width)
        after = jnp.where(last_group, pltpu.roll(after, size - 1, 0), after)
        before = jnp.where(first_group, pltpu.roll(before, 1, 0), before)
        return jnp.where(x_end, edge, after), jnp.where(x_start, edge, before)

    def y_pair(value):
        return lane_roll(value, -1), lane_roll(value, 1)

    def viscosity(rate):
        return jnp.exp2(jnp.log(strain_floor + rate) * (-1.0 / (3.0 * math.log(2.0))))

    def reciprocal(value):
        guess = pl.reciprocal(value, approx=True)
        return guess * (2.0 - value * guess)

    for part in range(plan.layer_size):
        for c in range(2):
            for k in range(here):
                field[c, part * here + k] = arrived(part, c * here + k)
    driving = [2.0 * column_input(c) for c in range(2)]
    observed = [column_input(2 + c) for c in range(2)]
    mask = column_input(5)
    ice = mask != 0.0
    friction = jnp.where(mask == 1.0, jnp.exp(column_input(4)), 0.0)

    def stencil(k, keep):
        u, v = field[0, k], field[1, k]
        u_east, u_west = x_pair(u, 0.0)
        v_east, v_west = x_pair(v, 0.0)
        u_north, u_south = y_pair(u)
        v_north, v_south = y_pair(v)
        stretch_x = u_east - u_west
        stretch_y = v_north - v_south
        shear = 0.5 * ((u_north - u_south) + (v_east - v_west))
        rate = 0.25 * (stretch_x * (stretch_x + stretch_y) + stretch_y * stretch_y + shear * shear)
        half_v = 0.5 * v
        eta = viscosity(rate)
        eta_edge = viscosity(0.25 * (u * u + half_v * half_v))
        eta_east, eta_west = x_pair(eta, eta_edge)
        eta_north, eta_south = y_pair(eta)
        east, west = eta + eta_east, eta + eta_west
        north, south = eta + eta_north, eta + eta_south
        along_x, along_y = east + west, north + south
        eta_ref[k] = eta
        side[0, k] = 4.0 * along_x + along_y
        side[1, k] = along_x + 4.0 * along_y
        rhs[0, k] = driving[0] + (4.0 * (east * u_east + west * u_west) + (north * u_north + south * u_south))
        rhs[1, k] = driving[1] + ((east * v_east + west * v_west) + 4.0 * (north * v_north + south * v_south))
        if keep:
            faces[0, k] = east
            faces[1, k] = west
            faces[2, k] = north
            faces[3, k] = south

    def coupling_of(k):
        return (2.0 * layers * layers) * (eta_ref[k] + eta_ref[k + 1])

    def eliminate(k, carry):
        lower, rest, value = carry
        coupling = coupling_of(k)
        new_rest, new_value = [], []
        for c in range(2):
            inv = reciprocal(coupling + rest[c])
            link = coupling * inv
            inverse[c, k] = inv
            ratio[c, k] = link
            out = (rhs[c, k] + lower * value[c]) * inv
            rhs[c, k] = out
            new_value.append(out)
            new_rest.append(side[c, k + 1] + rest[c] * link)
        return coupling, tuple(new_rest), tuple(new_value)

    def forward_solve():
        zero = jnp.zeros(shape, jnp.float32)
        rest = tuple(side[c, 0] + 2.0 * friction for c in range(2))
        lower, rest, value = repeat(plan, layers - 1, eliminate, (zero, rest, (zero, zero)))
        top = []
        for c in range(2):
            inv = reciprocal(rest[c])
            inverse[c, layers - 1] = inv
            top.append(jnp.where(ice, (rhs[c, layers - 1] + lower * value[c]) * inv, 0.0))
            field[c, layers - 1] = top[c]

        def back(step, following):
            k = layers - 2 - step
            current = tuple(jnp.where(ice, rhs[c, k] + ratio[c, k] * following[c], 0.0) for c in range(2))
            for c in range(2):
                field[c, k] = current[c]
            return current

        return top, repeat(plan, layers - 1, back, tuple(top))

    for sweep in range(2):

        def stencil_body(k, carry):
            stencil(k, sweep == 1)
            return carry

        repeat(plan, layers, stencil_body)
        top, base = forward_solve()

    centre = jnp.logical_and(lane % width >= plan.halo, lane % width < plan.halo + plan.cols)

    def send(k, carry):
        both = jnp.where(centre, field[0, k], lane_roll(field[1, k], plan.cols))
        out_ref[pl.ds((k // here) * plan.out_rows + k % here, size, stride=plan.layer_size * plan.out_rows), :] = both
        return carry

    repeat(plan, layers, send)

    mismatch = [jnp.where(ice, top[c] - observed[c], 0.0) for c in range(2)]
    source = [(2.0 * layers) * mismatch[c] for c in range(2)]

    first_top = tuple(source[c] * inverse[c, layers - 1] for c in range(2))

    def side_sum(k, value):
        east, west, north, south = (faces[n, k] for n in range(4))
        u_east, u_west = x_pair(value[0], 0.0)
        v_east, v_west = x_pair(value[1], 0.0)
        u_north, u_south = y_pair(value[0])
        v_north, v_south = y_pair(value[1])
        rhs[0, k] = 4.0 * (east * u_east + west * u_west) + (north * u_north + south * u_south)
        rhs[1, k] = (east * v_east + west * v_west) + 4.0 * (north * v_north + south * v_south)

    side_sum(layers - 1, first_top)

    def first_back(step, following):
        k = layers - 2 - step
        current = tuple(ratio[c, k] * following[c] for c in range(2))
        side_sum(k, current)
        return current

    repeat(plan, layers - 1, first_back, first_top)

    def second_forward(k, carry):
        lower, value = carry
        out = tuple((rhs[c, k] + lower * value[c]) * inverse[c, k] for c in range(2))
        for c in range(2):
            rhs[c, k] = out[c]
        return coupling_of(k), out

    zero = jnp.zeros(shape, jnp.float32)
    lower, value = repeat(plan, layers - 1, second_forward, (zero, (zero, zero)))
    second_top = tuple(
        (rhs[c, layers - 1] + source[c] + lower * value[c]) * inverse[c, layers - 1] for c in range(2)
    )

    def second_back(step, following):
        k = layers - 2 - step
        return tuple(rhs[c, k] + ratio[c, k] * following[c] for c in range(2))

    adjoint = repeat(plan, layers - 1, second_back, second_top)
    adjoint = [jnp.where(ice, adjoint[c], 0.0) for c in range(2)]
    gradient = -friction * (base[0] * adjoint[0] + base[1] * adjoint[1])
    misfit_part = jnp.where(centre, mismatch[0] * mismatch[0] + mismatch[1] * mismatch[1], 0.0)
    grad_part = jnp.where(centre, gradient * gradient, 0.0)
    misfit_row = jnp.broadcast_to(jnp.sum(misfit_part, axis=0, keepdims=True), shape)
    grad_row = jnp.broadcast_to(jnp.sum(grad_part, axis=0, keepdims=True), shape)
    for part in range(plan.layer_size):
        for n, plane in enumerate((gradient, misfit_row, grad_row)):
            out_ref[pl.ds(part * plan.out_rows + here + n, size, stride=plan.layer_size * plan.out_rows), :] = plane


def unpack_kernel(plan, in_ref, log_ref, vel_ref, friction_ref, misfit_ref, grad_ref):
    here, width, cols = plan.layers_here, plan.width, plan.cols
    lane = lax.broadcasted_iota(jnp.int32, (plan.out_rows, LANES), 1)
    total = jnp.zeros((plan.out_rows, LANES), jnp.float32)

    def chunk(i, total):
        blocks = [in_ref[i * plan.per_chunk + t] for t in range(plan.per_chunk)]
        span = pl.ds(pl.multiple_of(i * LANES, LANES), LANES)
        for r in range(plan.rows):
            for c in range(2):
                start = r * width + plan.halo + c * cols
                row = None
                for t in range(plan.per_chunk):
                    moved = lane_roll(blocks[t], t * cols - start)
                    row = moved if row is None else jnp.where(lane >= t * cols, moved, row)
                for k in range(here):
                    vel_ref[c, k, r : r + 1, span] = row[k : k + 1, :]
                if c == 0:
                    grad_ref[r : r + 1, span] = row[here : here + 1, :]
        for block in blocks:
            total = total + block
        return total

    total = repeat(plan, plan.chunks, chunk, total)
    sums = jnp.sum(total, axis=1, keepdims=True)
    misfit_ref[...] = 0.5 * sums[here + 1 : here + 2, :] / plan.column_count
    scale = step_size / jnp.sqrt(sums[here + 2 : here + 3, :] / plan.column_count + 1e-06)
    first = pl.multiple_of(lax.axis_index("layer") * plan.local_cols, LANES)
    gradient = grad_ref[:, pl.ds(first, plan.local_cols)]
    friction_ref[...] = log_ref[...] - gradient * scale


def on_device(mesh_shape, velocity_init, driving, observed, log_friction, ice_mask):
    plan = Plan(mesh_shape, velocity_init.shape)
    vmem = pl.BlockSpec(memory_space=pltpu.VMEM)
    f32 = jnp.float32
    limit = pltpu.CompilerParams(vmem_limit_bytes=(16 if plan.unrolled else 40) * MIB)

    packed = pl.pallas_call(
        functools.partial(pack_kernel, plan),
        out_shape=jax.ShapeDtypeStruct((plan.devices, plan.in_rows, LANES), f32),
        in_specs=[vmem] * 5,
        out_specs=vmem,
        scratch_shapes=[pltpu.VMEM((plan.rows, plan.in_rows, plan.ny + 2 * LANES), f32)],
        compiler_params=limit,
        name="pack",
    )(velocity_init, driving, observed, log_friction, ice_mask)

    windows = lax.all_to_all(packed, ("map", "layer"), split_axis=0, concat_axis=0, tiled=True)

    plane = (plan.layers, plan.map_size, LANES)
    solved = pl.pallas_call(
        functools.partial(solve_kernel, plan),
        out_shape=jax.ShapeDtypeStruct((plan.devices * plan.out_rows, LANES), f32),
        in_specs=[vmem],
        out_specs=vmem,
        scratch_shapes=[
            pltpu.VMEM((2,) + plane, f32),
            pltpu.VMEM(plane, f32),
            pltpu.VMEM((2,) + plane, f32),
            pltpu.VMEM((2,) + plane, f32),
            pltpu.VMEM((4,) + plane, f32),
            pltpu.VMEM((2,) + plane, f32),
            pltpu.VMEM((2,) + plane, f32),
        ],
        compiler_params=limit,
        name="solve",
    )(windows.reshape(plan.devices * plan.in_rows, LANES))

    back = lax.all_to_all(
        solved.reshape(plan.devices, plan.out_rows, LANES),
        ("map", "layer"),
        split_axis=0,
        concat_axis=0,
        tiled=True,
    )

    velocity, friction_new, misfit = pl.pallas_call(
        functools.partial(unpack_kernel, plan),
        out_shape=(
            jax.ShapeDtypeStruct(velocity_init.shape, f32),
            jax.ShapeDtypeStruct(log_friction.shape, f32),
            jax.ShapeDtypeStruct((1, 1), f32),
        ),
        in_specs=[vmem] * 2,
        out_specs=(vmem, vmem, vmem),
        scratch_shapes=[pltpu.VMEM((plan.rows, plan.ny), f32)],
        compiler_params=limit,
        name="unpack",
    )(back, log_friction)
    return velocity, friction_new, misfit.reshape(())


def solution(mesh):
    in_specs = (
        P(None, "layer", "map", None),
        P(None, "map", "layer"),
        P(None, "map", "layer"),
        P("map", "layer"),
        P("map", "layer"),
    )
    out_specs = (P(None, "layer", "map", None), P("map", "layer"), P())
    return jax.shard_map(
        functools.partial(on_device, dict(mesh.shape)),
        mesh=mesh,
        in_specs=in_specs,
        out_specs=out_specs,
        check_vma=False,
    )
```

time: 178 us -> 35.2 us (0.20)
  local copies, waits for them, and re-layouts: 54.7 us -> 3.57 us
  blocking collectives: 57.5 us -> 28.3 us
  starting transfers between devices: 25.3 us -> 0 us
  waiting for transfers between devices: 21.3 us -> 0 us
  other arithmetic: 13.2 us -> 0 us
  between operations: 4.38 us -> 0.67 us
  Pallas kernels: 0 us -> 2.32 us
    psum x1 -> x0, blocking collectives: 43 us -> none  [on_device(): lax.psum((0.5 * jnp.sum(mismatch * mismatch), jnp.sum(gradient * gradient...]
    unnamed x17 -> x12, local copies, waits for them, and re-layouts: 35.9 us -> 3.57 us
    all_to_all x4 -> x0, starting transfers between devices: 14.3 us -> none  [the longest x2 7.24 us: on_device(): lax.all_to_all(column_pack, 'layer', split_axis=3, concat_axis=1, tiled=T...]
    all_to_all x2, blocking collectives: 14.5 us -> 28.3 us  [the longest x1 18.1 us: on_device(): lax.all_to_all(packed, ('map', 'layer'), split_axis=0, concat_axis=0, til...]
    all_to_all x4 -> x0, waiting for transfers between devices: 13.4 us -> none  [the longest x2 9.94 us: on_device(): lax.all_to_all(column_pack, 'layer', split_axis=3, concat_axis=1, tiled=T...]
    ppermute x6 -> x0, starting transfers between devices: 10.9 us -> none  [the longest x3 7.07 us: with_halo(): lax.ppermute(lax.slice_in_dim(block, block.shape[dim] - width, None, axis...]
    all_to_all x10 -> x0, local copies, waits for them, and re-layouts: 9.46 us -> none  [the longest x3 7.61 us: on_device(): lax.all_to_all(column_pack, 'layer', split_axis=3, concat_axis=1, tiled=T...]
    ppermute x6 -> x0, waiting for transfers between devices: 7.88 us -> none  [the longest x3 7.87 us: with_halo(): lax.ppermute(lax.slice_in_dim(block, 0, width, axis=dim), axis, backward)]
  transfers between devices with their start and end apart: 10 -> 0, of which waited for: 6 -> 0; matrix products, arithmetic and copies ran while one was open for 4% -> 0% of each run, Pallas kernels for 0% -> 0%
where the time goes in v1:
time: 35.2 us; the launch traced here: 34.9 us
  blocking collectives  28.3 us (80%)
  local copies, waits for them, and re-layouts  3.57 us (10%)
  Pallas kernels  2.32 us (7%)
  between operations  0.67 us (2%)
    all_to_all x1, blocking collectives, on_device(): lax.all_to_all(packed, ('map', 'layer'), split_axis=0, concat_axis=0, til...  18.1 us
    all_to_all x1, blocking collectives, on_device(): lax.all_to_all(solved.reshape(plan.devices, plan.out_rows, LANES), ('map'...  10.3 us
    unnamed x12, local copies, waits for them, and re-layouts  3.57 us
    pallas_call x1, Pallas kernels, on_device(): pl.pallas_call(functools.partial(solve_kernel, plan), out_shape=jax.Shape...  1.25 us
    pallas_call x1, Pallas kernels, on_device(): pl.pallas_call(functools.partial(unpack_kernel, plan), out_shape=(jax.Sha...  0.85 us

profile of v1, /device:TPU:0, one launch (start us, length us, event | category | flops | bytes accessed | tf_op | source)
XLA Modules:
  0.0 34.9 jit_solution(1722402127240860901)
XLA Ops:
  0.6 0.0 copy-start
  0.6 0.8 %copy-done = f32[2,4,2,1024]{3,2,1,0:T(2,128)S(1)} copy-done((f32[2,4,2,1024]{3,2,1,0:T(2,128)S(1)}, f32[2,4,2,1024]{3,2,1,0:T(2,128)}, u32[]{:S(2)}) %copy-start) | copy-done | bytes 65560
  1.5 0.0 copy-start.1
  1.5 0.7 %copy-done.1 = f32[2,256]{1,0:T(2,128)S(1)} copy-done((f32[2,256]{1,0:T(2,128)S(1)}, f32[2,256]{1,0:T(2,128)}, u32[]{:S(2)}) %copy-start.1) | copy-done | bytes 2072
  2.2 0.0 copy-start.3
  2.2 0.7 %copy-done.3 = f32[2,2,256]{2,1,0:T(2,128)S(1)} copy-done((f32[2,2,256]{2,1,0:T(2,128)S(1)}, f32[2,2,256]{2,1,0:T(2,128)}, u32[]{:S(2)}) %copy-start.3) | copy-done | bytes 4120
  2.8 0.0 copy-start.4
  2.8 0.7 %copy-done.4 = f32[2,2,256]{2,1,0:T(2,128)S(1)} copy-done((f32[2,2,256]{2,1,0:T(2,128)S(1)}, f32[2,2,256]{2,1,0:T(2,128)}, u32[]{:S(2)}) %copy-start.4) | copy-done | bytes 4120
  3.5 0.0 copy-start.5
  3.5 0.7 %copy-done.5 = s32[2,256]{1,0:T(2,128)S(1)} copy-done((s32[2,256]{1,0:T(2,128)S(1)}, s32[2,256]{1,0:T(2,128)}, u32[]{:S(2)}) %copy-start.5) | copy-done | bytes 2072
  4.2 0.2 pack.1
  4.4 18.1 %all_to_all.10 = f32[32,16,128]{2,1,0:T(8,128)S(1)} all-to-all(f32[32,16,128]{2,1,0:T(8,128)S(1)} %pack.1), channel_id=1, replica_groups=mesh['map'=8,'layer'=4] {'map','layer'}, dimensions={0} | all-to-all | bytes 524288 | tf_op jit(solution)/shard_map/all_to_all | solution.py:333
  22.5 1.2 %solve.1 = f32[256,128]{1,0:T(8,128)S(1)} custom-call(f32[512,128]{1,0:T(8,128)S(1)} %bitcast.3), custom_call_target="tpu_custom_call" | custom-call | tf_op jit(solution)/shard_map/solve/pallas_call | solution.py:336
  23.7 0.0 copy-start.2
  23.8 10.3 %all_to_all.11.in_ref = f32[32,8,128]{2,1,0:T(8,128)S(1)} all-to-all(f32[32,8,128]{2,1,0:T(8,128)S(1)} %bitcast.4), channel_id=1, replica_groups=mesh['map'=8,'layer'=4] {'map','layer'}, dimensions={0} | all-to-all | bytes 262144 | tf_op jit(solution)/shard_map/all_to_all | solution.py:354
  34.0 0.0 copy-done.2
  34.0 0.8 %unpack.1 = (f32[2,4,2,1024]{3,2,1,0:T(2,128)}, f32[2,256]{1,0:T(2,128)}, f32[1,1]{1,0:T(1,128)}) custom-call(f32[32,8,128]{2,1,0:T(8,128)S(1)} %all_to_all.11.in_ref, f32[2,256]{1,0:T(2,128)S(1)} %copy-done.2), custom_call_target="tpu_custom_call" | custom-call | tf_op jit(solution)/shard_map/unpack/pallas_call | solution.py:362
Async XLA Ops:
  0.6 0.8 %copy-start = (f32[2,4,2,1024]{3,2,1,0:T(2,128)S(1)}, f32[2,4,2,1024]{3,2,1,0:T(2,128)}, u32[]{:S(2)}) copy-start(f32[2,4,2,1024]{3,2,1,0:T(2,128)} %vel_ref.1) | copy-start | bytes 196612
  1.5 0.7 %copy-start.1 = (f32[2,256]{1,0:T(2,128)S(1)}, f32[2,256]{1,0:T(2,128)}, u32[]{:S(2)}) copy-start(f32[2,256]{1,0:T(2,128)} %log_ref.3) | copy-start | bytes 6148
  2.2 0.7 %copy-start.3 = (f32[2,2,256]{2,1,0:T(2,128)S(1)}, f32[2,2,256]{2,1,0:T(2,128)}, u32[]{:S(2)}) copy-start(f32[2,2,256]{2,1,0:T(2,128)} %driving_ref.1) | copy-start | bytes 12292
  2.8 0.7 %copy-start.4 = (f32[2,2,256]{2,1,0:T(2,128)S(1)}, f32[2,2,256]{2,1,0:T(2,128)}, u32[]{:S(2)}) copy-start(f32[2,2,256]{2,1,0:T(2,128)} %observed_ref.1) | copy-start | bytes 12292
  3.5 0.7 %copy-start.5 = (s32[2,256]{1,0:T(2,128)S(1)}, s32[2,256]{1,0:T(2,128)}, u32[]{:S(2)}) copy-start(s32[2,256]{1,0:T(2,128)} %mask_ref.1) | copy-start | bytes 6148
  23.7 10.3 %copy-start.2 = (f32[2,256]{1,0:T(2,128)S(1)}, f32[2,256]{1,0:T(2,128)}, u32[]{:S(2)}) copy-start(f32[2,256]{1,0:T(2,128)} %log_ref.3) | copy-start | bytes 6148

commit v2 on v1

--- a/solution.py
+++ b/solution.py
@@ -13,10 +13,6 @@
 LANES = 128
 REACH = 5
 MIB = 1 << 20
-
-
-def rows_of_eight(count):
-    return -(-count // 8) * 8
 
 
 class Plan:
@@ -31,16 +27,22 @@
         self.cols = self.ny // self.devices
         self.width = LANES // self.rows
         self.halo = (self.width - self.cols) // 2
+        self.low = self.halo - REACH
+        self.wide = self.cols + 2 * REACH
+        self.half = self.wide // 2
+        self.gap = self.low + self.wide
         self.local_cols = self.ny // self.layer_size
         self.per_chunk = LANES // self.cols
         self.chunks = self.ny // LANES
         self.column_count = self.rows * self.map_size * self.ny
         self.vel_rows = 2 * self.layers_here
-        self.in_rows = rows_of_eight(self.vel_rows + 6)
-        self.out_rows = rows_of_eight(self.layers_here + 3)
+        self.in_rows = self.vel_rows + self.rows
+        self.out_rows = self.layers_here + 1
         self.unrolled = self.map_size <= 8
         assert self.width * self.rows == LANES and self.cols * self.per_chunk == LANES
-        assert self.halo >= REACH and 2 * self.cols <= self.width and self.local_cols % LANES == 0
+        assert self.low >= 0 and self.wide % 2 == 0 and self.width - self.wide >= self.half
+        assert 2 * self.cols <= self.width and self.local_cols % LANES == 0
+        assert self.vel_rows == 8 and self.rows == 2 and 3 * self.wide <= LANES
 
 
 def repeat(plan, count, body, carry=0):
@@ -56,45 +58,105 @@
     return value if shift == 0 else pltpu.roll(value, shift, 1)
 
 
-def pack_kernel(plan, vel_ref, driving_ref, observed_ref, log_ref, mask_ref, out_ref, held):
-    width, rows = plan.width, plan.rows
+def pack_kernel(
+    plan, vel_hbm, driving_hbm, observed_hbm, log_hbm, mask_hbm, out_hbm,
+    vel_ref, driving_ref, observed_ref, log_ref, mask_ref, out_ref, held, bed, arrival, leave,
+):
+    width, rows, wide = plan.width, plan.rows, plan.wide
+    copies = [
+        pltpu.make_async_copy(source, target, arrival.at[n])
+        for n, (source, target) in enumerate(
+            (
+                (vel_hbm, vel_ref),
+                (driving_hbm, driving_ref),
+                (observed_hbm, observed_ref),
+                (log_hbm, log_ref),
+                (mask_hbm, mask_ref),
+            )
+        )
+    ]
+    for copy in copies:
+        copy.start()
     held[...] = jnp.zeros_like(held)
+    bed[...] = jnp.zeros_like(bed)
+    first = pl.multiple_of(LANES + lax.axis_index("layer") * plan.local_cols, LANES)
+    here = pl.ds(first, plan.local_cols)
+    for copy in copies:
+        copy.wait()
     for r in range(rows):
         for c in range(2):
             for k in range(plan.layers_here):
                 held[r, c * plan.layers_here + k : c * plan.layers_here + k + 1, LANES : LANES + plan.ny] = vel_ref[
                     c, k, r : r + 1, :
                 ]
-    first = pl.multiple_of(LANES + lax.axis_index("layer") * plan.local_cols, LANES)
-    here = pl.ds(first, plan.local_cols)
-    base = plan.vel_rows
-    for r in range(rows):
-        for c in range(2):
-            held[r, base + c : base + c + 1, here] = driving_ref[c, r : r + 1, :]
-            held[r, base + 2 + c : base + 3 + c, here] = observed_ref[c, r : r + 1, :]
-        held[r, base + 4 : base + 5, here] = log_ref[r : r + 1, :]
-        held[r, base + 5 : base + 6, here] = mask_ref[r : r + 1, :].astype(jnp.float32)
-
-    lane = lax.broadcasted_iota(jnp.int32, (plan.in_rows, LANES), 1)
+        mask = mask_ref[r : r + 1, :].astype(jnp.float32)
+        for n, value in enumerate((observed_ref[0, r : r + 1, :], observed_ref[1, r : r + 1, :], mask)):
+            held[r, plan.vel_rows + 2 * n : plan.vel_rows + 2 * n + 1, here] = value
+            held[r, plan.vel_rows + 2 * n + 1 : plan.vel_rows + 2 * n + 2, here] = value
+    for n, value in enumerate((driving_ref[0], driving_ref[1], log_ref[...])):
+        bed[n, :, here] = value
+
+    shape = (plan.vel_rows, LANES)
+    lane = lax.broadcasted_iota(jnp.int32, shape, 1)
+    odd = lax.broadcasted_iota(jnp.int32, shape, 0) % 2 == 1
+    in_gap = jnp.logical_not(jnp.logical_and(lane % width >= plan.low, lane % width < plan.gap))
+    bed_lane = lax.broadcasted_iota(jnp.int32, (rows, LANES), 1)
+
+    chunk_rows = plan.per_chunk * plan.in_rows
+
+    def leaving(i):
+        start = i * chunk_rows
+        span = pl.ds(start if isinstance(i, int) else pl.multiple_of(start, 8), chunk_rows)
+        return pltpu.make_async_copy(out_ref.at[span, :], out_hbm.at[span, :], leave.at[i])
 
     def chunk_windows(i, carry):
-        def part(r, step):
-            return held[r, :, pl.ds(pl.multiple_of((i + 1 + step) * LANES, LANES), LANES)]
-
-        for t in range(plan.per_chunk):
-            relative = plan.cols * t - plan.halo
+        def window(read, relative, length, lanes):
             step, offset = relative // LANES, relative % LANES
+
+            def part(at):
+                return read(pl.ds(pl.multiple_of((i + 1 + at) * LANES, LANES), LANES))
+
+            if offset + length <= LANES:
+                return part(step), offset
+            return jnp.where(lanes >= offset, part(step), part(step + 1)), offset
+
+        def side_by_side(row_base, t):
             block = None
             for r in range(rows):
-                window = part(r, step)
-                if offset + width > LANES:
-                    window = jnp.where(lane >= offset, window, part(r, step + 1))
-                window = lane_roll(window, r * width - offset)
-                block = window if block is None else jnp.where(lane >= r * width, window, block)
-            out_ref[i * plan.per_chunk + t] = block
+                value, offset = window(
+                    lambda span: held[r, row_base : row_base + 8, span], plan.cols * t - plan.halo, width, lane
+                )
+                value = lane_roll(value, r * width - offset)
+                block = value if block is None else jnp.where(lane >= r * width, value, block)
+            return block
+
+        for t in range(plan.per_chunk):
+            block = side_by_side(0, t)
+            other = side_by_side(plan.vel_rows, t)
+            shift = plan.gap - plan.low
+            other = jnp.where(odd, lane_roll(other, shift - plan.half), lane_roll(other, shift))
+            block = jnp.where(in_gap, other, block)
+            line = None
+            for n in range(3):
+                value, offset = window(lambda span: bed[n, :, span], plan.cols * t - REACH, wide, bed_lane)
+                value = lane_roll(value, n * wide - offset)
+                line = value if line is None else jnp.where(bed_lane >= n * wide, value, line)
+            at = i * chunk_rows
+            if not isinstance(at, int):
+                at = pl.multiple_of(at, 8)
+            at = at + t * plan.in_rows
+            out_ref[pl.ds(at, plan.vel_rows), :] = block
+            out_ref[pl.ds(at + plan.vel_rows, rows), :] = line
+        leaving(i).start()
         return carry
 
     repeat(plan, plan.chunks, chunk_windows)
+
+    def left(i, carry):
+        leaving(i).wait()
+        return carry
+
+    repeat(plan, plan.chunks, left)
 
 
 def solve_kernel(plan, in_ref, out_ref, field, eta_ref, side, rhs, faces, ratio, inverse):
@@ -111,11 +173,22 @@
     def arrived(part, row):
         return in_ref[pl.ds(part * plan.in_rows + row, size, stride=plan.layer_size * plan.in_rows), :]
 
-    def column_input(index):
-        total = arrived(0, plan.vel_rows + index)
+    def over_parts(row):
+        total = arrived(0, row)
         for part in range(1, plan.layer_size):
-            total = total + arrived(part, plan.vel_rows + index)
+            total = total + arrived(part, row)
         return total
+
+    def from_gap(index):
+        shift = plan.low - plan.gap
+        left, right = over_parts(2 * index), over_parts(2 * index + 1)
+        return jnp.where(lane % width < plan.low + plan.half, lane_roll(left, shift), lane_roll(right, shift + plan.half))
+
+    def from_line(index):
+        plane = lane_roll(lines[0], plan.low - index * plan.wide)
+        for r in range(1, rows):
+            plane = jnp.where(lane >= r * width, lane_roll(lines[r], r * width + plan.low - index * plan.wide), plane)
+        return plane
 
     def x_pair(value, edge):
         after = lane_roll(value, -width)
@@ -138,11 +211,13 @@
         for c in range(2):
             for k in range(here):
                 field[c, part * here + k] = arrived(part, c * here + k)
-    driving = [2.0 * column_input(c) for c in range(2)]
-    observed = [column_input(2 + c) for c in range(2)]
-    mask = column_input(5)
+    lines = [over_parts(plan.vel_rows + r) for r in range(rows)]
+    reached = jnp.logical_and(lane % width >= plan.low, lane % width < plan.gap)
+    driving = [2.0 * from_line(c) for c in range(2)]
+    observed = [from_gap(c) for c in range(2)]
+    mask = jnp.where(reached, from_gap(2), 0.0)
     ice = mask != 0.0
-    friction = jnp.where(mask == 1.0, jnp.exp(column_input(4)), 0.0)
+    friction = jnp.where(mask == 1.0, jnp.exp(from_line(2)), 0.0)
 
     def stencil(k, keep):
         u, v = field[0, k], field[1, k]
@@ -273,25 +348,43 @@
     adjoint = repeat(plan, layers - 1, second_back, second_top)
     adjoint = [jnp.where(ice, adjoint[c], 0.0) for c in range(2)]
     gradient = -friction * (base[0] * adjoint[0] + base[1] * adjoint[1])
-    misfit_part = jnp.where(centre, mismatch[0] * mismatch[0] + mismatch[1] * mismatch[1], 0.0)
-    grad_part = jnp.where(centre, gradient * gradient, 0.0)
-    misfit_row = jnp.broadcast_to(jnp.sum(misfit_part, axis=0, keepdims=True), shape)
-    grad_row = jnp.broadcast_to(jnp.sum(grad_part, axis=0, keepdims=True), shape)
+
+    def partial_sum(value):
+        line = jnp.sum(jnp.where(centre, value, 0.0), axis=0, keepdims=True)
+        folded = line
+        for r in range(1, rows):
+            folded = folded + lane_roll(line, r * width)
+        return jnp.broadcast_to(lane_roll(folded, plan.cols), shape)
+
+    misfit_line = partial_sum(mismatch[0] * mismatch[0] + mismatch[1] * mismatch[1])
+    grad_line = partial_sum(gradient * gradient)
+    in_first = jnp.logical_and(lane >= plan.halo + plan.cols, lane < plan.halo + 2 * plan.cols)
+    last_row = jnp.where(centre, gradient, jnp.where(in_first, misfit_line, grad_line))
     for part in range(plan.layer_size):
-        for n, plane in enumerate((gradient, misfit_row, grad_row)):
-            out_ref[pl.ds(part * plan.out_rows + here + n, size, stride=plan.layer_size * plan.out_rows), :] = plane
-
-
-def unpack_kernel(plan, in_ref, log_ref, vel_ref, friction_ref, misfit_ref, grad_ref):
+        out_ref[pl.ds(part * plan.out_rows + here, size, stride=plan.layer_size * plan.out_rows), :] = last_row
+
+
+def unpack_kernel(
+    plan, in_ref, log_ref, vel_hbm, friction_hbm, misfit_hbm,
+    vel_ref, friction_ref, misfit_ref, grad_ref, leave,
+):
     here, width, cols = plan.layers_here, plan.width, plan.cols
     lane = lax.broadcasted_iota(jnp.int32, (plan.out_rows, LANES), 1)
-    total = jnp.zeros((plan.out_rows, LANES), jnp.float32)
-
-    def chunk(i, total):
-        blocks = [in_ref[i * plan.per_chunk + t] for t in range(plan.per_chunk)]
-        span = pl.ds(pl.multiple_of(i * LANES, LANES), LANES)
-        for r in range(plan.rows):
-            for c in range(2):
+
+    def block_at(i, t):
+        at = i * plan.per_chunk * plan.out_rows
+        if not isinstance(at, int):
+            at = pl.multiple_of(at, 8)
+        return in_ref[pl.ds(at + t * plan.out_rows, plan.out_rows), :]
+
+    def component(c):
+        def chunk(i, total):
+            blocks = [block_at(i, t) for t in range(plan.per_chunk)]
+            start = i * LANES
+            if not isinstance(start, int):
+                start = pl.multiple_of(start, LANES)
+            span = pl.ds(start, LANES)
+            for r in range(plan.rows):
                 start = r * width + plan.halo + c * cols
                 row = None
                 for t in range(plan.per_chunk):
@@ -301,36 +394,68 @@
                     vel_ref[c, k, r : r + 1, span] = row[k : k + 1, :]
                 if c == 0:
                     grad_ref[r : r + 1, span] = row[here : here + 1, :]
-        for block in blocks:
-            total = total + block
-        return total
-
-    total = repeat(plan, plan.chunks, chunk, total)
-    sums = jnp.sum(total, axis=1, keepdims=True)
-    misfit_ref[...] = 0.5 * sums[here + 1 : here + 2, :] / plan.column_count
-    scale = step_size / jnp.sqrt(sums[here + 2 : here + 3, :] / plan.column_count + 1e-06)
+            if c == 0:
+                for block in blocks:
+                    total = total + block
+            return total
+
+        return repeat(plan, plan.chunks, chunk, jnp.zeros((plan.out_rows, LANES), jnp.float32))
+
+    out = [pltpu.make_async_copy(vel_ref.at[c], vel_hbm.at[c], leave.at[c]) for c in range(2)]
+    out.append(pltpu.make_async_copy(friction_ref, friction_hbm, leave.at[2]))
+    out.append(pltpu.make_async_copy(misfit_ref, misfit_hbm, leave.at[3]))
+
+    total = component(0)[here:, :]
+    out[0].start()
+
+    def summed(first):
+        ahead = (lane[here:, :] + (LANES - first % LANES)) % LANES
+        return jnp.sum(jnp.where(ahead < cols, total, 0.0), axis=1, keepdims=True)
+
+    misfit_sum = summed(plan.halo + cols)
+    grad_sum = summed(plan.halo + cols + width)
+    misfit_ref[...] = 0.5 * misfit_sum / plan.column_count
+    scale = step_size / jnp.sqrt(grad_sum / plan.column_count + 1e-06)
     first = pl.multiple_of(lax.axis_index("layer") * plan.local_cols, LANES)
-    gradient = grad_ref[:, pl.ds(first, plan.local_cols)]
-    friction_ref[...] = log_ref[...] - gradient * scale
+    friction_ref[...] = log_ref[...] - grad_ref[:, pl.ds(first, plan.local_cols)] * scale
+    out[2].start()
+    out[3].start()
+    component(1)
+    out[1].start()
+    for copy in out:
+        copy.wait()
 
 
 def on_device(mesh_shape, velocity_init, driving, observed, log_friction, ice_mask):
     plan = Plan(mesh_shape, velocity_init.shape)
     vmem = pl.BlockSpec(memory_space=pltpu.VMEM)
+    hbm = pl.BlockSpec(memory_space=pltpu.HBM)
     f32 = jnp.float32
     limit = pltpu.CompilerParams(vmem_limit_bytes=(16 if plan.unrolled else 40) * MIB)
+    inputs = (velocity_init, driving, observed, log_friction, ice_mask)
+
+    def exchange(blocks, unit):
+        shaped = blocks.reshape(blocks.shape[0] // unit, unit, LANES)
+        return lax.all_to_all(shaped, ("map", "layer"), split_axis=0, concat_axis=0, tiled=True).reshape(blocks.shape)
 
     packed = pl.pallas_call(
         functools.partial(pack_kernel, plan),
-        out_shape=jax.ShapeDtypeStruct((plan.devices, plan.in_rows, LANES), f32),
-        in_specs=[vmem] * 5,
-        out_specs=vmem,
-        scratch_shapes=[pltpu.VMEM((plan.rows, plan.in_rows, plan.ny + 2 * LANES), f32)],
-        compiler_params=limit,
+        out_shape=jax.ShapeDtypeStruct((plan.devices * plan.in_rows, LANES), f32),
+        in_specs=[hbm] * 5,
+        out_specs=hbm,
+        scratch_shapes=[pltpu.VMEM(x.shape, x.dtype) for x in inputs]
+        + [
+            pltpu.VMEM((plan.devices * plan.in_rows, LANES), f32),
+            pltpu.VMEM((plan.rows, plan.vel_rows + 8, plan.ny + 2 * LANES), f32),
+            pltpu.VMEM((3, plan.rows, plan.ny + 2 * LANES), f32),
+            pltpu.SemaphoreType.DMA((5,)),
+            pltpu.SemaphoreType.DMA((plan.chunks,)),
+        ],
+        compiler_params=pltpu.CompilerParams(vmem_limit_bytes=60 * MIB),
         name="pack",
-    )(velocity_init, driving, observed, log_friction, ice_mask)
-
-    windows = lax.all_to_all(packed, ("map", "layer"), split_axis=0, concat_axis=0, tiled=True)
+    )(*inputs)
+
+    windows = exchange(packed, 2)
 
     plane = (plan.layers, plan.map_size, LANES)
     solved = pl.pallas_call(
@@ -349,15 +474,9 @@
         ],
         compiler_params=limit,
         name="solve",
-    )(windows.reshape(plan.devices * plan.in_rows, LANES))
-
-    back = lax.all_to_all(
-        solved.reshape(plan.devices, plan.out_rows, LANES),
-        ("map", "layer"),
-        split_axis=0,
-        concat_axis=0,
-        tiled=True,
-    )
+    )(windows)
+
+    back = exchange(solved, 1)
 
     velocity, friction_new, misfit = pl.pallas_call(
         functools.partial(unpack_kernel, plan),
@@ -367,8 +486,14 @@
             jax.ShapeDtypeStruct((1, 1), f32),
         ),
         in_specs=[vmem] * 2,
-        out_specs=(vmem, vmem, vmem),
-        scratch_shapes=[pltpu.VMEM((plan.rows, plan.ny), f32)],
+        out_specs=(hbm, hbm, hbm),
+        scratch_shapes=[
+            pltpu.VMEM(velocity_init.shape, f32),
+            pltpu.VMEM(log_friction.shape, f32),
+            pltpu.VMEM((1, 1), f32),
+            pltpu.VMEM((plan.rows, plan.ny), f32),
+            pltpu.SemaphoreType.DMA((4,)),
+        ],
         compiler_params=limit,
         name="unpack",
     )(back, log_friction)

time: 35.2 us -> 31.9 us (0.906)
  local copies, waits for them, and re-layouts: 3.57 us -> 0.01 us
  Pallas kernels: 2.32 us -> 5.3 us
  blocking collectives: 28.3 us -> 25.7 us
    unnamed x12 -> x2, local copies, waits for them, and re-layouts: 3.57 us -> 0.01 us
    pallas_call x1, Pallas kernels: 0.22 us -> 3.07 us  [on_device(): pl.pallas_call(functools.partial(pack_kernel, plan), out_shape=jax.ShapeD...]
    all_to_all x2, blocking collectives: 28.3 us -> 25.7 us  [exchange(): lax.all_to_all(shaped, ('map', 'layer'), split_axis=0, concat_axis=0, til...]
where the time goes in v2:
time: 31.9 us; the launch traced here: 31.7 us
  blocking collectives  25.7 us (81%)
  Pallas kernels  5.3 us (17%)
  between operations  0.64 us (2%)
    all_to_all x2, blocking collectives, exchange(): lax.all_to_all(shaped, ('map', 'layer'), split_axis=0, concat_axis=0, til...  25.7 us
    pallas_call x1, Pallas kernels, on_device(): pl.pallas_call(functools.partial(pack_kernel, plan), out_shape=jax.ShapeD...  3.07 us
    pallas_call x1, Pallas kernels, on_device(): pl.pallas_call(functools.partial(solve_kernel, plan), out_shape=jax.Shape...  1.35 us
    pallas_call x1, Pallas kernels, on_device(): pl.pallas_call(functools.partial(unpack_kernel, plan), out_shape=(jax.Sha...  0.88 us

profile of v2, /device:TPU:0, one launch (start us, length us, event | category | flops | bytes accessed | tf_op | source)
XLA Modules:
  0.0 31.7 jit_solution(2234175785033952793)
XLA Ops:
  0.6 3.1 %pack.1 = f32[320,128]{1,0:T(8,128)} custom-call(f32[2,4,2,1024]{3,2,1,0:T(2,128)} %vel_hbm.1, f32[2,2,256]{2,1,0:T(2,128)} %driving_hbm.1, f32[2,2,256]{2,1,0:T(2,128)} %observed_hbm.1, f32[2,256]{1,0:T(2,128)} %log_ref.1, s32[2,256]{1,0:T(2,128)} %mask_hbm.1), custom_call_target="tpu_custom_call" | custom-call | tf_op jit(solution)/shard_map/pack/pallas_call | solution.py:441
  3.7 16.2 %all_to_all.10 = f32[160,2,128]{2,1,0:T(2,128)S(1)} all-to-all(f32[160,2,128]{2,1,0:T(2,128)} %bitcast.10), channel_id=1, replica_groups=mesh['map'=8,'layer'=4] {'map','layer'}, dimensions={0} | all-to-all | bytes 327680 | tf_op jit(solution)/shard_map/all_to_all | solution.py:439
  19.9 1.3 %solve.1 = f32[160,128]{1,0:T(8,128)S(1)} custom-call(f32[320,128]{1,0:T(8,128)S(1)} %bitcast.7), custom_call_target="tpu_custom_call" | custom-call | tf_op jit(solution)/shard_map/solve/pallas_call | solution.py:461
  21.2 0.0 copy-start
  21.2 9.5 %all_to_all.11 = f32[160,1,128]{2,1,0:T(1,128)S(1)} all-to-all(f32[160,1,128]{2,1,0:T(1,128)S(1)} %bitcast.9), channel_id=1, replica_groups=mesh['map'=8,'layer'=4] {'map','layer'}, dimensions={0} | all-to-all | bytes 163840 | tf_op jit(solution)/shard_map/all_to_all | solution.py:439
  30.8 0.0 copy-done
  30.8 0.9 %unpack.1 = (f32[2,4,2,1024]{3,2,1,0:T(2,128)}, f32[2,256]{1,0:T(2,128)}, f32[1,1]{1,0:T(1,128)}) custom-call(f32[160,128]{1,0:T(8,128)S(1)} %bitcast.8, f32[2,256]{1,0:T(2,128)S(1)} %copy-done), custom_call_target="tpu_custom_call" | custom-call | tf_op jit(solution)/shard_map/unpack/pallas_call | solution.py:481
Async XLA Ops:
  21.2 9.6 %copy-start = (f32[2,256]{1,0:T(2,128)S(1)}, f32[2,256]{1,0:T(2,128)}, u32[]{:S(2)}) copy-start(f32[2,256]{1,0:T(2,128)} %log_ref.1) | copy-start | bytes 6148

commit v3 on v2

--- a/solution.py
+++ b/solution.py
@@ -59,8 +59,8 @@
 
 
 def pack_kernel(
-    plan, vel_hbm, driving_hbm, observed_hbm, log_hbm, mask_hbm, out_hbm,
-    vel_ref, driving_ref, observed_ref, log_ref, mask_ref, out_ref, held, bed, arrival, leave,
+    plan, vel_hbm, driving_hbm, observed_hbm, log_hbm, mask_hbm, out_ref,
+    vel_ref, driving_ref, observed_ref, log_ref, mask_ref, held, bed, arrival,
 ):
     width, rows, wide = plan.width, plan.rows, plan.wide
     copies = [
@@ -104,11 +104,6 @@
 
     chunk_rows = plan.per_chunk * plan.in_rows
 
-    def leaving(i):
-        start = i * chunk_rows
-        span = pl.ds(start if isinstance(i, int) else pl.multiple_of(start, 8), chunk_rows)
-        return pltpu.make_async_copy(out_ref.at[span, :], out_hbm.at[span, :], leave.at[i])
-
     def chunk_windows(i, carry):
         def window(read, relative, length, lanes):
             step, offset = relative // LANES, relative % LANES
@@ -147,16 +142,9 @@
             at = at + t * plan.in_rows
             out_ref[pl.ds(at, plan.vel_rows), :] = block
             out_ref[pl.ds(at + plan.vel_rows, rows), :] = line
-        leaving(i).start()
         return carry
 
     repeat(plan, plan.chunks, chunk_windows)
-
-    def left(i, carry):
-        leaving(i).wait()
-        return carry
-
-    repeat(plan, plan.chunks, left)
 
 
 def solve_kernel(plan, in_ref, out_ref, field, eta_ref, side, rhs, faces, ratio, inverse):
@@ -442,18 +430,16 @@
         functools.partial(pack_kernel, plan),
         out_shape=jax.ShapeDtypeStruct((plan.devices * plan.in_rows, LANES), f32),
         in_specs=[hbm] * 5,
-        out_specs=hbm,
+        out_specs=vmem,
         scratch_shapes=[pltpu.VMEM(x.shape, x.dtype) for x in inputs]
         + [
-            pltpu.VMEM((plan.devices * plan.in_rows, LANES), f32),
             pltpu.VMEM((plan.rows, plan.vel_rows + 8, plan.ny + 2 * LANES), f32),
             pltpu.VMEM((3, plan.rows, plan.ny + 2 * LANES), f32),
             pltpu.SemaphoreType.DMA((5,)),
-            pltpu.SemaphoreType.DMA((plan.chunks,)),
         ],
-        compiler_params=pltpu.CompilerParams(vmem_limit_bytes=60 * MIB),
+        compiler_params=limit,
         name="pack",
-    )(*inputs)
+    )(*(pltpu.with_memory_space_constraint(x, pltpu.HBM) for x in inputs))
 
     windows = exchange(packed, 2)
 

time: 31.9 us -> 31.1 us (0.975)
  Pallas kernels: 5.3 us -> 4.69 us
    pallas_call x1, Pallas kernels: 3.07 us -> 2.46 us  [on_device(): pl.pallas_call(functools.partial(pack_kernel, plan), out_shape=jax.ShapeD...]
where the time goes in v3:
time: 31.1 us; the launch traced here: 30.9 us
  blocking collectives  25.5 us (82%)
  Pallas kernels  4.69 us (15%)
  between operations  0.64 us (2%)
    all_to_all x2, blocking collectives, exchange(): lax.all_to_all(shaped, ('map', 'layer'), split_axis=0, concat_axis=0, til...  25.5 us
    pallas_call x1, Pallas kernels, on_device(): pl.pallas_call(functools.partial(pack_kernel, plan), out_shape=jax.ShapeD...  2.46 us
    pallas_call x1, Pallas kernels, on_device(): pl.pallas_call(functools.partial(solve_kernel, plan), out_shape=jax.Shape...  1.35 us
    pallas_call x1, Pallas kernels, on_device(): pl.pallas_call(functools.partial(unpack_kernel, plan), out_shape=(jax.Sha...  0.88 us

profile of v3, /device:TPU:0, one launch (start us, length us, event | category | flops | bytes accessed | tf_op | source)
XLA Modules:
  0.0 30.9 jit_solution(14504865532107149975)
XLA Ops:
  0.6 2.5 %pack.1 = f32[320,128]{1,0:T(8,128)S(1)} custom-call(f32[2,4,2,1024]{3,2,1,0:T(2,128)} %vel_hbm.1, f32[2,2,256]{2,1,0:T(2,128)} %driving_hbm.1, f32[2,2,256]{2,1,0:T(2,128)} %observed_hbm.1, f32[2,256]{1,0:T(2,128)} %log_ref.1, s32[2,256]{1,0:T(2,128)} %mask_hbm.1), custom_call_target="tpu_custom_call" | custom-call | tf_op jit(solution)/shard_map/pack/pallas_call | solution.py:429
  3.1 16.0 %all_to_all.10 = f32[160,2,128]{2,1,0:T(2,128)S(1)} all-to-all(f32[160,2,128]{2,1,0:T(2,128)S(1)} %bitcast.8), channel_id=1, replica_groups=mesh['map'=8,'layer'=4] {'map','layer'}, dimensions={0} | all-to-all | bytes 327680 | tf_op jit(solution)/shard_map/all_to_all | solution.py:427
  19.1 1.3 %solve.1 = f32[160,128]{1,0:T(8,128)S(1)} custom-call(f32[320,128]{1,0:T(8,128)S(1)} %bitcast.7), custom_call_target="tpu_custom_call" | custom-call | tf_op jit(solution)/shard_map/solve/pallas_call | solution.py:447
  20.4 0.0 copy-start
  20.4 9.5 %all_to_all.11 = f32[160,1,128]{2,1,0:T(1,128)S(1)} all-to-all(f32[160,1,128]{2,1,0:T(1,128)S(1)} %bitcast.10), channel_id=1, replica_groups=mesh['map'=8,'layer'=4] {'map','layer'}, dimensions={0} | all-to-all | bytes 163840 | tf_op jit(solution)/shard_map/all_to_all | solution.py:427
  30.0 0.0 copy-done
  30.0 0.9 %unpack.1 = (f32[2,4,2,1024]{3,2,1,0:T(2,128)}, f32[2,256]{1,0:T(2,128)}, f32[1,1]{1,0:T(1,128)}) custom-call(f32[160,128]{1,0:T(8,128)S(1)} %bitcast.9, f32[2,256]{1,0:T(2,128)S(1)} %copy-done), custom_call_target="tpu_custom_call" | custom-call | tf_op jit(solution)/shard_map/unpack/pallas_call | solution.py:467
Async XLA Ops:
  20.4 9.6 %copy-start = (f32[2,256]{1,0:T(2,128)S(1)}, f32[2,256]{1,0:T(2,128)}, u32[]{:S(2)}) copy-start(f32[2,256]{1,0:T(2,128)} %log_ref.1) | copy-start | bytes 6148

commit v4 on v3

--- a/solution.py
+++ b/solution.py
@@ -136,15 +136,12 @@
                 value, offset = window(lambda span: bed[n, :, span], plan.cols * t - REACH, wide, bed_lane)
                 value = lane_roll(value, n * wide - offset)
                 line = value if line is None else jnp.where(bed_lane >= n * wide, value, line)
-            at = i * chunk_rows
-            if not isinstance(at, int):
-                at = pl.multiple_of(at, 8)
-            at = at + t * plan.in_rows
+            at = pl.multiple_of(i * chunk_rows, 8) + t * plan.in_rows
             out_ref[pl.ds(at, plan.vel_rows), :] = block
             out_ref[pl.ds(at + plan.vel_rows, rows), :] = line
         return carry
 
-    repeat(plan, plan.chunks, chunk_windows)
+    lax.fori_loop(0, plan.chunks, chunk_windows, 0)
 
 
 def solve_kernel(plan, in_ref, out_ref, field, eta_ref, side, rhs, faces, ratio, inverse):

time: 31.1 us -> 30.7 us (0.987)
  Pallas kernels: 4.69 us -> 4.34 us
    pallas_call x1, Pallas kernels: 2.46 us -> 2.11 us  [on_device(): pl.pallas_call(functools.partial(pack_kernel, plan), out_shape=jax.ShapeD...]
where the time goes in v4:
time: 30.7 us; the launch traced here: 30.5 us
  blocking collectives  25.5 us (83%)
  Pallas kernels  4.34 us (14%)
  between operations  0.64 us (2%)
    all_to_all x2, blocking collectives, exchange(): lax.all_to_all(shaped, ('map', 'layer'), split_axis=0, concat_axis=0, til...  25.5 us
    pallas_call x1, Pallas kernels, on_device(): pl.pallas_call(functools.partial(pack_kernel, plan), out_shape=jax.ShapeD...  2.11 us
    pallas_call x1, Pallas kernels, on_device(): pl.pallas_call(functools.partial(solve_kernel, plan), out_shape=jax.Shape...  1.35 us
    pallas_call x1, Pallas kernels, on_device(): pl.pallas_call(functools.partial(unpack_kernel, plan), out_shape=(jax.Sha...  0.88 us

profile of v4, /device:TPU:0, one launch (start us, length us, event | category | flops | bytes accessed | tf_op | source)
XLA Modules:
  0.0 30.5 jit_solution(616033591546910419)
XLA Ops:
  0.6 2.1 %pack.1 = f32[320,128]{1,0:T(8,128)S(1)} custom-call(f32[2,4,2,1024]{3,2,1,0:T(2,128)} %vel_hbm.1, f32[2,2,256]{2,1,0:T(2,128)} %driving_hbm.1, f32[2,2,256]{2,1,0:T(2,128)} %observed_hbm.1, f32[2,256]{1,0:T(2,128)} %log_ref.1, s32[2,256]{1,0:T(2,128)} %mask_hbm.1), custom_call_target="tpu_custom_call" | custom-call | tf_op jit(solution)/shard_map/pack/pallas_call | solution.py:426
  2.8 16.0 %all_to_all.10 = f32[160,2,128]{2,1,0:T(2,128)S(1)} all-to-all(f32[160,2,128]{2,1,0:T(2,128)S(1)} %bitcast.8), channel_id=1, replica_groups=mesh['map'=8,'layer'=4] {'map','layer'}, dimensions={0} | all-to-all | bytes 327680 | tf_op jit(solution)/shard_map/all_to_all | solution.py:424
  18.7 1.3 %solve.1 = f32[160,128]{1,0:T(8,128)S(1)} custom-call(f32[320,128]{1,0:T(8,128)S(1)} %bitcast.7), custom_call_target="tpu_custom_call" | custom-call | tf_op jit(solution)/shard_map/solve/pallas_call | solution.py:444
  20.1 0.0 copy-start
  20.1 9.5 %all_to_all.11 = f32[160,1,128]{2,1,0:T(1,128)S(1)} all-to-all(f32[160,1,128]{2,1,0:T(1,128)S(1)} %bitcast.10), channel_id=1, replica_groups=mesh['map'=8,'layer'=4] {'map','layer'}, dimensions={0} | all-to-all | bytes 163840 | tf_op jit(solution)/shard_map/all_to_all | solution.py:424
  29.6 0.0 copy-done
  29.6 0.9 %unpack.1 = (f32[2,4,2,1024]{3,2,1,0:T(2,128)}, f32[2,256]{1,0:T(2,128)}, f32[1,1]{1,0:T(1,128)}) custom-call(f32[160,128]{1,0:T(8,128)S(1)} %bitcast.9, f32[2,256]{1,0:T(2,128)S(1)} %copy-done), custom_call_target="tpu_custom_call" | custom-call | tf_op jit(solution)/shard_map/unpack/pallas_call | solution.py:464
Async XLA Ops:
  20.1 9.6 %copy-start = (f32[2,256]{1,0:T(2,128)S(1)}, f32[2,256]{1,0:T(2,128)}, u32[]{:S(2)}) copy-start(f32[2,256]{1,0:T(2,128)} %log_ref.1) | copy-start | bytes 6148

commit v5 on v3

--- a/solution.py
+++ b/solution.py
@@ -60,91 +60,129 @@
 
 def pack_kernel(
     plan, vel_hbm, driving_hbm, observed_hbm, log_hbm, mask_hbm, out_ref,
-    vel_ref, driving_ref, observed_ref, log_ref, mask_ref, held, bed, arrival,
+    vel_ref, driving_ref, observed_ref, log_ref, mask_ref, arrival,
 ):
-    width, rows, wide = plan.width, plan.rows, plan.wide
-    copies = [
-        pltpu.make_async_copy(source, target, arrival.at[n])
-        for n, (source, target) in enumerate(
-            (
-                (vel_hbm, vel_ref),
-                (driving_hbm, driving_ref),
-                (observed_hbm, observed_ref),
-                (log_hbm, log_ref),
-                (mask_hbm, mask_ref),
-            )
-        )
-    ]
+    width, rows, wide, half = plan.width, plan.rows, plan.wide, plan.half
+    pairs = (
+        (vel_hbm, vel_ref),
+        (driving_hbm, driving_ref),
+        (observed_hbm, observed_ref),
+        (log_hbm, log_ref),
+        (mask_hbm, mask_ref),
+    )
+    copies = [pltpu.make_async_copy(pair[0], pair[1], arrival.at[n]) for n, pair in enumerate(pairs)]
     for copy in copies:
         copy.start()
-    held[...] = jnp.zeros_like(held)
-    bed[...] = jnp.zeros_like(bed)
-    first = pl.multiple_of(LANES + lax.axis_index("layer") * plan.local_cols, LANES)
-    here = pl.ds(first, plan.local_cols)
-    for copy in copies:
-        copy.wait()
-    for r in range(rows):
-        for c in range(2):
-            for k in range(plan.layers_here):
-                held[r, c * plan.layers_here + k : c * plan.layers_here + k + 1, LANES : LANES + plan.ny] = vel_ref[
-                    c, k, r : r + 1, :
-                ]
-        mask = mask_ref[r : r + 1, :].astype(jnp.float32)
-        for n, value in enumerate((observed_ref[0, r : r + 1, :], observed_ref[1, r : r + 1, :], mask)):
-            held[r, plan.vel_rows + 2 * n : plan.vel_rows + 2 * n + 1, here] = value
-            held[r, plan.vel_rows + 2 * n + 1 : plan.vel_rows + 2 * n + 2, here] = value
-    for n, value in enumerate((driving_ref[0], driving_ref[1], log_ref[...])):
-        bed[n, :, here] = value
-
     shape = (plan.vel_rows, LANES)
     lane = lax.broadcasted_iota(jnp.int32, shape, 1)
-    odd = lax.broadcasted_iota(jnp.int32, shape, 0) % 2 == 1
+    sub = lax.broadcasted_iota(jnp.int32, shape, 0)
     in_gap = jnp.logical_not(jnp.logical_and(lane % width >= plan.low, lane % width < plan.gap))
-    bed_lane = lax.broadcasted_iota(jnp.int32, (rows, LANES), 1)
-
-    chunk_rows = plan.per_chunk * plan.in_rows
+    no_line = jnp.zeros((rows, LANES), jnp.float32)
+
+    def slide(part, start, length, place):
+        step, offset = start // LANES, start % LANES
+        value = part(step)
+        if offset + length > LANES:
+            after = part(step + 1)
+            value = jnp.where(lax.broadcasted_iota(jnp.int32, value.shape, 1) >= offset, value, after)
+        return lane_roll(value, place - offset)
+
+    copies[0].wait()
 
     def chunk_windows(i, carry):
-        def window(read, relative, length, lanes):
-            step, offset = relative // LANES, relative % LANES
-
-            def part(at):
-                return read(pl.ds(pl.multiple_of((i + 1 + at) * LANES, LANES), LANES))
-
-            if offset + length <= LANES:
-                return part(step), offset
-            return jnp.where(lanes >= offset, part(step), part(step + 1)), offset
-
-        def side_by_side(row_base, t):
+        def velocity(r):
+            def part(step):
+                chunk = i + step
+                if isinstance(chunk, int) and not 0 <= chunk < plan.chunks:
+                    return jnp.zeros(shape, jnp.float32)
+                at = chunk if isinstance(chunk, int) else jnp.clip(chunk, 0, plan.chunks - 1)
+                value = vel_ref[pl.ds(at * rows + r, plan.vel_rows, stride=plan.chunks * rows), :]
+                if isinstance(chunk, int):
+                    return value
+                return jnp.where(jnp.logical_and(chunk >= 0, chunk < plan.chunks), value, 0.0)
+
+            return part
+
+        for t in range(plan.per_chunk):
             block = None
             for r in range(rows):
-                value, offset = window(
-                    lambda span: held[r, row_base : row_base + 8, span], plan.cols * t - plan.halo, width, lane
-                )
-                value = lane_roll(value, r * width - offset)
+                value = slide(velocity(r), plan.cols * t - plan.halo, width, r * width)
                 block = value if block is None else jnp.where(lane >= r * width, value, block)
-            return block
-
-        for t in range(plan.per_chunk):
-            block = side_by_side(0, t)
-            other = side_by_side(plan.vel_rows, t)
-            shift = plan.gap - plan.low
-            other = jnp.where(odd, lane_roll(other, shift - plan.half), lane_roll(other, shift))
-            block = jnp.where(in_gap, other, block)
-            line = None
-            for n in range(3):
-                value, offset = window(lambda span: bed[n, :, span], plan.cols * t - REACH, wide, bed_lane)
-                value = lane_roll(value, n * wide - offset)
-                line = value if line is None else jnp.where(bed_lane >= n * wide, value, line)
-            at = i * chunk_rows
+            at = i * plan.per_chunk * plan.in_rows
             if not isinstance(at, int):
                 at = pl.multiple_of(at, 8)
             at = at + t * plan.in_rows
-            out_ref[pl.ds(at, plan.vel_rows), :] = block
-            out_ref[pl.ds(at + plan.vel_rows, rows), :] = line
+            out_ref[pl.ds(at, plan.vel_rows), :] = jnp.where(in_gap, 0.0, block)
+            out_ref[pl.ds(at + plan.vel_rows, rows), :] = no_line
         return carry
 
     repeat(plan, plan.chunks, chunk_windows)
+    for copy in copies[1:]:
+        copy.wait()
+
+    place = lax.axis_index("layer")
+    local_chunks = plan.local_cols // LANES
+
+    def line_part(ref, row):
+        def part(step):
+            if not 0 <= step < local_chunks:
+                return no_line
+            return ref[row + step * rows : row + (step + 1) * rows, :]
+
+        return part
+
+    def gap_part(r):
+        def part(step):
+            if not 0 <= step < local_chunks:
+                return jnp.zeros(shape, jnp.float32)
+            at = step * rows + r
+            skip = local_chunks * rows
+            first = jnp.broadcast_to(observed_ref[at : at + 1, :], shape)
+            second = jnp.broadcast_to(observed_ref[skip + at : skip + at + 1, :], shape)
+            third = jnp.broadcast_to(mask_ref[at : at + 1, :], shape).astype(jnp.float32)
+            return jnp.where(sub < 2, first, jnp.where(sub < 4, second, third))
+
+        return part
+
+    gap_parts = [[gap_part(r)(step) for step in range(-1, local_chunks + 1)] for r in range(rows)]
+    own = plan.local_cols // plan.cols
+    spill = -(-REACH // plan.cols)
+
+    def column_block(q):
+        start = q * plan.cols - REACH
+        line = None
+        for n, part in enumerate(
+            (line_part(driving_ref, 0), line_part(driving_ref, local_chunks * rows), line_part(log_ref, 0))
+        ):
+            value = slide(part, start, wide, n * wide)
+            lanes = lax.broadcasted_iota(jnp.int32, value.shape, 1)
+            line = value if line is None else jnp.where(lanes >= n * wide, value, line)
+        block = None
+        for r in range(rows):
+            halves = [
+                slide(lambda step: gap_parts[r][step + 1], start + h * half, half, (r * width + plan.gap) % LANES)
+                for h in range(2)
+            ]
+            value = jnp.where(sub % 2 == 0, halves[0], halves[1])
+            ahead = (lane + (LANES - plan.gap)) % LANES
+            block = value if block is None else jnp.where(ahead >= r * width, value, block)
+        at = pl.multiple_of(place * (own * plan.in_rows), 8) + q * plan.in_rows
+        here = pl.ds(at, plan.vel_rows)
+        out_ref[here, :] = jnp.where(in_gap, block, out_ref[here, :])
+        out_ref[pl.ds(at + plan.vel_rows, rows), :] = line
+
+    for q in range(own):
+        column_block(q)
+
+    @pl.when(place > 0)
+    def _():
+        for q in range(-spill, 0):
+            column_block(q)
+
+    @pl.when(place < plan.layer_size - 1)
+    def _():
+        for q in range(own, own + spill):
+            column_block(q)
 
 
 def solve_kernel(plan, in_ref, out_ref, field, eta_ref, side, rhs, faces, ratio, inverse):
@@ -356,62 +394,68 @@
     plan, in_ref, log_ref, vel_hbm, friction_hbm, misfit_hbm,
     vel_ref, friction_ref, misfit_ref, grad_ref, leave,
 ):
-    here, width, cols = plan.layers_here, plan.width, plan.cols
-    lane = lax.broadcasted_iota(jnp.int32, (plan.out_rows, LANES), 1)
-
-    def block_at(i, t):
-        at = i * plan.per_chunk * plan.out_rows
-        if not isinstance(at, int):
-            at = pl.multiple_of(at, 8)
-        return in_ref[pl.ds(at + t * plan.out_rows, plan.out_rows), :]
-
-    def component(c):
-        def chunk(i, total):
-            blocks = [block_at(i, t) for t in range(plan.per_chunk)]
-            start = i * LANES
-            if not isinstance(start, int):
-                start = pl.multiple_of(start, LANES)
-            span = pl.ds(start, LANES)
-            for r in range(plan.rows):
-                start = r * width + plan.halo + c * cols
-                row = None
-                for t in range(plan.per_chunk):
-                    moved = lane_roll(blocks[t], t * cols - start)
-                    row = moved if row is None else jnp.where(lane >= t * cols, moved, row)
-                for k in range(here):
-                    vel_ref[c, k, r : r + 1, span] = row[k : k + 1, :]
-                if c == 0:
-                    grad_ref[r : r + 1, span] = row[here : here + 1, :]
-            if c == 0:
-                for block in blocks:
-                    total = total + block
-            return total
-
-        return repeat(plan, plan.chunks, chunk, jnp.zeros((plan.out_rows, LANES), jnp.float32))
-
-    out = [pltpu.make_async_copy(vel_ref.at[c], vel_hbm.at[c], leave.at[c]) for c in range(2)]
-    out.append(pltpu.make_async_copy(friction_ref, friction_hbm, leave.at[2]))
-    out.append(pltpu.make_async_copy(misfit_ref, misfit_hbm, leave.at[3]))
-
-    total = component(0)[here:, :]
-    out[0].start()
+    here, width, cols, rows = plan.layers_here, plan.width, plan.cols, plan.rows
+    local_chunks = plan.local_cols // LANES
+
+    total = jnp.sum(
+        in_ref[pl.ds(here, plan.devices, stride=plan.out_rows), :].astype(jnp.float32), axis=0, keepdims=True
+    )
+    line_lane = lax.broadcasted_iota(jnp.int32, (1, LANES), 1)
 
     def summed(first):
-        ahead = (lane[here:, :] + (LANES - first % LANES)) % LANES
+        ahead = (line_lane + (LANES - first % LANES)) % LANES
         return jnp.sum(jnp.where(ahead < cols, total, 0.0), axis=1, keepdims=True)
 
     misfit_sum = summed(plan.halo + cols)
     grad_sum = summed(plan.halo + cols + width)
     misfit_ref[...] = 0.5 * misfit_sum / plan.column_count
     scale = step_size / jnp.sqrt(grad_sum / plan.column_count + 1e-06)
-    first = pl.multiple_of(lax.axis_index("layer") * plan.local_cols, LANES)
-    friction_ref[...] = log_ref[...] - grad_ref[:, pl.ds(first, plan.local_cols)] * scale
+
+    lane = lax.broadcasted_iota(jnp.int32, (plan.out_rows, LANES), 1)
+    starts = [(r, c, r * width + plan.halo + c * cols) for r in range(rows) for c in range(2)]
+
+    def chunk(i, carry):
+        at = i * plan.per_chunk * plan.out_rows
+        if not isinstance(at, int):
+            at = pl.multiple_of(at, 8)
+        turned = [
+            lane_roll(in_ref[pl.ds(at + t * plan.out_rows, plan.out_rows), :], t * cols)
+            for t in range(plan.per_chunk)
+        ]
+        for r, c, start in starts:
+            ahead = (lane + (LANES - start % LANES)) % LANES
+            row = turned[0]
+            for t in range(1, plan.per_chunk):
+                row = jnp.where(ahead >= t * cols, turned[t], row)
+            row = lane_roll(row, -start)
+            vel_ref[pl.ds(c * here * plan.chunks * rows + i * rows + r, here, stride=plan.chunks * rows), :] = row[:here]
+            if c == 0:
+                owner, step = i // local_chunks, i % local_chunks
+                grad_ref[owner, pl.ds(step * rows + r, 1), :] = row[here : here + 1]
+        return carry
+
+    repeat(plan, plan.chunks, chunk)
+    out = [
+        pltpu.make_async_copy(vel_ref, vel_hbm, leave.at[0]),
+        pltpu.make_async_copy(friction_ref, friction_hbm, leave.at[1]),
+        pltpu.make_async_copy(misfit_ref, misfit_hbm, leave.at[2]),
+    ]
+    out[0].start()
+    friction_ref[...] = log_ref[...] - grad_ref[lax.axis_index("layer")] * scale
+    out[1].start()
     out[2].start()
-    out[3].start()
-    component(1)
-    out[1].start()
     for copy in out:
         copy.wait()
+
+
+def as_lines(x):
+    chunked = x.reshape(x.shape[:-1] + (x.shape[-1] // LANES, LANES))
+    return jnp.swapaxes(chunked, -3, -2).reshape(-1, LANES)
+
+
+def from_lines(lines, shape):
+    chunked = lines.reshape(shape[:-2] + (shape[-1] // LANES, shape[-2], LANES))
+    return jnp.swapaxes(chunked, -3, -2).reshape(shape)
 
 
 def on_device(mesh_shape, velocity_init, driving, observed, log_friction, ice_mask):
@@ -420,7 +464,7 @@
     hbm = pl.BlockSpec(memory_space=pltpu.HBM)
     f32 = jnp.float32
     limit = pltpu.CompilerParams(vmem_limit_bytes=(16 if plan.unrolled else 40) * MIB)
-    inputs = (velocity_init, driving, observed, log_friction, ice_mask)
+    inputs = [as_lines(x) for x in (velocity_init, driving, observed, log_friction, ice_mask)]
 
     def exchange(blocks, unit):
         shaped = blocks.reshape(blocks.shape[0] // unit, unit, LANES)
@@ -433,8 +477,6 @@
         out_specs=vmem,
         scratch_shapes=[pltpu.VMEM(x.shape, x.dtype) for x in inputs]
         + [
-            pltpu.VMEM((plan.rows, plan.vel_rows + 8, plan.ny + 2 * LANES), f32),
-            pltpu.VMEM((3, plan.rows, plan.ny + 2 * LANES), f32),
             pltpu.SemaphoreType.DMA((5,)),
         ],
         compiler_params=limit,
@@ -464,26 +506,31 @@
 
     back = exchange(solved, 1)
 
+    vel_lines, log_lines = inputs[0], inputs[3]
     velocity, friction_new, misfit = pl.pallas_call(
         functools.partial(unpack_kernel, plan),
         out_shape=(
-            jax.ShapeDtypeStruct(velocity_init.shape, f32),
-            jax.ShapeDtypeStruct(log_friction.shape, f32),
+            jax.ShapeDtypeStruct(vel_lines.shape, f32),
+            jax.ShapeDtypeStruct(log_lines.shape, f32),
             jax.ShapeDtypeStruct((1, 1), f32),
         ),
         in_specs=[vmem] * 2,
         out_specs=(hbm, hbm, hbm),
         scratch_shapes=[
-            pltpu.VMEM(velocity_init.shape, f32),
-            pltpu.VMEM(log_friction.shape, f32),
+            pltpu.VMEM(vel_lines.shape, f32),
+            pltpu.VMEM(log_lines.shape, f32),
             pltpu.VMEM((1, 1), f32),
-            pltpu.VMEM((plan.rows, plan.ny), f32),
-            pltpu.SemaphoreType.DMA((4,)),
+            pltpu.VMEM((plan.layer_size,) + log_lines.shape, f32),
+            pltpu.SemaphoreType.DMA((3,)),
         ],
         compiler_params=limit,
         name="unpack",
-    )(back, log_friction)
-    return velocity, friction_new, misfit.reshape(())
+    )(back, log_lines)
+    return (
+        from_lines(velocity, velocity_init.shape),
+        from_lines(friction_new, log_friction.shape),
+        misfit.reshape(()),
+    )
 
 
 def solution(mesh):

time: 31.1 us -> 29.8 us (0.958)
  Pallas kernels: 4.69 us -> 3.46 us
    pallas_call x1, Pallas kernels: 2.46 us -> 1.24 us  [on_device(): pl.pallas_call(functools.partial(pack_kernel, plan), out_shape=jax.ShapeD...]
where the time goes in v5:
time: 29.8 us; the launch traced here: 29.6 us
  blocking collectives  25.5 us (86%)
  Pallas kernels  3.46 us (12%)
  between operations  0.64 us (2%)
    all_to_all x2, blocking collectives, exchange(): lax.all_to_all(shaped, ('map', 'layer'), split_axis=0, concat_axis=0, til...  25.5 us
    pallas_call x1, Pallas kernels, on_device(): pl.pallas_call(functools.partial(solve_kernel, plan), out_shape=jax.Shape...  1.35 us
    pallas_call x1, Pallas kernels, on_device(): pl.pallas_call(functools.partial(pack_kernel, plan), out_shape=jax.ShapeD...  1.24 us
    pallas_call x1, Pallas kernels, on_device(): pl.pallas_call(functools.partial(unpack_kernel, plan), out_shape=(jax.Sha...  0.87 us

profile of v5, /device:TPU:0, one launch (start us, length us, event | category | flops | bytes accessed | tf_op | source)
XLA Modules:
  0.0 29.6 jit_solution(12683942243544935017)
XLA Ops:
  0.6 1.2 %pack.1 = f32[320,128]{1,0:T(8,128)S(1)} custom-call(f32[128,128]{1,0:T(8,128)} %bitcast.48, f32[8,128]{1,0:T(8,128)} %bitcast.49, f32[8,128]{1,0:T(8,128)} %bitcast.50, f32[4,128]{1,0:T(4,128)} %bitcast.46, s32[4,128]{1,0:T(4,128)} %bitcast.51), custom_call_target="tpu_custom_call" | custom-call | tf_op jit(solution)/shard_map/pack/pallas_call | solution.py:473
  1.9 15.9 %all_to_all.10 = f32[160,2,128]{2,1,0:T(2,128)S(1)} all-to-all(f32[160,2,128]{2,1,0:T(2,128)S(1)} %bitcast.43), channel_id=1, replica_groups=mesh['map'=8,'layer'=4] {'map','layer'}, dimensions={0} | all-to-all | bytes 327680 | tf_op jit(solution)/shard_map/all_to_all | solution.py:471
  17.8 1.3 %solve.1 = f32[160,128]{1,0:T(8,128)S(1)} custom-call(f32[320,128]{1,0:T(8,128)S(1)} %bitcast.42), custom_call_target="tpu_custom_call" | custom-call | tf_op jit(solution)/shard_map/solve/pallas_call | solution.py:489
  19.2 0.0 copy-start
  19.2 9.5 %all_to_all.11 = f32[160,1,128]{2,1,0:T(1,128)S(1)} all-to-all(f32[160,1,128]{2,1,0:T(1,128)S(1)} %bitcast.45), channel_id=1, replica_groups=mesh['map'=8,'layer'=4] {'map','layer'}, dimensions={0} | all-to-all | bytes 163840 | tf_op jit(solution)/shard_map/all_to_all | solution.py:471
  28.7 0.0 copy-done
  28.7 0.9 %unpack.1 = (f32[128,128]{1,0:T(8,128)}, f32[4,128]{1,0:T(4,128)}, f32[1,1]{1,0:T(1,128)}) custom-call(f32[160,128]{1,0:T(8,128)S(1)} %bitcast.44, f32[4,128]{1,0:T(4,128)S(1)} %bitcast.47), custom_call_target="tpu_custom_call" | custom-call | tf_op jit(solution)/shard_map/unpack/pallas_call | solution.py:510
Async XLA Ops:
  19.2 9.6 %copy-start = (f32[2,256]{1,0:T(2,128)S(1)}, f32[2,256]{1,0:T(2,128)}, u32[]{:S(2)}) copy-start(f32[2,256]{1,0:T(2,128)} %param.8) | copy-start | bytes 6148

commit v6 on v5

--- a/solution.py
+++ b/solution.py
@@ -229,10 +229,6 @@
     def viscosity(rate):
         return jnp.exp2(jnp.log(strain_floor + rate) * (-1.0 / (3.0 * math.log(2.0))))
 
-    def reciprocal(value):
-        guess = pl.reciprocal(value, approx=True)
-        return guess * (2.0 - value * guess)
-
     for part in range(plan.layer_size):
         for c in range(2):
             for k in range(here):
@@ -277,49 +273,86 @@
     def coupling_of(k):
         return (2.0 * layers * layers) * (eta_ref[k] + eta_ref[k + 1])
 
-    def eliminate(k, carry):
-        lower, rest, value = carry
-        coupling = coupling_of(k)
-        new_rest, new_value = [], []
+    middle = layers // 2
+    zero = jnp.zeros(shape, jnp.float32)
+
+    def eliminate(k, coupling, carry):
+        before, passed, value = carry
+        new_passed, new_value = [], []
         for c in range(2):
-            inv = reciprocal(coupling + rest[c])
-            link = coupling * inv
+            rest = side[c, k] + passed[c]
+            pivot = coupling + rest
+            guess = pl.reciprocal(pivot, approx=True)
+            correct = 2.0 - pivot * guess
+            new_passed.append((coupling * rest * guess) * correct)
+            inv = guess * correct
             inverse[c, k] = inv
-            ratio[c, k] = link
-            out = (rhs[c, k] + lower * value[c]) * inv
+            ratio[c, k] = coupling * inv
+            out = (rhs[c, k] + before * value[c]) * inv
             rhs[c, k] = out
             new_value.append(out)
-            new_rest.append(side[c, k + 1] + rest[c] * link)
-        return coupling, tuple(new_rest), tuple(new_value)
-
-    def forward_solve():
-        zero = jnp.zeros(shape, jnp.float32)
-        rest = tuple(side[c, 0] + 2.0 * friction for c in range(2))
-        lower, rest, value = repeat(plan, layers - 1, eliminate, (zero, rest, (zero, zero)))
-        top = []
+        return coupling, tuple(new_passed), tuple(new_value)
+
+    def lower_step(k, carry):
+        return eliminate(k, coupling_of(k), carry)
+
+    def upper_step(k, carry):
+        return eliminate(k, coupling_of(k - 1), carry)
+
+    def fronts(step, carry):
+        lower, upper = carry
+        return lower_step(step, lower), upper_step(layers - 1 - step, upper)
+
+    def spread(first, body):
+        def outward(step, carry):
+            below, above = carry
+            return body(middle - 1 - step, below), body(middle + 1 + step, above)
+
+        below, above = repeat(plan, layers - 1 - middle, outward, (first, first))
+        for k in range(2 * middle - layers, -1, -1):
+            below = body(k, below)
+        return below, above
+
+    def sweep(keep):
+        def stencil_body(k, carry):
+            stencil(k, keep)
+            return carry
+
+        bed = tuple(2.0 * friction for _ in range(2))
+        lower, upper = (zero, bed, (zero, zero)), (zero, (zero, zero), (zero, zero))
+        if plan.unrolled:
+            stencil(0, keep)
+            stencil(layers - 1, keep)
+            for step in range(layers - 1 - middle):
+                stencil(step + 1, keep)
+                if layers - 2 - step > step + 1:
+                    stencil(layers - 2 - step, keep)
+                lower, upper = fronts(step, (lower, upper))
+        else:
+            repeat(plan, layers, stencil_body)
+            lower, upper = repeat(plan, layers - 1 - middle, fronts, (lower, upper))
+        for k in range(layers - 1 - middle, middle):
+            lower = lower_step(k, lower)
+        centre_value = []
         for c in range(2):
-            inv = reciprocal(rest[c])
-            inverse[c, layers - 1] = inv
-            top.append(jnp.where(ice, (rhs[c, layers - 1] + lower * value[c]) * inv, 0.0))
-            field[c, layers - 1] = top[c]
-
-        def back(step, following):
-            k = layers - 2 - step
-            current = tuple(jnp.where(ice, rhs[c, k] + ratio[c, k] * following[c], 0.0) for c in range(2))
+            pivot = side[c, middle] + lower[1][c] + upper[1][c]
+            guess = pl.reciprocal(pivot, approx=True)
+            inv = guess * (2.0 - pivot * guess)
+            inverse[c, middle] = inv
+            total = rhs[c, middle] + (lower[0] * lower[2][c] + upper[0] * upper[2][c])
+            centre_value.append(jnp.where(ice, total * inv, 0.0))
+            field[c, middle] = centre_value[c]
+
+        def solved(k, nearer):
+            current = tuple(jnp.where(ice, rhs[c, k] + ratio[c, k] * nearer[c], 0.0) for c in range(2))
             for c in range(2):
                 field[c, k] = current[c]
             return current
 
-        return top, repeat(plan, layers - 1, back, tuple(top))
-
-    for sweep in range(2):
-
-        def stencil_body(k, carry):
-            stencil(k, sweep == 1)
-            return carry
-
-        repeat(plan, layers, stencil_body)
-        top, base = forward_solve()
+        return spread(tuple(centre_value), solved)
+
+    sweep(False)
+    base, top = sweep(True)
 
     centre = jnp.logical_and(lane % width >= plan.halo, lane % width < plan.halo + plan.cols)
 
@@ -332,8 +365,6 @@
 
     mismatch = [jnp.where(ice, top[c] - observed[c], 0.0) for c in range(2)]
     source = [(2.0 * layers) * mismatch[c] for c in range(2)]
-
-    first_top = tuple(source[c] * inverse[c, layers - 1] for c in range(2))
 
     def side_sum(k, value):
         east, west, north, south = (faces[n, k] for n in range(4))
@@ -341,37 +372,74 @@
         v_east, v_west = x_pair(value[1], 0.0)
         u_north, u_south = y_pair(value[0])
         v_north, v_south = y_pair(value[1])
-        rhs[0, k] = 4.0 * (east * u_east + west * u_west) + (north * u_north + south * u_south)
-        rhs[1, k] = (east * v_east + west * v_west) + 4.0 * (north * v_north + south * v_south)
-
-    side_sum(layers - 1, first_top)
-
-    def first_back(step, following):
+        first = 4.0 * (east * u_east + west * u_west) + (north * u_north + south * u_south)
+        second = (east * v_east + west * v_west) + 4.0 * (north * v_north + south * v_south)
+        return first, second
+
+    carried = tuple(source[c] * inverse[c, layers - 1] for c in range(2))
+    for c in range(2):
+        rhs[c, layers - 1] = carried[c]
+
+    def first_inward(step, carried):
         k = layers - 2 - step
-        current = tuple(ratio[c, k] * following[c] for c in range(2))
-        side_sum(k, current)
-        return current
-
-    repeat(plan, layers - 1, first_back, first_top)
-
-    def second_forward(k, carry):
-        lower, value = carry
-        out = tuple((rhs[c, k] + lower * value[c]) * inverse[c, k] for c in range(2))
+        out = tuple(coupling_of(k) * carried[c] * inverse[c, k] for c in range(2))
         for c in range(2):
             rhs[c, k] = out[c]
-        return coupling_of(k), out
-
-    zero = jnp.zeros(shape, jnp.float32)
-    lower, value = repeat(plan, layers - 1, second_forward, (zero, (zero, zero)))
-    second_top = tuple(
-        (rhs[c, layers - 1] + source[c] + lower * value[c]) * inverse[c, layers - 1] for c in range(2)
+        return out
+
+    carried = repeat(plan, layers - 2 - middle, first_inward, carried)
+    first_middle = tuple(coupling_of(middle) * carried[c] * inverse[c, middle] for c in range(2))
+
+    def first_outward(step, carry):
+        below, above = carry
+        low, high = middle - 1 - step, middle + 1 + step
+        below = tuple(ratio[c, low] * below[c] for c in range(2))
+        above = tuple(rhs[c, high] + ratio[c, high] * above[c] for c in range(2))
+        for k, value in ((low, below), (high, above)):
+            total = side_sum(k, value)
+            for c in range(2):
+                rhs[c, k] = total[c] * inverse[c, k]
+        return below, above
+
+    middle_sum = side_sum(middle, first_middle)
+    below, above = repeat(plan, layers - 1 - middle, first_outward, (first_middle, first_middle))
+    for k in range(2 * middle - layers, -1, -1):
+        below = tuple(ratio[c, k] * below[c] for c in range(2))
+        total = side_sum(k, below)
+        for c in range(2):
+            rhs[c, k] = total[c] * inverse[c, k]
+    for c in range(2):
+        rhs[c, layers - 1] = rhs[c, layers - 1] + source[c] * inverse[c, layers - 1]
+
+    def second_inward(step, carry):
+        below, above = carry
+        low, high = step + 1, layers - 2 - step
+        below = tuple(rhs[c, low] + (coupling_of(low - 1) * inverse[c, low]) * below[c] for c in range(2))
+        above = tuple(rhs[c, high] + (coupling_of(high) * inverse[c, high]) * above[c] for c in range(2))
+        for c in range(2):
+            rhs[c, low] = below[c]
+        return below, above
+
+    below, above = repeat(
+        plan,
+        layers - 2 - middle,
+        second_inward,
+        (tuple(rhs[c, 0] for c in range(2)), tuple(rhs[c, layers - 1] for c in range(2))),
     )
-
-    def second_back(step, following):
-        k = layers - 2 - step
-        return tuple(rhs[c, k] + ratio[c, k] * following[c] for c in range(2))
-
-    adjoint = repeat(plan, layers - 1, second_back, second_top)
+    for k in range(layers - 1 - middle, middle):
+        below = tuple(rhs[c, k] + (coupling_of(k - 1) * inverse[c, k]) * below[c] for c in range(2))
+        for c in range(2):
+            rhs[c, k] = below[c]
+    adjoint = tuple(
+        (middle_sum[c] + (coupling_of(middle - 1) * below[c] + coupling_of(middle) * above[c])) * inverse[c, middle]
+        for c in range(2)
+    )
+
+    def second_outward(step, nearer):
+        k = middle - 1 - step
+        return tuple(rhs[c, k] + ratio[c, k] * nearer[c] for c in range(2))
+
+    adjoint = repeat(plan, middle, second_outward, adjoint)
     adjoint = [jnp.where(ice, adjoint[c], 0.0) for c in range(2)]
     gradient = -friction * (base[0] * adjoint[0] + base[1] * adjoint[1])
 
@@ -398,7 +466,7 @@
     local_chunks = plan.local_cols // LANES
 
     total = jnp.sum(
-        in_ref[pl.ds(here, plan.devices, stride=plan.out_rows), :].astype(jnp.float32), axis=0, keepdims=True
+        in_ref[pl.ds(here, plan.devices, stride=plan.out_rows), :], axis=0, keepdims=True
     )
     line_lane = lax.broadcasted_iota(jnp.int32, (1, LANES), 1)
 
@@ -412,9 +480,7 @@
     scale = step_size / jnp.sqrt(grad_sum / plan.column_count + 1e-06)
 
     lane = lax.broadcasted_iota(jnp.int32, (plan.out_rows, LANES), 1)
-    starts = [(r, c, r * width + plan.halo + c * cols) for r in range(rows) for c in range(2)]
-
-    def chunk(i, carry):
+    def chunk(c, i):
         at = i * plan.per_chunk * plan.out_rows
         if not isinstance(at, int):
             at = pl.multiple_of(at, 8)
@@ -422,28 +488,33 @@
             lane_roll(in_ref[pl.ds(at + t * plan.out_rows, plan.out_rows), :], t * cols)
             for t in range(plan.per_chunk)
         ]
-        for r, c, start in starts:
+        for r in range(rows):
+            start = r * width + plan.halo + c * cols
             ahead = (lane + (LANES - start % LANES)) % LANES
             row = turned[0]
             for t in range(1, plan.per_chunk):
                 row = jnp.where(ahead >= t * cols, turned[t], row)
             row = lane_roll(row, -start)
-            vel_ref[pl.ds(c * here * plan.chunks * rows + i * rows + r, here, stride=plan.chunks * rows), :] = row[:here]
+            vel_ref[c, pl.ds(i * rows + r, here, stride=plan.chunks * rows), :] = row[:here]
             if c == 0:
                 owner, step = i // local_chunks, i % local_chunks
                 grad_ref[owner, pl.ds(step * rows + r, 1), :] = row[here : here + 1]
-        return carry
-
-    repeat(plan, plan.chunks, chunk)
-    out = [
-        pltpu.make_async_copy(vel_ref, vel_hbm, leave.at[0]),
-        pltpu.make_async_copy(friction_ref, friction_hbm, leave.at[1]),
-        pltpu.make_async_copy(misfit_ref, misfit_hbm, leave.at[2]),
-    ]
-    out[0].start()
-    friction_ref[...] = log_ref[...] - grad_ref[lax.axis_index("layer")] * scale
-    out[1].start()
-    out[2].start()
+
+    out = [pltpu.make_async_copy(vel_ref.at[c], vel_hbm.at[c], leave.at[c]) for c in range(2)]
+    out.append(pltpu.make_async_copy(friction_ref, friction_hbm, leave.at[2]))
+    out.append(pltpu.make_async_copy(misfit_ref, misfit_hbm, leave.at[3]))
+    out[3].start()
+    for c in range(2):
+
+        def chunk_body(i, carry):
+            chunk(c, i)
+            return carry
+
+        repeat(plan, plan.chunks, chunk_body)
+        out[c].start()
+        if c == 0:
+            friction_ref[...] = log_ref[...] - grad_ref[lax.axis_index("layer")] * scale
+            out[2].start()
     for copy in out:
         copy.wait()
 
@@ -506,7 +577,7 @@
 
     back = exchange(solved, 1)
 
-    vel_lines, log_lines = inputs[0], inputs[3]
+    vel_lines, log_lines = inputs[0].reshape(2, -1, LANES), inputs[3]
     velocity, friction_new, misfit = pl.pallas_call(
         functools.partial(unpack_kernel, plan),
         out_shape=(
@@ -521,7 +592,7 @@
             pltpu.VMEM(log_lines.shape, f32),
             pltpu.VMEM((1, 1), f32),
             pltpu.VMEM((plan.layer_size,) + log_lines.shape, f32),
-            pltpu.SemaphoreType.DMA((3,)),
+            pltpu.SemaphoreType.DMA((4,)),
         ],
         compiler_params=limit,
         name="unpack",

time: 29.8 us -> 29.6 us (level)
  no operation moved by 1% of the time
where the time goes in v6:
time: 29.6 us; the launch traced here: 29.3 us
  blocking collectives  25.5 us (86%)
  Pallas kernels  3.21 us (11%)
  between operations  0.64 us (2%)
    all_to_all x2, blocking collectives, exchange(): lax.all_to_all(shaped, ('map', 'layer'), split_axis=0, concat_axis=0, til...  25.5 us
    pallas_call x1, Pallas kernels, on_device(): pl.pallas_call(functools.partial(pack_kernel, plan), out_shape=jax.ShapeD...  1.24 us
    pallas_call x1, Pallas kernels, on_device(): pl.pallas_call(functools.partial(solve_kernel, plan), out_shape=jax.Shape...  1.1 us
    pallas_call x1, Pallas kernels, on_device(): pl.pallas_call(functools.partial(unpack_kernel, plan), out_shape=(jax.Sha...  0.86 us

profile of v6, /device:TPU:0, one launch (start us, length us, event | category | flops | bytes accessed | tf_op | source)
XLA Modules:
  0.0 29.3 jit_solution(4513211751598002995)
XLA Ops:
  0.6 1.2 %pack.1 = f32[320,128]{1,0:T(8,128)S(1)} custom-call(f32[128,128]{1,0:T(8,128)} %bitcast.48, f32[8,128]{1,0:T(8,128)} %bitcast.49, f32[8,128]{1,0:T(8,128)} %bitcast.50, f32[4,128]{1,0:T(4,128)} %bitcast.46, s32[4,128]{1,0:T(4,128)} %bitcast.51), custom_call_target="tpu_custom_call" | custom-call | tf_op jit(solution)/shard_map/pack/pallas_call | solution.py:544
  1.9 15.9 %all_to_all.10 = f32[160,2,128]{2,1,0:T(2,128)S(1)} all-to-all(f32[160,2,128]{2,1,0:T(2,128)S(1)} %bitcast.43), channel_id=1, replica_groups=mesh['map'=8,'layer'=4] {'map','layer'}, dimensions={0} | all-to-all | bytes 327680 | tf_op jit(solution)/shard_map/all_to_all | solution.py:542
  17.8 1.1 %solve.1 = f32[160,128]{1,0:T(8,128)S(1)} custom-call(f32[320,128]{1,0:T(8,128)S(1)} %bitcast.42), custom_call_target="tpu_custom_call" | custom-call | tf_op jit(solution)/shard_map/solve/pallas_call | solution.py:560
  18.9 0.0 copy-start
  18.9 9.5 %all_to_all.11 = f32[160,1,128]{2,1,0:T(1,128)S(1)} all-to-all(f32[160,1,128]{2,1,0:T(1,128)S(1)} %bitcast.45), channel_id=1, replica_groups=mesh['map'=8,'layer'=4] {'map','layer'}, dimensions={0} | all-to-all | bytes 163840 | tf_op jit(solution)/shard_map/all_to_all | solution.py:542
  28.5 0.0 copy-done
  28.5 0.9 %unpack.1 = (f32[2,64,128]{2,1,0:T(8,128)}, f32[4,128]{1,0:T(4,128)}, f32[1,1]{1,0:T(1,128)}) custom-call(f32[160,128]{1,0:T(8,128)S(1)} %bitcast.44, f32[4,128]{1,0:T(4,128)S(1)} %bitcast.47), custom_call_target="tpu_custom_call" | custom-call | tf_op jit(solution)/shard_map/unpack/pallas_call | solution.py:581
Async XLA Ops:
  18.9 9.6 %copy-start = (f32[2,256]{1,0:T(2,128)S(1)}, f32[2,256]{1,0:T(2,128)}, u32[]{:S(2)}) copy-start(f32[2,256]{1,0:T(2,128)} %param.8) | copy-start | bytes 6148

commit v7 on v6

--- a/solution.py
+++ b/solution.py
@@ -13,6 +13,7 @@
 LANES = 128
 REACH = 5
 MIB = 1 << 20
+VELOCITY_COPIES = 4
 
 
 class Plan:
@@ -63,13 +64,14 @@
     vel_ref, driving_ref, observed_ref, log_ref, mask_ref, arrival,
 ):
     width, rows, wide, half = plan.width, plan.rows, plan.wide, plan.half
-    pairs = (
-        (vel_hbm, vel_ref),
+    piece = vel_ref.shape[0] // VELOCITY_COPIES
+    spans = [pl.ds(n * piece, piece) for n in range(VELOCITY_COPIES)]
+    pairs = [(vel_hbm.at[span, :], vel_ref.at[span, :]) for span in spans] + [
         (driving_hbm, driving_ref),
         (observed_hbm, observed_ref),
         (log_hbm, log_ref),
         (mask_hbm, mask_ref),
-    )
+    ]
     copies = [pltpu.make_async_copy(pair[0], pair[1], arrival.at[n]) for n, pair in enumerate(pairs)]
     for copy in copies:
         copy.start()
@@ -87,7 +89,8 @@
             value = jnp.where(lax.broadcasted_iota(jnp.int32, value.shape, 1) >= offset, value, after)
         return lane_roll(value, place - offset)
 
-    copies[0].wait()
+    for copy in copies[:VELOCITY_COPIES]:
+        copy.wait()
 
     def chunk_windows(i, carry):
         def velocity(r):
@@ -117,7 +120,7 @@
         return carry
 
     repeat(plan, plan.chunks, chunk_windows)
-    for copy in copies[1:]:
+    for copy in copies[VELOCITY_COPIES:]:
         copy.wait()
 
     place = lax.axis_index("layer")
@@ -476,7 +479,6 @@
 
     misfit_sum = summed(plan.halo + cols)
     grad_sum = summed(plan.halo + cols + width)
-    misfit_ref[...] = 0.5 * misfit_sum / plan.column_count
     scale = step_size / jnp.sqrt(grad_sum / plan.column_count + 1e-06)
 
     lane = lax.broadcasted_iota(jnp.int32, (plan.out_rows, LANES), 1)
@@ -503,7 +505,6 @@
     out = [pltpu.make_async_copy(vel_ref.at[c], vel_hbm.at[c], leave.at[c]) for c in range(2)]
     out.append(pltpu.make_async_copy(friction_ref, friction_hbm, leave.at[2]))
     out.append(pltpu.make_async_copy(misfit_ref, misfit_hbm, leave.at[3]))
-    out[3].start()
     for c in range(2):
 
         def chunk_body(i, carry):
@@ -512,9 +513,10 @@
 
         repeat(plan, plan.chunks, chunk_body)
         out[c].start()
-        if c == 0:
-            friction_ref[...] = log_ref[...] - grad_ref[lax.axis_index("layer")] * scale
-            out[2].start()
+    friction_ref[...] = log_ref[...] - grad_ref[lax.axis_index("layer")] * scale
+    out[2].start()
+    misfit_ref[...] = 0.5 * misfit_sum / plan.column_count
+    out[3].start()
     for copy in out:
         copy.wait()
 
@@ -548,7 +550,7 @@
         out_specs=vmem,
         scratch_shapes=[pltpu.VMEM(x.shape, x.dtype) for x in inputs]
         + [
-            pltpu.SemaphoreType.DMA((5,)),
+            pltpu.SemaphoreType.DMA((VELOCITY_COPIES + 4,)),
         ],
         compiler_params=limit,
         name="pack",

time: 29.6 us -> 29.6 us (level)
  no operation moved by 1% of the time
where the time goes in v7:
time: 29.6 us; the launch traced here: 29.3 us
  blocking collectives  25.5 us (86%)
  Pallas kernels  3.16 us (11%)
  between operations  0.64 us (2%)
    all_to_all x2, blocking collectives, exchange(): lax.all_to_all(shaped, ('map', 'layer'), split_axis=0, concat_axis=0, til...  25.5 us
    pallas_call x1, Pallas kernels, on_device(): pl.pallas_call(functools.partial(pack_kernel, plan), out_shape=jax.ShapeD...  1.19 us
    pallas_call x1, Pallas kernels, on_device(): pl.pallas_call(functools.partial(solve_kernel, plan), out_shape=jax.Shape...  1.1 us
    pallas_call x1, Pallas kernels, on_device(): pl.pallas_call(functools.partial(unpack_kernel, plan), out_shape=(jax.Sha...  0.86 us

profile of v7, /device:TPU:0, one launch (start us, length us, event | category | flops | bytes accessed | tf_op | source)
XLA Modules:
  0.0 29.3 jit_solution(5967688783196999997)
XLA Ops:
  0.6 1.2 %pack.1 = f32[320,128]{1,0:T(8,128)S(1)} custom-call(f32[128,128]{1,0:T(8,128)} %bitcast.48, f32[8,128]{1,0:T(8,128)} %bitcast.49, f32[8,128]{1,0:T(8,128)} %bitcast.50, f32[4,128]{1,0:T(4,128)} %bitcast.46, s32[4,128]{1,0:T(4,128)} %bitcast.51), custom_call_target="tpu_custom_call" | custom-call | tf_op jit(solution)/shard_map/pack/pallas_call | solution.py:546
  1.8 15.9 %all_to_all.10 = f32[160,2,128]{2,1,0:T(2,128)S(1)} all-to-all(f32[160,2,128]{2,1,0:T(2,128)S(1)} %bitcast.43), channel_id=1, replica_groups=mesh['map'=8,'layer'=4] {'map','layer'}, dimensions={0} | all-to-all | bytes 327680 | tf_op jit(solution)/shard_map/all_to_all | solution.py:544
  17.8 1.1 %solve.1 = f32[160,128]{1,0:T(8,128)S(1)} custom-call(f32[320,128]{1,0:T(8,128)S(1)} %bitcast.42), custom_call_target="tpu_custom_call" | custom-call | tf_op jit(solution)/shard_map/solve/pallas_call | solution.py:562
  18.9 0.0 copy-start
  18.9 9.5 %all_to_all.11 = f32[160,1,128]{2,1,0:T(1,128)S(1)} all-to-all(f32[160,1,128]{2,1,0:T(1,128)S(1)} %bitcast.45), channel_id=1, replica_groups=mesh['map'=8,'layer'=4] {'map','layer'}, dimensions={0} | all-to-all | bytes 163840 | tf_op jit(solution)/shard_map/all_to_all | solution.py:544
  28.4 0.0 copy-done
  28.4 0.9 %unpack.1 = (f32[2,64,128]{2,1,0:T(8,128)}, f32[4,128]{1,0:T(4,128)}, f32[1,1]{1,0:T(1,128)}) custom-call(f32[160,128]{1,0:T(8,128)S(1)} %bitcast.44, f32[4,128]{1,0:T(4,128)S(1)} %bitcast.47), custom_call_target="tpu_custom_call" | custom-call | tf_op jit(solution)/shard_map/unpack/pallas_call | solution.py:583
Async XLA Ops:
  18.9 9.6 %copy-start = (f32[2,256]{1,0:T(2,128)S(1)}, f32[2,256]{1,0:T(2,128)}, u32[]{:S(2)}) copy-start(f32[2,256]{1,0:T(2,128)} %param.8) | copy-start | bytes 6148

commit v8 on v7

--- a/solution.py
+++ b/solution.py
@@ -444,7 +444,8 @@
 
     adjoint = repeat(plan, middle, second_outward, adjoint)
     adjoint = [jnp.where(ice, adjoint[c], 0.0) for c in range(2)]
-    gradient = -friction * (base[0] * adjoint[0] + base[1] * adjoint[1])
+    product = base[0] * adjoint[0] + base[1] * adjoint[1]
+    gradient = -friction * product
 
     def partial_sum(value):
         line = jnp.sum(jnp.where(centre, value, 0.0), axis=0, keepdims=True)
@@ -456,13 +457,13 @@
     misfit_line = partial_sum(mismatch[0] * mismatch[0] + mismatch[1] * mismatch[1])
     grad_line = partial_sum(gradient * gradient)
     in_first = jnp.logical_and(lane >= plan.halo + plan.cols, lane < plan.halo + 2 * plan.cols)
-    last_row = jnp.where(centre, gradient, jnp.where(in_first, misfit_line, grad_line))
+    last_row = jnp.where(centre, product, jnp.where(in_first, misfit_line, grad_line))
     for part in range(plan.layer_size):
         out_ref[pl.ds(part * plan.out_rows + here, size, stride=plan.layer_size * plan.out_rows), :] = last_row
 
 
 def unpack_kernel(
-    plan, in_ref, log_ref, vel_hbm, friction_hbm, misfit_hbm,
+    plan, in_ref, log_ref, bed_ref, vel_hbm, friction_hbm, misfit_hbm,
     vel_ref, friction_ref, misfit_ref, grad_ref, leave,
 ):
     here, width, cols, rows = plan.layers_here, plan.width, plan.cols, plan.rows
@@ -513,7 +514,8 @@
 
         repeat(plan, plan.chunks, chunk_body)
         out[c].start()
-    friction_ref[...] = log_ref[...] - grad_ref[lax.axis_index("layer")] * scale
+    gradient = -bed_ref[...] * grad_ref[lax.axis_index("layer")]
+    friction_ref[...] = log_ref[...] - gradient * scale
     out[2].start()
     misfit_ref[...] = 0.5 * misfit_sum / plan.column_count
     out[3].start()
@@ -557,6 +559,7 @@
     )(*(pltpu.with_memory_space_constraint(x, pltpu.HBM) for x in inputs))
 
     windows = exchange(packed, 2)
+    bed_lines = jnp.where(inputs[4] == 1, jnp.exp(inputs[3]), 0.0)
 
     plane = (plan.layers, plan.map_size, LANES)
     solved = pl.pallas_call(
@@ -587,7 +590,7 @@
             jax.ShapeDtypeStruct(log_lines.shape, f32),
             jax.ShapeDtypeStruct((1, 1), f32),
         ),
-        in_specs=[vmem] * 2,
+        in_specs=[vmem] * 3,
         out_specs=(hbm, hbm, hbm),
         scratch_shapes=[
             pltpu.VMEM(vel_lines.shape, f32),
@@ -598,7 +601,7 @@
         ],
         compiler_params=limit,
         name="unpack",
-    )(back, log_lines)
+    )(back, log_lines, bed_lines)
     return (
         from_lines(velocity, velocity_init.shape),
         from_lines(friction_new, log_friction.shape),

time: 29.6 us -> 31.1 us (1.051)
  blocking collectives: 25.5 us -> 15.9 us
  waiting for transfers between devices: 0 us -> 7.68 us
  starting transfers between devices: 0 us -> 2.7 us
  Pallas kernels: 3.16 us -> 3.79 us
    all_to_all x2 -> x1, blocking collectives: 25.5 us -> 15.9 us  [exchange(): lax.all_to_all(shaped, ('map', 'layer'), split_axis=0, concat_axis=0, til...]
    all_to_all x0 -> x1, waiting for transfers between devices: none -> 7.68 us  [exchange(): lax.all_to_all(shaped, ('map', 'layer'), split_axis=0, concat_axis=0, til...]
    all_to_all x0 -> x1, starting transfers between devices: none -> 2.7 us  [exchange(): lax.all_to_all(shaped, ('map', 'layer'), split_axis=0, concat_axis=0, til...]
    pallas_call x1, Pallas kernels: 1.1 us -> 1.73 us  [on_device(): pl.pallas_call(functools.partial(solve_kernel, plan), out_shape=jax.Shape...]
  transfers between devices with their start and end apart: 0 -> 1, of which waited for: 0 -> 1; matrix products, arithmetic and copies ran while one was open for 0% -> 0% of each run, Pallas kernels for 0% -> 0%
where the time goes in v8:
time: 31.1 us; the launch traced here: 30.8 us
  blocking collectives  15.9 us (51%)
  waiting for transfers between devices  7.68 us (25%)
  Pallas kernels  3.79 us (12%)
  starting transfers between devices  2.7 us (9%)
  between operations  0.67 us (2%)
    all_to_all x1, blocking collectives, exchange(): lax.all_to_all(shaped, ('map', 'layer'), split_axis=0, concat_axis=0, til...  15.9 us
    all_to_all x1, waiting for transfers between devices, exchange(): lax.all_to_all(shaped, ('map', 'layer'), split_axis=0, concat_axis=0, til...  7.68 us
    all_to_all x1, starting transfers between devices, exchange(): lax.all_to_all(shaped, ('map', 'layer'), split_axis=0, concat_axis=0, til...  2.7 us
    pallas_call x1, Pallas kernels, on_device(): pl.pallas_call(functools.partial(solve_kernel, plan), out_shape=jax.Shape...  1.73 us
    pallas_call x1, Pallas kernels, on_device(): pl.pallas_call(functools.partial(pack_kernel, plan), out_shape=jax.ShapeD...  1.19 us
    pallas_call x1, Pallas kernels, on_device(): pl.pallas_call(functools.partial(unpack_kernel, plan), out_shape=(jax.Sha...  0.86 us
  transfers between devices with their start and end apart: 1, of which 1 were waited for; matrix products, arithmetic and copies ran while one was open for 0% of the time, Pallas kernels for 0%

profile of v8, /device:TPU:0, one launch (start us, length us, event | category | flops | bytes accessed | tf_op | source)
XLA Modules:
  0.0 30.8 jit_solution(4377940700991385612)
XLA Ops:
  0.6 1.2 %pack.1 = f32[320,128]{1,0:T(8,128)S(1)} custom-call(f32[128,128]{1,0:T(8,128)} %bitcast.48, f32[8,128]{1,0:T(8,128)} %bitcast.51, f32[8,128]{1,0:T(8,128)} %bitcast.52, f32[4,128]{1,0:T(4,128)} %bitcast.45, s32[4,128]{1,0:T(4,128)} %bitcast.49), custom_call_target="tpu_custom_call" | custom-call | tf_op jit(solution)/shard_map/pack/pallas_call | solution.py:548
  1.8 15.9 %all_to_all.10 = f32[160,2,128]{2,1,0:T(2,128)S(1)} all-to-all(f32[160,2,128]{2,1,0:T(2,128)S(1)} %bitcast.43), channel_id=1, replica_groups=mesh['map'=8,'layer'=4] {'map','layer'}, dimensions={0} | all-to-all | bytes 327680 | tf_op jit(solution)/shard_map/all_to_all | solution.py:546
  17.8 1.7 %solve.1 = f32[160,128]{1,0:T(8,128)} custom-call(f32[320,128]{1,0:T(8,128)S(1)} %bitcast.42), custom_call_target="tpu_custom_call" | custom-call | tf_op jit(solution)/shard_map/solve/pallas_call | solution.py:565
  19.5 0.0 copy-start
  19.5 0.0 copy-start.1
  19.5 2.7 %all-to-all-start.1 = ((f32[160,1,128]{2,1,0:T(1,128)}), f32[160,1,128]{2,1,0:T(1,128)S(1)}, u32[]{:S(2)}, u32[]{:S(2)}) async-start(f32[160,1,128]{2,1,0:T(1,128)} %bitcast.18), calls=%async_computation.1 | async-start | bytes 163840 | tf_op jit(solution)/shard_map/all_to_all | solution.py:546
  22.2 0.0 copy-done
  22.2 0.0 copy-done.1
  22.3 7.7 %all-to-all-done.1 = f32[160,1,128]{2,1,0:T(1,128)S(1)} async-done(((f32[160,1,128]{2,1,0:T(1,128)}), f32[160,1,128]{2,1,0:T(1,128)S(1)}, u32[]{:S(2)}, u32[]{:S(2)}) %all-to-all-start.1) | async-done | bytes 81952 | tf_op jit(solution)/shard_map/all_to_all | solution.py:546
  29.9 0.9 %unpack.1 = (f32[2,64,128]{2,1,0:T(8,128)}, f32[4,128]{1,0:T(4,128)}, f32[1,1]{1,0:T(1,128)}) custom-call(f32[160,128]{1,0:T(8,128)S(1)} %bitcast.44, f32[4,128]{1,0:T(4,128)S(1)} %bitcast.47, f32[4,128]{1,0:T(4,128)S(1)} %exponential_select_fusion.bed_ref), custom_call_target="tpu_custom_call" | custom-call | tf_op jit(solution)/shard_map/unpack/pallas_call | solution.py:586
  (1 shorter events, 0.0 us)
Async XLA Ops:
  19.5 2.7 %copy-start = (f32[2,256]{1,0:T(2,128)S(1)}, f32[2,256]{1,0:T(2,128)}, u32[]{:S(2)}) copy-start(f32[2,256]{1,0:T(2,128)} %param.8) | copy-start | bytes 6148
  19.5 2.7 %copy-start.1 = (s32[2,256]{1,0:T(2,128)S(1)}, s32[2,256]{1,0:T(2,128)}, u32[]{:S(2)}) copy-start(s32[2,256]{1,0:T(2,128)} %param.9) | copy-start | bytes 6148
  19.5 10.4 %all-to-all-start.1 = ((f32[160,1,128]{2,1,0:T(1,128)}), f32[160,1,128]{2,1,0:T(1,128)S(1)}, u32[]{:S(2)}, u32[]{:S(2)}) async-start(f32[160,1,128]{2,1,0:T(1,128)} %bitcast.18), calls=%async_computation.1 | async-start | bytes 163840 | tf_op jit(solution)/shard_map/all_to_all | solution.py:546

commit v9 on v7

--- a/solution.py
+++ b/solution.py
@@ -200,7 +200,7 @@
     x_start = jnp.logical_and(first_group, sub == 0)
 
     def arrived(part, row):
-        return in_ref[pl.ds(part * plan.in_rows + row, size, stride=plan.layer_size * plan.in_rows), :]
+        return in_ref[pl.ds(part * size * plan.in_rows + row, size, stride=plan.in_rows), :]
 
     def over_parts(row):
         total = arrived(0, row)
@@ -361,7 +361,7 @@
 
     def send(k, carry):
         both = jnp.where(centre, field[0, k], lane_roll(field[1, k], plan.cols))
-        out_ref[pl.ds((k // here) * plan.out_rows + k % here, size, stride=plan.layer_size * plan.out_rows), :] = both
+        out_ref[pl.ds((k // here) * size * plan.out_rows + k % here, size, stride=plan.out_rows), :] = both
         return carry
 
     repeat(plan, layers, send)
@@ -458,7 +458,7 @@
     in_first = jnp.logical_and(lane >= plan.halo + plan.cols, lane < plan.halo + 2 * plan.cols)
     last_row = jnp.where(centre, gradient, jnp.where(in_first, misfit_line, grad_line))
     for part in range(plan.layer_size):
-        out_ref[pl.ds(part * plan.out_rows + here, size, stride=plan.layer_size * plan.out_rows), :] = last_row
+        out_ref[pl.ds(part * size * plan.out_rows + here, size, stride=plan.out_rows), :] = last_row
 
 
 def unpack_kernel(
@@ -541,7 +541,7 @@
 
     def exchange(blocks, unit):
         shaped = blocks.reshape(blocks.shape[0] // unit, unit, LANES)
-        return lax.all_to_all(shaped, ("map", "layer"), split_axis=0, concat_axis=0, tiled=True).reshape(blocks.shape)
+        return lax.all_to_all(shaped, ("layer", "map"), split_axis=0, concat_axis=0, tiled=True).reshape(blocks.shape)
 
     packed = pl.pallas_call(
         functools.partial(pack_kernel, plan),

time: 29.6 us -> 29.3 us (0.990)
  blocking collectives: 25.5 us -> 25.2 us
where the time goes in v9:
time: 29.3 us; the launch traced here: 29 us
  blocking collectives  25.2 us (86%)
  Pallas kernels  3.16 us (11%)
  between operations  0.64 us (2%)
    all_to_all x2, blocking collectives, exchange(): lax.all_to_all(shaped, ('layer', 'map'), split_axis=0, concat_axis=0, til...  25.2 us
    pallas_call x1, Pallas kernels, on_device(): pl.pallas_call(functools.partial(pack_kernel, plan), out_shape=jax.ShapeD...  1.19 us
    pallas_call x1, Pallas kernels, on_device(): pl.pallas_call(functools.partial(solve_kernel, plan), out_shape=jax.Shape...  1.1 us
    pallas_call x1, Pallas kernels, on_device(): pl.pallas_call(functools.partial(unpack_kernel, plan), out_shape=(jax.Sha...  0.86 us

profile of v9, /device:TPU:0, one launch (start us, length us, event | category | flops | bytes accessed | tf_op | source)
XLA Modules:
  0.0 29.0 jit_solution(4719695508409744484)
XLA Ops:
  0.6 1.2 %pack.1 = f32[320,128]{1,0:T(8,128)S(1)} custom-call(f32[128,128]{1,0:T(8,128)} %bitcast.48, f32[8,128]{1,0:T(8,128)} %bitcast.49, f32[8,128]{1,0:T(8,128)} %bitcast.50, f32[4,128]{1,0:T(4,128)} %bitcast.46, s32[4,128]{1,0:T(4,128)} %bitcast.51), custom_call_target="tpu_custom_call" | custom-call | tf_op jit(solution)/shard_map/pack/pallas_call | solution.py:546
  1.8 15.5 %all_to_all.10 = f32[160,2,128]{2,1,0:T(2,128)S(1)} all-to-all(f32[160,2,128]{2,1,0:T(2,128)S(1)} %bitcast.43), channel_id=1, replica_groups=mesh['map'=8,'layer'=4] {'layer','map'}, dimensions={0} | all-to-all | bytes 327680 | tf_op jit(solution)/shard_map/all_to_all | solution.py:544
  17.4 1.1 %solve.1 = f32[160,128]{1,0:T(8,128)S(1)} custom-call(f32[320,128]{1,0:T(8,128)S(1)} %bitcast.42), custom_call_target="tpu_custom_call" | custom-call | tf_op jit(solution)/shard_map/solve/pallas_call | solution.py:562
  18.5 0.0 copy-start
  18.5 9.7 %all_to_all.11 = f32[160,1,128]{2,1,0:T(1,128)S(1)} all-to-all(f32[160,1,128]{2,1,0:T(1,128)S(1)} %bitcast.45), channel_id=1, replica_groups=mesh['map'=8,'layer'=4] {'layer','map'}, dimensions={0} | all-to-all | bytes 163840 | tf_op jit(solution)/shard_map/all_to_all | solution.py:544
  28.2 0.0 copy-done
  28.2 0.9 %unpack.1 = (f32[2,64,128]{2,1,0:T(8,128)}, f32[4,128]{1,0:T(4,128)}, f32[1,1]{1,0:T(1,128)}) custom-call(f32[160,128]{1,0:T(8,128)S(1)} %bitcast.44, f32[4,128]{1,0:T(4,128)S(1)} %bitcast.47), custom_call_target="tpu_custom_call" | custom-call | tf_op jit(solution)/shard_map/unpack/pallas_call | solution.py:583
Async XLA Ops:
  18.5 9.7 %copy-start = (f32[2,256]{1,0:T(2,128)S(1)}, f32[2,256]{1,0:T(2,128)}, u32[]{:S(2)}) copy-start(f32[2,256]{1,0:T(2,128)} %param.8) | copy-start | bytes 6148

commit v10 on v9

--- a/solution.py
+++ b/solution.py
@@ -12,6 +12,7 @@
 step_size = 0.5
 LANES = 128
 REACH = 5
+BED_REACH = 3
 MIB = 1 << 20
 VELOCITY_COPIES = 4
 
@@ -37,13 +38,15 @@
         self.chunks = self.ny // LANES
         self.column_count = self.rows * self.map_size * self.ny
         self.vel_rows = 2 * self.layers_here
-        self.in_rows = self.vel_rows + self.rows
+        self.in_rows = self.vel_rows + 1
+        self.left_at = self.gap
+        self.right_at = self.gap + self.cols // 2 + 1
         self.out_rows = self.layers_here + 1
         self.unrolled = self.map_size <= 8
         assert self.width * self.rows == LANES and self.cols * self.per_chunk == LANES
         assert self.low >= 0 and self.wide % 2 == 0 and self.width - self.wide >= self.half
         assert 2 * self.cols <= self.width and self.local_cols % LANES == 0
-        assert self.vel_rows == 8 and self.rows == 2 and 3 * self.wide <= LANES
+        assert self.vel_rows == 8 and self.rows == 2 and 4 * self.cols <= LANES
 
 
 def repeat(plan, count, body, carry=0):
@@ -63,7 +66,7 @@
     plan, vel_hbm, driving_hbm, observed_hbm, log_hbm, mask_hbm, out_ref,
     vel_ref, driving_ref, observed_ref, log_ref, mask_ref, arrival,
 ):
-    width, rows, wide, half = plan.width, plan.rows, plan.wide, plan.half
+    width, rows, cols, half = plan.width, plan.rows, plan.cols, plan.half
     piece = vel_ref.shape[0] // VELOCITY_COPIES
     spans = [pl.ds(n * piece, piece) for n in range(VELOCITY_COPIES)]
     pairs = [(vel_hbm.at[span, :], vel_ref.at[span, :]) for span in spans] + [
@@ -79,7 +82,7 @@
     lane = lax.broadcasted_iota(jnp.int32, shape, 1)
     sub = lax.broadcasted_iota(jnp.int32, shape, 0)
     in_gap = jnp.logical_not(jnp.logical_and(lane % width >= plan.low, lane % width < plan.gap))
-    no_line = jnp.zeros((rows, LANES), jnp.float32)
+    no_line = jnp.zeros((1, LANES), jnp.float32)
 
     def slide(part, start, length, place):
         step, offset = start // LANES, start % LANES
@@ -116,7 +119,7 @@
                 at = pl.multiple_of(at, 8)
             at = at + t * plan.in_rows
             out_ref[pl.ds(at, plan.vel_rows), :] = jnp.where(in_gap, 0.0, block)
-            out_ref[pl.ds(at + plan.vel_rows, rows), :] = no_line
+            out_ref[pl.ds(at + plan.vel_rows, 1), :] = no_line
         return carry
 
     repeat(plan, plan.chunks, chunk_windows)
@@ -126,53 +129,67 @@
     place = lax.axis_index("layer")
     local_chunks = plan.local_cols // LANES
 
-    def line_part(ref, row):
-        def part(step):
-            if not 0 <= step < local_chunks:
-                return no_line
-            return ref[row + step * rows : row + (step + 1) * rows, :]
-
-        return part
-
-    def gap_part(r):
-        def part(step):
-            if not 0 <= step < local_chunks:
-                return jnp.zeros(shape, jnp.float32)
-            at = step * rows + r
-            skip = local_chunks * rows
-            first = jnp.broadcast_to(observed_ref[at : at + 1, :], shape)
-            second = jnp.broadcast_to(observed_ref[skip + at : skip + at + 1, :], shape)
-            third = jnp.broadcast_to(mask_ref[at : at + 1, :], shape).astype(jnp.float32)
-            return jnp.where(sub < 2, first, jnp.where(sub < 4, second, third))
-
-        return part
-
-    gap_parts = [[gap_part(r)(step) for step in range(-1, local_chunks + 1)] for r in range(rows)]
-    own = plan.local_cols // plan.cols
-    spill = -(-REACH // plan.cols)
+    skip = local_chunks * rows
+    no_block = jnp.zeros(shape, jnp.float32)
+
+    def whole(ref, row):
+        return jnp.broadcast_to(ref[row : row + 1, :], shape).astype(jnp.float32)
+
+    def gap_part(r, step):
+        at = step * rows + r
+        observed = jnp.where(sub < 2, whole(observed_ref, at), whole(observed_ref, skip + at))
+        return jnp.where(sub < 4, observed, jnp.where(sub < 6, whole(mask_ref, at), whole(log_ref, at)))
+
+    def driving_part(r, step):
+        at = step * rows + r
+        return jnp.where(sub < 2, whole(driving_ref, at), whole(driving_ref, skip + at))
+
+    def sequence(make):
+        return [
+            [no_block] + [make(r, step) for step in range(local_chunks)] + [no_block] for r in range(rows)
+        ]
+
+    gap_parts, driving_parts = sequence(gap_part), sequence(driving_part)
+    own = plan.local_cols // cols
+    spill = -(-REACH // cols)
 
     def column_block(q):
-        start = q * plan.cols - REACH
-        line = None
-        for n, part in enumerate(
-            (line_part(driving_ref, 0), line_part(driving_ref, local_chunks * rows), line_part(log_ref, 0))
-        ):
-            value = slide(part, start, wide, n * wide)
-            lanes = lax.broadcasted_iota(jnp.int32, value.shape, 1)
-            line = value if line is None else jnp.where(lanes >= n * wide, value, line)
+        start = q * cols
         block = None
         for r in range(rows):
-            halves = [
-                slide(lambda step: gap_parts[r][step + 1], start + h * half, half, (r * width + plan.gap) % LANES)
-                for h in range(2)
-            ]
-            value = jnp.where(sub % 2 == 0, halves[0], halves[1])
+
+            def in_gaps(step):
+                return gap_parts[r][step + 1]
+
+            def of_driving(step):
+                return driving_parts[r][step + 1]
+
+            at = r * width
+            first = slide(in_gaps, start - REACH, half, (at + plan.gap) % LANES)
+            second = slide(in_gaps, start - REACH + half, half, (at + plan.gap) % LANES)
+            before = slide(of_driving, start - BED_REACH, BED_REACH, (at + plan.left_at) % LANES)
+            after = slide(of_driving, start + cols, BED_REACH, (at + plan.right_at) % LANES)
+            ahead = (lane + (LANES - plan.gap - at)) % LANES
+            of_observed = sub < 4
+            first = jnp.where(jnp.logical_and(of_observed, ahead < BED_REACH), before, first)
+            second = jnp.where(jnp.logical_and(of_observed, ahead >= plan.right_at - plan.gap), after, second)
+            value = jnp.where(sub % 2 == 0, first, second)
             ahead = (lane + (LANES - plan.gap)) % LANES
             block = value if block is None else jnp.where(ahead >= r * width, value, block)
         at = pl.multiple_of(place * (own * plan.in_rows), 8) + q * plan.in_rows
         here = pl.ds(at, plan.vel_rows)
         out_ref[here, :] = jnp.where(in_gap, block, out_ref[here, :])
-        out_ref[pl.ds(at + plan.vel_rows, rows), :] = line
+        if not 0 <= q < own:
+            return
+        line = None
+        step, offset = start // LANES, start % LANES
+        for r in range(rows):
+            for c in range(2):
+                row = c * skip + step * rows + r
+                put = (2 * r + c) * cols
+                value = lane_roll(driving_ref[row : row + 1, :], put - offset)
+                line = value if line is None else jnp.where(lane[:1] >= put, value, line)
+        out_ref[pl.ds(at + plan.vel_rows, 1), :] = line
 
     for q in range(own):
         column_block(q)
@@ -208,16 +225,24 @@
             total = total + arrived(part, row)
         return total
 
-    def from_gap(index):
-        shift = plan.low - plan.gap
-        left, right = over_parts(2 * index), over_parts(2 * index + 1)
-        return jnp.where(lane % width < plan.low + plan.half, lane_roll(left, shift), lane_roll(right, shift + plan.half))
-
-    def from_line(index):
-        plane = lane_roll(lines[0], plan.low - index * plan.wide)
-        for r in range(1, rows):
-            plane = jnp.where(lane >= r * width, lane_roll(lines[r], r * width + plan.low - index * plan.wide), plane)
+    def moved(value, source, target):
+        return lane_roll(value, target - source)
+
+    def from_gap(halves):
+        left, right = (moved(value, plan.gap, plan.low + h * plan.half) for h, value in enumerate(halves))
+        return jnp.where(lane % width < plan.low + plan.half, left, right)
+
+    def from_line(c):
+        plane = None
+        for r in range(rows):
+            value = moved(line, (2 * r + c) * plan.cols, r * width + plan.halo)
+            plane = value if plane is None else jnp.where(lane >= r * width, value, plane)
         return plane
+
+    def driving_of(c, halves):
+        left = moved(halves[0], plan.left_at, plan.halo - BED_REACH)
+        right = moved(halves[1], plan.right_at, plan.halo + plan.cols)
+        return jnp.where(centre, from_line(c), jnp.where(lane % width < plan.halo, left, right))
 
     def x_pair(value, edge):
         after = lane_roll(value, -width)
@@ -236,13 +261,15 @@
         for c in range(2):
             for k in range(here):
                 field[c, part * here + k] = arrived(part, c * here + k)
-    lines = [over_parts(plan.vel_rows + r) for r in range(rows)]
+    line = over_parts(plan.vel_rows)
+    gaps = [[over_parts(2 * n), over_parts(2 * n + 1)] for n in range(4)]
     reached = jnp.logical_and(lane % width >= plan.low, lane % width < plan.gap)
-    driving = [2.0 * from_line(c) for c in range(2)]
-    observed = [from_gap(c) for c in range(2)]
-    mask = jnp.where(reached, from_gap(2), 0.0)
+    centre = jnp.logical_and(lane % width >= plan.halo, lane % width < plan.halo + plan.cols)
+    driving = [2.0 * driving_of(c, gaps[c]) for c in range(2)]
+    observed = [from_gap(gaps[c]) for c in range(2)]
+    mask = jnp.where(reached, from_gap(gaps[2]), 0.0)
     ice = mask != 0.0
-    friction = jnp.where(mask == 1.0, jnp.exp(from_line(2)), 0.0)
+    friction = jnp.where(mask == 1.0, jnp.exp(from_gap(gaps[3])), 0.0)
 
     def stencil(k, keep):
         u, v = field[0, k], field[1, k]
@@ -357,8 +384,6 @@
     sweep(False)
     base, top = sweep(True)
 
-    centre = jnp.logical_and(lane % width >= plan.halo, lane % width < plan.halo + plan.cols)
-
     def send(k, carry):
         both = jnp.where(centre, field[0, k], lane_roll(field[1, k], plan.cols))
         out_ref[pl.ds((k // here) * size * plan.out_rows + k % here, size, stride=plan.out_rows), :] = both
@@ -539,8 +564,8 @@
     limit = pltpu.CompilerParams(vmem_limit_bytes=(16 if plan.unrolled else 40) * MIB)
     inputs = [as_lines(x) for x in (velocity_init, driving, observed, log_friction, ice_mask)]
 
-    def exchange(blocks, unit):
-        shaped = blocks.reshape(blocks.shape[0] // unit, unit, LANES)
+    def exchange(blocks):
+        shaped = blocks.reshape(blocks.shape[0], 1, LANES)
         return lax.all_to_all(shaped, ("layer", "map"), split_axis=0, concat_axis=0, tiled=True).reshape(blocks.shape)
 
     packed = pl.pallas_call(
@@ -556,7 +581,7 @@
         name="pack",
     )(*(pltpu.with_memory_space_constraint(x, pltpu.HBM) for x in inputs))
 
-    windows = exchange(packed, 2)
+    windows = exchange(packed)
 
     plane = (plan.layers, plan.map_size, LANES)
     solved = pl.pallas_call(
@@ -577,7 +602,7 @@
         name="solve",
     )(windows)
 
-    back = exchange(solved, 1)
+    back = exchange(solved)
 
     vel_lines, log_lines = inputs[0].reshape(2, -1, LANES), inputs[3]
     velocity, friction_new, misfit = pl.pallas_call(

time: 29.3 us -> 29 us (0.990)
  blocking collectives: 25.2 us -> 24.9 us
    all_to_all x2, blocking collectives: 25.2 us -> 24.9 us  [exchange(): lax.all_to_all(shaped, ('layer', 'map'), split_axis=0, concat_axis=0, til...]
where the time goes in v10:
time: 29 us; the launch traced here: 28.7 us
  blocking collectives  24.9 us (86%)
  Pallas kernels  3.19 us (11%)
  between operations  0.64 us (2%)
    all_to_all x2, blocking collectives, exchange(): lax.all_to_all(shaped, ('layer', 'map'), split_axis=0, concat_axis=0, til...  24.9 us
    pallas_call x1, Pallas kernels, on_device(): pl.pallas_call(functools.partial(pack_kernel, plan), out_shape=jax.ShapeD...  1.23 us
    pallas_call x1, Pallas kernels, on_device(): pl.pallas_call(functools.partial(solve_kernel, plan), out_shape=jax.Shape...  1.09 us
    pallas_call x1, Pallas kernels, on_device(): pl.pallas_call(functools.partial(unpack_kernel, plan), out_shape=(jax.Sha...  0.86 us

profile of v10, /device:TPU:0, one launch (start us, length us, event | category | flops | bytes accessed | tf_op | source)
XLA Modules:
  0.0 28.7 jit_solution(145302426009066134)
XLA Ops:
  0.6 1.2 %pack.1 = f32[288,128]{1,0:T(8,128)S(1)} custom-call(f32[128,128]{1,0:T(8,128)} %bitcast.50, f32[8,128]{1,0:T(8,128)} %bitcast.51, f32[8,128]{1,0:T(8,128)} %bitcast.52, f32[4,128]{1,0:T(4,128)} %bitcast.48, s32[4,128]{1,0:T(4,128)} %bitcast.53), custom_call_target="tpu_custom_call" | custom-call | tf_op jit(solution)/shard_map/pack/pallas_call | solution.py:571
  1.9 15.4 %all_to_all.10 = f32[288,1,128]{2,1,0:T(1,128)S(1)} all-to-all(f32[288,1,128]{2,1,0:T(1,128)S(1)} %bitcast.45), channel_id=1, replica_groups=mesh['map'=8,'layer'=4] {'layer','map'}, dimensions={0} | all-to-all | bytes 294912 | tf_op jit(solution)/shard_map/all_to_all | solution.py:569
  17.3 1.1 %solve.1 = f32[160,128]{1,0:T(8,128)S(1)} custom-call(f32[288,128]{1,0:T(8,128)S(1)} %bitcast.44), custom_call_target="tpu_custom_call" | custom-call | tf_op jit(solution)/shard_map/solve/pallas_call | solution.py:587
  18.4 0.0 copy-start
  18.4 9.5 %all_to_all.11 = f32[160,1,128]{2,1,0:T(1,128)S(1)} all-to-all(f32[160,1,128]{2,1,0:T(1,128)S(1)} %bitcast.46), channel_id=1, replica_groups=mesh['map'=8,'layer'=4] {'layer','map'}, dimensions={0} | all-to-all | bytes 163840 | tf_op jit(solution)/shard_map/all_to_all | solution.py:569
  27.8 0.0 copy-done
  27.8 0.9 %unpack.1 = (f32[2,64,128]{2,1,0:T(8,128)}, f32[4,128]{1,0:T(4,128)}, f32[1,1]{1,0:T(1,128)}) custom-call(f32[160,128]{1,0:T(8,128)S(1)} %bitcast.47, f32[4,128]{1,0:T(4,128)S(1)} %bitcast.49), custom_call_target="tpu_custom_call" | custom-call | tf_op jit(solution)/shard_map/unpack/pallas_call | solution.py:608
Async XLA Ops:
  18.4 9.5 %copy-start = (f32[2,256]{1,0:T(2,128)S(1)}, f32[2,256]{1,0:T(2,128)}, u32[]{:S(2)}) copy-start(f32[2,256]{1,0:T(2,128)} %param.8) | copy-start | bytes 6148

commit v11 on v10

--- a/solution.py
+++ b/solution.py
@@ -114,10 +114,10 @@
             for r in range(rows):
                 value = slide(velocity(r), plan.cols * t - plan.halo, width, r * width)
                 block = value if block is None else jnp.where(lane >= r * width, value, block)
-            at = i * plan.per_chunk * plan.in_rows
+            at = (plan.chunks - 1 - i) * plan.per_chunk * plan.in_rows
             if not isinstance(at, int):
                 at = pl.multiple_of(at, 8)
-            at = at + t * plan.in_rows
+            at = at + (plan.per_chunk - 1 - t) * plan.in_rows
             out_ref[pl.ds(at, plan.vel_rows), :] = jnp.where(in_gap, 0.0, block)
             out_ref[pl.ds(at + plan.vel_rows, 1), :] = no_line
         return carry
@@ -176,7 +176,7 @@
             value = jnp.where(sub % 2 == 0, first, second)
             ahead = (lane + (LANES - plan.gap)) % LANES
             block = value if block is None else jnp.where(ahead >= r * width, value, block)
-        at = pl.multiple_of(place * (own * plan.in_rows), 8) + q * plan.in_rows
+        at = pl.multiple_of((plan.layer_size - 1 - place) * (own * plan.in_rows), 8) + (own - 1 - q) * plan.in_rows
         here = pl.ds(at, plan.vel_rows)
         out_ref[here, :] = jnp.where(in_gap, block, out_ref[here, :])
         if not 0 <= q < own:
@@ -213,11 +213,15 @@
     sub = lax.broadcasted_iota(jnp.int32, shape, 0)
     last_group = lane >= LANES - width
     first_group = lane < width
-    x_end = jnp.logical_and(last_group, sub == size - 1)
-    x_start = jnp.logical_and(first_group, sub == 0)
+    x_end = jnp.logical_and(last_group, sub == 0)
+    x_start = jnp.logical_and(first_group, sub == size - 1)
+
+    def block_row(part, rows_of_block, row):
+        first = (plan.layer_size - 1 - part) * size * rows_of_block
+        return pl.ds(first + row, size, stride=rows_of_block)
 
     def arrived(part, row):
-        return in_ref[pl.ds(part * size * plan.in_rows + row, size, stride=plan.in_rows), :]
+        return in_ref[block_row(part, plan.in_rows, row), :]
 
     def over_parts(row):
         total = arrived(0, row)
@@ -247,8 +251,8 @@
     def x_pair(value, edge):
         after = lane_roll(value, -width)
         before = after if 2 * width == LANES else lane_roll(value, width)
-        after = jnp.where(last_group, pltpu.roll(after, size - 1, 0), after)
-        before = jnp.where(first_group, pltpu.roll(before, 1, 0), before)
+        after = jnp.where(last_group, pltpu.roll(after, 1, 0), after)
+        before = jnp.where(first_group, pltpu.roll(before, size - 1, 0), before)
         return jnp.where(x_end, edge, after), jnp.where(x_start, edge, before)
 
     def y_pair(value):
@@ -386,7 +390,7 @@
 
     def send(k, carry):
         both = jnp.where(centre, field[0, k], lane_roll(field[1, k], plan.cols))
-        out_ref[pl.ds((k // here) * size * plan.out_rows + k % here, size, stride=plan.out_rows), :] = both
+        out_ref[block_row(k // here, plan.out_rows, k % here), :] = both
         return carry
 
     repeat(plan, layers, send)
@@ -483,7 +487,7 @@
     in_first = jnp.logical_and(lane >= plan.halo + plan.cols, lane < plan.halo + 2 * plan.cols)
     last_row = jnp.where(centre, gradient, jnp.where(in_first, misfit_line, grad_line))
     for part in range(plan.layer_size):
-        out_ref[pl.ds(part * size * plan.out_rows + here, size, stride=plan.out_rows), :] = last_row
+        out_ref[block_row(part, plan.out_rows, here), :] = last_row
 
 
 def unpack_kernel(
@@ -508,11 +512,11 @@
 
     lane = lax.broadcasted_iota(jnp.int32, (plan.out_rows, LANES), 1)
     def chunk(c, i):
-        at = i * plan.per_chunk * plan.out_rows
+        at = (plan.chunks - 1 - i) * plan.per_chunk * plan.out_rows
         if not isinstance(at, int):
             at = pl.multiple_of(at, 8)
         turned = [
-            lane_roll(in_ref[pl.ds(at + t * plan.out_rows, plan.out_rows), :], t * cols)
+            lane_roll(in_ref[pl.ds(at + (plan.per_chunk - 1 - t) * plan.out_rows, plan.out_rows), :], t * cols)
             for t in range(plan.per_chunk)
         ]
         for r in range(rows):
@@ -566,7 +570,14 @@
 
     def exchange(blocks):
         shaped = blocks.reshape(blocks.shape[0], 1, LANES)
-        return lax.all_to_all(shaped, ("layer", "map"), split_axis=0, concat_axis=0, tiled=True).reshape(blocks.shape)
+        ranks = [
+            m * plan.layer_size + part
+            for part in reversed(range(plan.layer_size))
+            for m in reversed(range(plan.map_size))
+        ]
+        return lax.all_to_all(
+            shaped, ("map", "layer"), split_axis=0, concat_axis=0, tiled=True, axis_index_groups=[ranks]
+        ).reshape(blocks.shape)
 
     packed = pl.pallas_call(
         functools.partial(pack_kernel, plan),

time: 29 us -> 28.9 us (level)
  no operation moved by 1% of the time
where the time goes in v11:
time: 28.9 us; the launch traced here: 28.6 us
  blocking collectives  24.8 us (86%)
  Pallas kernels  3.19 us (11%)
  between operations  0.64 us (2%)
    all_to_all x2, blocking collectives, exchange(): lax.all_to_all(shaped, ('map', 'layer'), split_axis=0, concat_axis=0, til...  24.8 us
    pallas_call x1, Pallas kernels, on_device(): pl.pallas_call(functools.partial(pack_kernel, plan), out_shape=jax.ShapeD...  1.23 us
    pallas_call x1, Pallas kernels, on_device(): pl.pallas_call(functools.partial(solve_kernel, plan), out_shape=jax.Shape...  1.09 us
    pallas_call x1, Pallas kernels, on_device(): pl.pallas_call(functools.partial(unpack_kernel, plan), out_shape=(jax.Sha...  0.86 us

profile of v11, /device:TPU:0, one launch (start us, length us, event | category | flops | bytes accessed | tf_op | source)
XLA Modules:
  0.0 28.6 jit_solution(4286076511798236111)
XLA Ops:
  0.6 1.2 %pack.1 = f32[288,128]{1,0:T(8,128)S(1)} custom-call(f32[128,128]{1,0:T(8,128)} %bitcast.50, f32[8,128]{1,0:T(8,128)} %bitcast.51, f32[8,128]{1,0:T(8,128)} %bitcast.52, f32[4,128]{1,0:T(4,128)} %bitcast.48, s32[4,128]{1,0:T(4,128)} %bitcast.53), custom_call_target="tpu_custom_call" | custom-call | tf_op jit(solution)/shard_map/pack/pallas_call | solution.py:582
  1.9 15.3 %all_to_all.10 = f32[288,1,128]{2,1,0:T(1,128)S(1)} all-to-all(f32[288,1,128]{2,1,0:T(1,128)S(1)} %bitcast.45), channel_id=1, replica_groups={{31,27,23,19,15,11,7,3,30,26,22,18,14,10,6,2,29,25,21,17,13,9,5,1,28,24..., dimensions={0} | all-to-all | bytes 294912 | tf_op jit(solution)/shard_map/all_to_all | solution.py:578
  17.2 1.1 %solve.1 = f32[160,128]{1,0:T(8,128)S(1)} custom-call(f32[288,128]{1,0:T(8,128)S(1)} %bitcast.44), custom_call_target="tpu_custom_call" | custom-call | tf_op jit(solution)/shard_map/solve/pallas_call | solution.py:598
  18.3 0.0 copy-start
  18.3 9.5 %all_to_all.11 = f32[160,1,128]{2,1,0:T(1,128)S(1)} all-to-all(f32[160,1,128]{2,1,0:T(1,128)S(1)} %bitcast.46), channel_id=1, replica_groups={{31,27,23,19,15,11,7,3,30,26,22,18,14,10,6,2,29,25,21,17,13,9,5,1,28,24..., dimensions={0} | all-to-all | bytes 163840 | tf_op jit(solution)/shard_map/all_to_all | solution.py:578
  27.8 0.0 copy-done
  27.8 0.9 %unpack.1 = (f32[2,64,128]{2,1,0:T(8,128)}, f32[4,128]{1,0:T(4,128)}, f32[1,1]{1,0:T(1,128)}) custom-call(f32[160,128]{1,0:T(8,128)S(1)} %bitcast.47, f32[4,128]{1,0:T(4,128)S(1)} %bitcast.49), custom_call_target="tpu_custom_call" | custom-call | tf_op jit(solution)/shard_map/unpack/pallas_call | solution.py:619
Async XLA Ops:
  18.3 9.5 %copy-start = (f32[2,256]{1,0:T(2,128)S(1)}, f32[2,256]{1,0:T(2,128)}, u32[]{:S(2)}) copy-start(f32[2,256]{1,0:T(2,128)} %param.8) | copy-start | bytes 6148

commit v12 on v11

--- a/solution.py
+++ b/solution.py
@@ -13,6 +13,7 @@
 LANES = 128
 REACH = 5
 BED_REACH = 3
+PAD = 8
 MIB = 1 << 20
 VELOCITY_COPIES = 4
 
@@ -46,7 +47,7 @@
         assert self.width * self.rows == LANES and self.cols * self.per_chunk == LANES
         assert self.low >= 0 and self.wide % 2 == 0 and self.width - self.wide >= self.half
         assert 2 * self.cols <= self.width and self.local_cols % LANES == 0
-        assert self.vel_rows == 8 and self.rows == 2 and 4 * self.cols <= LANES
+        assert self.vel_rows == 8 and self.rows == 2 and 4 * self.cols <= LANES and self.map_size % 8 == 0
 
 
 def repeat(plan, count, body, carry=0):
@@ -205,17 +206,13 @@
             column_block(q)
 
 
-def solve_kernel(plan, in_ref, out_ref, field, eta_ref, side, rhs, faces, ratio, inverse):
+def solve_kernel(plan, in_ref, out_ref, field, eta_ref, side, rhs, faces, ratio, inverse, swapped, eta_swapped):
     size, width, rows = plan.map_size, plan.width, plan.rows
     layers, here = plan.layers, plan.layers_here
     shape = (size, LANES)
     lane = lax.broadcasted_iota(jnp.int32, shape, 1)
-    sub = lax.broadcasted_iota(jnp.int32, shape, 0)
     last_group = lane >= LANES - width
     first_group = lane < width
-    x_end = jnp.logical_and(last_group, sub == 0)
-    x_start = jnp.logical_and(first_group, sub == size - 1)
-
     def block_row(part, rows_of_block, row):
         first = (plan.layer_size - 1 - part) * size * rows_of_block
         return pl.ds(first + row, size, stride=rows_of_block)
@@ -248,12 +245,20 @@
         right = moved(halves[1], plan.right_at, plan.halo + plan.cols)
         return jnp.where(centre, from_line(c), jnp.where(lane % width < plan.halo, left, right))
 
-    def x_pair(value, edge):
-        after = lane_roll(value, -width)
-        before = after if 2 * width == LANES else lane_roll(value, width)
-        after = jnp.where(last_group, pltpu.roll(after, 1, 0), after)
-        before = jnp.where(first_group, pltpu.roll(before, size - 1, 0), before)
-        return jnp.where(x_end, edge, after), jnp.where(x_start, edge, before)
+    body = pl.ds(PAD, size)
+
+    def x_pair(ref, index):
+        same = ref[index + (body,)]
+        after = jnp.where(last_group, ref[index + (pl.ds(PAD - 1, size),)], same)
+        before = jnp.where(first_group, ref[index + (pl.ds(PAD + 1, size),)], same)
+        return after, before
+
+    def swap_in(c, k, value):
+        swapped[c, k, body] = lane_roll(value, width)
+
+    edge = jnp.zeros((2, layers, PAD, LANES), jnp.float32)
+    swapped[:, :, pl.ds(0, PAD)] = edge
+    swapped[:, :, pl.ds(PAD + size, PAD)] = edge
 
     def y_pair(value):
         return lane_roll(value, -1), lane_roll(value, 1)
@@ -264,7 +269,9 @@
     for part in range(plan.layer_size):
         for c in range(2):
             for k in range(here):
-                field[c, part * here + k] = arrived(part, c * here + k)
+                value = arrived(part, c * here + k)
+                field[c, part * here + k] = value
+                swap_in(c, part * here + k, value)
     line = over_parts(plan.vel_rows)
     gaps = [[over_parts(2 * n), over_parts(2 * n + 1)] for n in range(4)]
     reached = jnp.logical_and(lane % width >= plan.low, lane % width < plan.gap)
@@ -277,8 +284,8 @@
 
     def stencil(k, keep):
         u, v = field[0, k], field[1, k]
-        u_east, u_west = x_pair(u, 0.0)
-        v_east, v_west = x_pair(v, 0.0)
+        u_east, u_west = x_pair(swapped, (0, k))
+        v_east, v_west = x_pair(swapped, (1, k))
         u_north, u_south = y_pair(u)
         v_north, v_south = y_pair(v)
         stretch_x = u_east - u_west
@@ -288,7 +295,10 @@
         half_v = 0.5 * v
         eta = viscosity(rate)
         eta_edge = viscosity(0.25 * (u * u + half_v * half_v))
-        eta_east, eta_west = x_pair(eta, eta_edge)
+        eta_swapped[k, body] = lane_roll(eta, width)
+        eta_swapped[k, pl.ds(PAD - 1, 1)] = eta_edge[:1]
+        eta_swapped[k, pl.ds(PAD + size, 1)] = eta_edge[size - 1 :]
+        eta_east, eta_west = x_pair(eta_swapped, (k,))
         eta_north, eta_south = y_pair(eta)
         east, west = eta + eta_east, eta + eta_west
         north, south = eta + eta_north, eta + eta_south
@@ -376,11 +386,13 @@
             total = rhs[c, middle] + (lower[0] * lower[2][c] + upper[0] * upper[2][c])
             centre_value.append(jnp.where(ice, total * inv, 0.0))
             field[c, middle] = centre_value[c]
+            swap_in(c, middle, centre_value[c])
 
         def solved(k, nearer):
             current = tuple(jnp.where(ice, rhs[c, k] + ratio[c, k] * nearer[c], 0.0) for c in range(2))
             for c in range(2):
                 field[c, k] = current[c]
+                swap_in(c, k, current[c])
             return current
 
         return spread(tuple(centre_value), solved)
@@ -400,8 +412,10 @@
 
     def side_sum(k, value):
         east, west, north, south = (faces[n, k] for n in range(4))
-        u_east, u_west = x_pair(value[0], 0.0)
-        v_east, v_west = x_pair(value[1], 0.0)
+        for c in range(2):
+            swap_in(c, k, value[c])
+        u_east, u_west = x_pair(swapped, (0, k))
+        v_east, v_west = x_pair(swapped, (1, k))
         u_north, u_south = y_pair(value[0])
         v_north, v_south = y_pair(value[1])
         first = 4.0 * (east * u_east + west * u_west) + (north * u_north + south * u_south)
@@ -608,6 +622,8 @@
             pltpu.VMEM((4,) + plane, f32),
             pltpu.VMEM((2,) + plane, f32),
             pltpu.VMEM((2,) + plane, f32),
+            pltpu.VMEM((2, plan.layers, plan.map_size + 2 * PAD, LANES), f32),
+            pltpu.VMEM((plan.layers, plan.map_size + 2 * PAD, LANES), f32),
         ],
         compiler_params=limit,
         name="solve",

time: 28.9 us -> 29 us (level)
  no operation moved by 1% of the time
where the time goes in v12:
time: 29 us; the launch traced here: 28.7 us
  blocking collectives  24.8 us (86%)
  Pallas kernels  3.25 us (11%)
  between operations  0.64 us (2%)
    all_to_all x2, blocking collectives, exchange(): lax.all_to_all(shaped, ('map', 'layer'), split_axis=0, concat_axis=0, til...  24.8 us
    pallas_call x1, Pallas kernels, on_device(): pl.pallas_call(functools.partial(pack_kernel, plan), out_shape=jax.ShapeD...  1.23 us
    pallas_call x1, Pallas kernels, on_device(): pl.pallas_call(functools.partial(solve_kernel, plan), out_shape=jax.Shape...  1.15 us
    pallas_call x1, Pallas kernels, on_device(): pl.pallas_call(functools.partial(unpack_kernel, plan), out_shape=(jax.Sha...  0.86 us

profile of v12, /device:TPU:0, one launch (start us, length us, event | category | flops | bytes accessed | tf_op | source)
XLA Modules:
  0.0 28.7 jit_solution(13663209086387250096)
XLA Ops:
  0.6 1.2 %pack.1 = f32[288,128]{1,0:T(8,128)S(1)} custom-call(f32[128,128]{1,0:T(8,128)} %bitcast.50, f32[8,128]{1,0:T(8,128)} %bitcast.51, f32[8,128]{1,0:T(8,128)} %bitcast.52, f32[4,128]{1,0:T(4,128)} %bitcast.48, s32[4,128]{1,0:T(4,128)} %bitcast.53), custom_call_target="tpu_custom_call" | custom-call | tf_op jit(solution)/shard_map/pack/pallas_call | solution.py:596
  1.9 15.3 %all_to_all.10 = f32[288,1,128]{2,1,0:T(1,128)S(1)} all-to-all(f32[288,1,128]{2,1,0:T(1,128)S(1)} %bitcast.45), channel_id=1, replica_groups={{31,27,23,19,15,11,7,3,30,26,22,18,14,10,6,2,29,25,21,17,13,9,5,1,28,24..., dimensions={0} | all-to-all | bytes 294912 | tf_op jit(solution)/shard_map/all_to_all | solution.py:592
  17.2 1.2 %solve.1 = f32[160,128]{1,0:T(8,128)S(1)} custom-call(f32[288,128]{1,0:T(8,128)S(1)} %bitcast.44), custom_call_target="tpu_custom_call" | custom-call | tf_op jit(solution)/shard_map/solve/pallas_call | solution.py:612
  18.3 0.0 copy-start
  18.3 9.5 %all_to_all.11 = f32[160,1,128]{2,1,0:T(1,128)S(1)} all-to-all(f32[160,1,128]{2,1,0:T(1,128)S(1)} %bitcast.46), channel_id=1, replica_groups={{31,27,23,19,15,11,7,3,30,26,22,18,14,10,6,2,29,25,21,17,13,9,5,1,28,24..., dimensions={0} | all-to-all | bytes 163840 | tf_op jit(solution)/shard_map/all_to_all | solution.py:592
  27.8 0.0 copy-done
  27.8 0.9 %unpack.1 = (f32[2,64,128]{2,1,0:T(8,128)}, f32[4,128]{1,0:T(4,128)}, f32[1,1]{1,0:T(1,128)}) custom-call(f32[160,128]{1,0:T(8,128)S(1)} %bitcast.47, f32[4,128]{1,0:T(4,128)S(1)} %bitcast.49), custom_call_target="tpu_custom_call" | custom-call | tf_op jit(solution)/shard_map/unpack/pallas_call | solution.py:635
Async XLA Ops:
  18.3 9.5 %copy-start = (f32[2,256]{1,0:T(2,128)S(1)}, f32[2,256]{1,0:T(2,128)}, u32[]{:S(2)}) copy-start(f32[2,256]{1,0:T(2,128)} %param.8) | copy-start | bytes 6148

commit v13 on v11

--- a/solution.py
+++ b/solution.py
@@ -275,7 +275,7 @@
     ice = mask != 0.0
     friction = jnp.where(mask == 1.0, jnp.exp(from_gap(gaps[3])), 0.0)
 
-    def stencil(k, keep):
+    def stencil(k):
         u, v = field[0, k], field[1, k]
         u_east, u_west = x_pair(u, 0.0)
         v_east, v_west = x_pair(v, 0.0)
@@ -298,11 +298,10 @@
         side[1, k] = along_x + 4.0 * along_y
         rhs[0, k] = driving[0] + (4.0 * (east * u_east + west * u_west) + (north * u_north + south * u_south))
         rhs[1, k] = driving[1] + ((east * v_east + west * v_west) + 4.0 * (north * v_north + south * v_south))
-        if keep:
-            faces[0, k] = east
-            faces[1, k] = west
-            faces[2, k] = north
-            faces[3, k] = south
+        faces[0, k] = east
+        faces[1, k] = west
+        faces[2, k] = north
+        faces[3, k] = south
 
     def coupling_of(k):
         return (2.0 * layers * layers) * (eta_ref[k] + eta_ref[k + 1])
@@ -347,20 +346,20 @@
             below = body(k, below)
         return below, above
 
-    def sweep(keep):
+    def sweep():
         def stencil_body(k, carry):
-            stencil(k, keep)
+            stencil(k)
             return carry
 
         bed = tuple(2.0 * friction for _ in range(2))
         lower, upper = (zero, bed, (zero, zero)), (zero, (zero, zero), (zero, zero))
         if plan.unrolled:
-            stencil(0, keep)
-            stencil(layers - 1, keep)
+            stencil(0)
+            stencil(layers - 1)
             for step in range(layers - 1 - middle):
-                stencil(step + 1, keep)
+                stencil(step + 1)
                 if layers - 2 - step > step + 1:
-                    stencil(layers - 2 - step, keep)
+                    stencil(layers - 2 - step)
                 lower, upper = fronts(step, (lower, upper))
         else:
             repeat(plan, layers, stencil_body)
@@ -385,8 +384,8 @@
 
         return spread(tuple(centre_value), solved)
 
-    sweep(False)
-    base, top = sweep(True)
+    nothing = (zero, zero)
+    base, top = lax.fori_loop(0, 2, lambda _, carry: sweep(), (nothing, nothing))
 
     def send(k, carry):
         both = jnp.where(centre, field[0, k], lane_roll(field[1, k], plan.cols))

time: 28.9 us -> 29 us (level)
  no operation moved by 1% of the time
where the time goes in v13:
time: 29 us; the launch traced here: 28.7 us
  blocking collectives  24.8 us (86%)
  Pallas kernels  3.25 us (11%)
  between operations  0.64 us (2%)
    all_to_all x2, blocking collectives, exchange(): lax.all_to_all(shaped, ('map', 'layer'), split_axis=0, concat_axis=0, til...  24.8 us
    pallas_call x1, Pallas kernels, on_device(): pl.pallas_call(functools.partial(pack_kernel, plan), out_shape=jax.ShapeD...  1.23 us
    pallas_call x1, Pallas kernels, on_device(): pl.pallas_call(functools.partial(solve_kernel, plan), out_shape=jax.Shape...  1.16 us
    pallas_call x1, Pallas kernels, on_device(): pl.pallas_call(functools.partial(unpack_kernel, plan), out_shape=(jax.Sha...  0.86 us

profile of v13, /device:TPU:0, one launch (start us, length us, event | category | flops | bytes accessed | tf_op | source)
XLA Modules:
  0.0 28.7 jit_solution(1142157788841396897)
XLA Ops:
  0.6 1.2 %pack.1 = f32[288,128]{1,0:T(8,128)S(1)} custom-call(f32[128,128]{1,0:T(8,128)} %bitcast.50, f32[8,128]{1,0:T(8,128)} %bitcast.51, f32[8,128]{1,0:T(8,128)} %bitcast.52, f32[4,128]{1,0:T(4,128)} %bitcast.48, s32[4,128]{1,0:T(4,128)} %bitcast.53), custom_call_target="tpu_custom_call" | custom-call | tf_op jit(solution)/shard_map/pack/pallas_call | solution.py:581
  1.9 15.3 %all_to_all.10 = f32[288,1,128]{2,1,0:T(1,128)S(1)} all-to-all(f32[288,1,128]{2,1,0:T(1,128)S(1)} %bitcast.45), channel_id=1, replica_groups={{31,27,23,19,15,11,7,3,30,26,22,18,14,10,6,2,29,25,21,17,13,9,5,1,28,24..., dimensions={0} | all-to-all | bytes 294912 | tf_op jit(solution)/shard_map/all_to_all | solution.py:577
  17.2 1.2 %solve.1 = f32[160,128]{1,0:T(8,128)S(1)} custom-call(f32[288,128]{1,0:T(8,128)S(1)} %bitcast.44), custom_call_target="tpu_custom_call" | custom-call | tf_op jit(solution)/shard_map/solve/pallas_call | solution.py:597
  18.3 0.0 copy-start
  18.3 9.5 %all_to_all.11 = f32[160,1,128]{2,1,0:T(1,128)S(1)} all-to-all(f32[160,1,128]{2,1,0:T(1,128)S(1)} %bitcast.46), channel_id=1, replica_groups={{31,27,23,19,15,11,7,3,30,26,22,18,14,10,6,2,29,25,21,17,13,9,5,1,28,24..., dimensions={0} | all-to-all | bytes 163840 | tf_op jit(solution)/shard_map/all_to_all | solution.py:577
  27.8 0.0 copy-done
  27.8 0.9 %unpack.1 = (f32[2,64,128]{2,1,0:T(8,128)}, f32[4,128]{1,0:T(4,128)}, f32[1,1]{1,0:T(1,128)}) custom-call(f32[160,128]{1,0:T(8,128)S(1)} %bitcast.47, f32[4,128]{1,0:T(4,128)S(1)} %bitcast.49), custom_call_target="tpu_custom_call" | custom-call | tf_op jit(solution)/shard_map/unpack/pallas_call | solution.py:618
Async XLA Ops:
  18.3 9.5 %copy-start = (f32[2,256]{1,0:T(2,128)S(1)}, f32[2,256]{1,0:T(2,128)}, u32[]{:S(2)}) copy-start(f32[2,256]{1,0:T(2,128)} %param.8) | copy-start | bytes 6148

commit v14 on v12

--- a/solution.py
+++ b/solution.py
@@ -522,7 +522,7 @@
 
     misfit_sum = summed(plan.halo + cols)
     grad_sum = summed(plan.halo + cols + width)
-    scale = step_size / jnp.sqrt(grad_sum / plan.column_count + 1e-06)
+    scale = step_size * lax.rsqrt(grad_sum / plan.column_count + 1e-06)
 
     lane = lax.broadcasted_iota(jnp.int32, (plan.out_rows, LANES), 1)
     def chunk(c, i):
@@ -545,9 +545,13 @@
                 owner, step = i // local_chunks, i % local_chunks
                 grad_ref[owner, pl.ds(step * rows + r, 1), :] = row[here : here + 1]
 
-    out = [pltpu.make_async_copy(vel_ref.at[c], vel_hbm.at[c], leave.at[c]) for c in range(2)]
-    out.append(pltpu.make_async_copy(friction_ref, friction_hbm, leave.at[2]))
-    out.append(pltpu.make_async_copy(misfit_ref, misfit_hbm, leave.at[3]))
+    def leaving(n, source, target):
+        return pltpu.make_async_copy(source, target, leave.at[n])
+
+    lines = plan.chunks * rows
+    spans = [(c, pl.ds(k * lines, lines)) for c in range(2) for k in range(here)]
+    out = [leaving(n, vel_ref.at[span], vel_hbm.at[span]) for n, span in enumerate(spans)]
+    small = [leaving(2 * here, friction_ref, friction_hbm), leaving(2 * here + 1, misfit_ref, misfit_hbm)]
     for c in range(2):
 
         def chunk_body(i, carry):
@@ -555,12 +559,13 @@
             return carry
 
         repeat(plan, plan.chunks, chunk_body)
-        out[c].start()
+        for copy in out[c * here : (c + 1) * here]:
+            copy.start()
     friction_ref[...] = log_ref[...] - grad_ref[lax.axis_index("layer")] * scale
-    out[2].start()
+    small[0].start()
     misfit_ref[...] = 0.5 * misfit_sum / plan.column_count
-    out[3].start()
-    for copy in out:
+    small[1].start()
+    for copy in out + small:
         copy.wait()
 
 
@@ -646,7 +651,7 @@
             pltpu.VMEM(log_lines.shape, f32),
             pltpu.VMEM((1, 1), f32),
             pltpu.VMEM((plan.layer_size,) + log_lines.shape, f32),
-            pltpu.SemaphoreType.DMA((4,)),
+            pltpu.SemaphoreType.DMA((plan.vel_rows + 2,)),
         ],
         compiler_params=limit,
         name="unpack",

time: 29 us -> 29 us (level)
  no operation moved by 1% of the time
where the time goes in v14:
time: 29 us; the launch traced here: 28.7 us
  blocking collectives  24.8 us (86%)
  Pallas kernels  3.3 us (11%)
  between operations  0.64 us (2%)
    all_to_all x2, blocking collectives, exchange(): lax.all_to_all(shaped, ('map', 'layer'), split_axis=0, concat_axis=0, til...  24.8 us
    pallas_call x1, Pallas kernels, on_device(): pl.pallas_call(functools.partial(pack_kernel, plan), out_shape=jax.ShapeD...  1.23 us
    pallas_call x1, Pallas kernels, on_device(): pl.pallas_call(functools.partial(solve_kernel, plan), out_shape=jax.Shape...  1.15 us
    pallas_call x1, Pallas kernels, on_device(): pl.pallas_call(functools.partial(unpack_kernel, plan), out_shape=(jax.Sha...  0.91 us

profile of v14, /device:TPU:0, one launch (start us, length us, event | category | flops | bytes accessed | tf_op | source)
XLA Modules:
  0.0 28.7 jit_solution(16747018521538479707)
XLA Ops:
  0.6 1.2 %pack.1 = f32[288,128]{1,0:T(8,128)S(1)} custom-call(f32[128,128]{1,0:T(8,128)} %bitcast.50, f32[8,128]{1,0:T(8,128)} %bitcast.51, f32[8,128]{1,0:T(8,128)} %bitcast.52, f32[4,128]{1,0:T(4,128)} %bitcast.48, s32[4,128]{1,0:T(4,128)} %bitcast.53), custom_call_target="tpu_custom_call" | custom-call | tf_op jit(solution)/shard_map/pack/pallas_call | solution.py:601
  1.9 15.3 %all_to_all.10 = f32[288,1,128]{2,1,0:T(1,128)S(1)} all-to-all(f32[288,1,128]{2,1,0:T(1,128)S(1)} %bitcast.45), channel_id=1, replica_groups={{31,27,23,19,15,11,7,3,30,26,22,18,14,10,6,2,29,25,21,17,13,9,5,1,28,24..., dimensions={0} | all-to-all | bytes 294912 | tf_op jit(solution)/shard_map/all_to_all | solution.py:597
  17.2 1.2 %solve.1 = f32[160,128]{1,0:T(8,128)S(1)} custom-call(f32[288,128]{1,0:T(8,128)S(1)} %bitcast.44), custom_call_target="tpu_custom_call" | custom-call | tf_op jit(solution)/shard_map/solve/pallas_call | solution.py:617
  18.3 0.0 copy-start
  18.3 9.5 %all_to_all.11 = f32[160,1,128]{2,1,0:T(1,128)S(1)} all-to-all(f32[160,1,128]{2,1,0:T(1,128)S(1)} %bitcast.46), channel_id=1, replica_groups={{31,27,23,19,15,11,7,3,30,26,22,18,14,10,6,2,29,25,21,17,13,9,5,1,28,24..., dimensions={0} | all-to-all | bytes 163840 | tf_op jit(solution)/shard_map/all_to_all | solution.py:597
  27.8 0.0 copy-done
  27.8 0.9 %unpack.1 = (f32[2,64,128]{2,1,0:T(8,128)}, f32[4,128]{1,0:T(4,128)}, f32[1,1]{1,0:T(1,128)}) custom-call(f32[160,128]{1,0:T(8,128)S(1)} %bitcast.47, f32[4,128]{1,0:T(4,128)S(1)} %bitcast.49), custom_call_target="tpu_custom_call" | custom-call | tf_op jit(solution)/shard_map/unpack/pallas_call | solution.py:640
Async XLA Ops:
  18.3 9.5 %copy-start = (f32[2,256]{1,0:T(2,128)S(1)}, f32[2,256]{1,0:T(2,128)}, u32[]{:S(2)}) copy-start(f32[2,256]{1,0:T(2,128)} %param.8) | copy-start | bytes 6148

commit v15 on v12

--- a/solution.py
+++ b/solution.py
@@ -44,10 +44,19 @@
         self.right_at = self.gap + self.cols // 2 + 1
         self.out_rows = self.layers_here + 1
         self.unrolled = self.map_size <= 8
+        assert self.layer_size & (self.layer_size - 1) == 0
         assert self.width * self.rows == LANES and self.cols * self.per_chunk == LANES
         assert self.low >= 0 and self.wide % 2 == 0 and self.width - self.wide >= self.half
         assert 2 * self.cols <= self.width and self.local_cols % LANES == 0
         assert self.vel_rows == 8 and self.rows == 2 and 4 * self.cols <= LANES and self.map_size % 8 == 0
+
+    def chunk_place(self, i):
+        here = self.local_cols // LANES
+        return group_at(i // here) * here + (here - 1 - i % here)
+
+
+def group_at(layer):
+    return layer ^ (layer >> 1)
 
 
 def repeat(plan, count, body, carry=0):
@@ -115,7 +124,7 @@
             for r in range(rows):
                 value = slide(velocity(r), plan.cols * t - plan.halo, width, r * width)
                 block = value if block is None else jnp.where(lane >= r * width, value, block)
-            at = (plan.chunks - 1 - i) * plan.per_chunk * plan.in_rows
+            at = plan.chunk_place(i) * plan.per_chunk * plan.in_rows
             if not isinstance(at, int):
                 at = pl.multiple_of(at, 8)
             at = at + (plan.per_chunk - 1 - t) * plan.in_rows
@@ -177,7 +186,8 @@
             value = jnp.where(sub % 2 == 0, first, second)
             ahead = (lane + (LANES - plan.gap)) % LANES
             block = value if block is None else jnp.where(ahead >= r * width, value, block)
-        at = pl.multiple_of((plan.layer_size - 1 - place) * (own * plan.in_rows), 8) + (own - 1 - q) * plan.in_rows
+        owner = place if 0 <= q < own else place - 1 if q < 0 else place + 1
+        at = pl.multiple_of(group_at(owner) * (own * plan.in_rows), 8) + (own - 1 - q % own) * plan.in_rows
         here = pl.ds(at, plan.vel_rows)
         out_ref[here, :] = jnp.where(in_gap, block, out_ref[here, :])
         if not 0 <= q < own:
@@ -214,7 +224,7 @@
     last_group = lane >= LANES - width
     first_group = lane < width
     def block_row(part, rows_of_block, row):
-        first = (plan.layer_size - 1 - part) * size * rows_of_block
+        first = group_at(part) * size * rows_of_block
         return pl.ds(first + row, size, stride=rows_of_block)
 
     def arrived(part, row):
@@ -526,7 +536,7 @@
 
     lane = lax.broadcasted_iota(jnp.int32, (plan.out_rows, LANES), 1)
     def chunk(c, i):
-        at = (plan.chunks - 1 - i) * plan.per_chunk * plan.out_rows
+        at = plan.chunk_place(i) * plan.per_chunk * plan.out_rows
         if not isinstance(at, int):
             at = pl.multiple_of(at, 8)
         turned = [
@@ -586,7 +596,7 @@
         shaped = blocks.reshape(blocks.shape[0], 1, LANES)
         ranks = [
             m * plan.layer_size + part
-            for part in reversed(range(plan.layer_size))
+            for part in sorted(range(plan.layer_size), key=group_at)
             for m in reversed(range(plan.map_size))
         ]
         return lax.all_to_all(

time: 29 us -> 28.9 us (level)
  no operation moved by 1% of the time
where the time goes in v15:
time: 28.9 us; the launch traced here: 28.6 us
  blocking collectives  24.7 us (85%)
  Pallas kernels  3.25 us (11%)
  between operations  0.64 us (2%)
    all_to_all x2, blocking collectives, exchange(): lax.all_to_all(shaped, ('map', 'layer'), split_axis=0, concat_axis=0, til...  24.7 us
    pallas_call x1, Pallas kernels, on_device(): pl.pallas_call(functools.partial(pack_kernel, plan), out_shape=jax.ShapeD...  1.23 us
    pallas_call x1, Pallas kernels, on_device(): pl.pallas_call(functools.partial(solve_kernel, plan), out_shape=jax.Shape...  1.15 us
    pallas_call x1, Pallas kernels, on_device(): pl.pallas_call(functools.partial(unpack_kernel, plan), out_shape=(jax.Sha...  0.86 us

profile of v15, /device:TPU:0, one launch (start us, length us, event | category | flops | bytes accessed | tf_op | source)
XLA Modules:
  0.0 28.6 jit_solution(15788904304239725090)
XLA Ops:
  0.6 1.2 %pack.1 = f32[288,128]{1,0:T(8,128)S(1)} custom-call(f32[128,128]{1,0:T(8,128)} %bitcast.50, f32[8,128]{1,0:T(8,128)} %bitcast.51, f32[8,128]{1,0:T(8,128)} %bitcast.52, f32[4,128]{1,0:T(4,128)} %bitcast.48, s32[4,128]{1,0:T(4,128)} %bitcast.53), custom_call_target="tpu_custom_call" | custom-call | tf_op jit(solution)/shard_map/pack/pallas_call | solution.py:606
  1.9 15.0 %all_to_all.10 = f32[288,1,128]{2,1,0:T(1,128)S(1)} all-to-all(f32[288,1,128]{2,1,0:T(1,128)S(1)} %bitcast.45), channel_id=1, replica_groups={{28,24,20,16,12,8,4,0,29,25,21,17,13,9,5,1,31,27,23,19,15,11,7,3,30,26,..., dimensions={0} | all-to-all | bytes 294912 | tf_op jit(solution)/shard_map/all_to_all | solution.py:602
  16.9 1.2 %solve.1 = f32[160,128]{1,0:T(8,128)S(1)} custom-call(f32[288,128]{1,0:T(8,128)S(1)} %bitcast.44), custom_call_target="tpu_custom_call" | custom-call | tf_op jit(solution)/shard_map/solve/pallas_call | solution.py:622
  18.0 0.0 copy-start
  18.0 9.7 %all_to_all.11 = f32[160,1,128]{2,1,0:T(1,128)S(1)} all-to-all(f32[160,1,128]{2,1,0:T(1,128)S(1)} %bitcast.46), channel_id=1, replica_groups={{28,24,20,16,12,8,4,0,29,25,21,17,13,9,5,1,31,27,23,19,15,11,7,3,30,26,..., dimensions={0} | all-to-all | bytes 163840 | tf_op jit(solution)/shard_map/all_to_all | solution.py:602
  27.7 0.0 copy-done
  27.7 0.9 %unpack.1 = (f32[2,64,128]{2,1,0:T(8,128)}, f32[4,128]{1,0:T(4,128)}, f32[1,1]{1,0:T(1,128)}) custom-call(f32[160,128]{1,0:T(8,128)S(1)} %bitcast.47, f32[4,128]{1,0:T(4,128)S(1)} %bitcast.49), custom_call_target="tpu_custom_call" | custom-call | tf_op jit(solution)/shard_map/unpack/pallas_call | solution.py:645
Async XLA Ops:
  18.0 9.7 %copy-start = (f32[2,256]{1,0:T(2,128)S(1)}, f32[2,256]{1,0:T(2,128)}, u32[]{:S(2)}) copy-start(f32[2,256]{1,0:T(2,128)} %param.8) | copy-start | bytes 6148

commit v16 on v12

--- a/solution.py
+++ b/solution.py
@@ -96,16 +96,20 @@
     for copy in copies[:VELOCITY_COPIES]:
         copy.wait()
 
+    def velocity_chunk(at, r):
+        return vel_ref[pl.ds(at * rows + r, plan.vel_rows, stride=plan.chunks * rows), :]
+
+    held = None
+    if plan.unrolled:
+        held = [[velocity_chunk(at, r) for at in range(plan.chunks)] for r in range(rows)]
+
     def chunk_windows(i, carry):
         def velocity(r):
             def part(step):
                 chunk = i + step
-                if isinstance(chunk, int) and not 0 <= chunk < plan.chunks:
-                    return jnp.zeros(shape, jnp.float32)
-                at = chunk if isinstance(chunk, int) else jnp.clip(chunk, 0, plan.chunks - 1)
-                value = vel_ref[pl.ds(at * rows + r, plan.vel_rows, stride=plan.chunks * rows), :]
-                if isinstance(chunk, int):
-                    return value
+                if held is not None:
+                    return held[r][chunk] if 0 <= chunk < plan.chunks else jnp.zeros(shape, jnp.float32)
+                value = velocity_chunk(jnp.clip(chunk, 0, plan.chunks - 1), r)
                 return jnp.where(jnp.logical_and(chunk >= 0, chunk < plan.chunks), value, 0.0)
 
             return part

time: 29 us -> 29 us (level)
  no operation moved by 1% of the time
where the time goes in v16:
time: 29 us; the launch traced here: 28.7 us
  blocking collectives  24.8 us (86%)
  Pallas kernels  3.25 us (11%)
  between operations  0.64 us (2%)
    all_to_all x2, blocking collectives, exchange(): lax.all_to_all(shaped, ('map', 'layer'), split_axis=0, concat_axis=0, til...  24.8 us
    pallas_call x1, Pallas kernels, on_device(): pl.pallas_call(functools.partial(pack_kernel, plan), out_shape=jax.ShapeD...  1.23 us
    pallas_call x1, Pallas kernels, on_device(): pl.pallas_call(functools.partial(solve_kernel, plan), out_shape=jax.Shape...  1.15 us
    pallas_call x1, Pallas kernels, on_device(): pl.pallas_call(functools.partial(unpack_kernel, plan), out_shape=(jax.Sha...  0.86 us

profile of v16, /device:TPU:0, one launch (start us, length us, event | category | flops | bytes accessed | tf_op | source)
XLA Modules:
  0.0 28.7 jit_solution(13663209086387250096)
XLA Ops:
  0.6 1.2 %pack.1 = f32[288,128]{1,0:T(8,128)S(1)} custom-call(f32[128,128]{1,0:T(8,128)} %bitcast.50, f32[8,128]{1,0:T(8,128)} %bitcast.51, f32[8,128]{1,0:T(8,128)} %bitcast.52, f32[4,128]{1,0:T(4,128)} %bitcast.48, s32[4,128]{1,0:T(4,128)} %bitcast.53), custom_call_target="tpu_custom_call" | custom-call | tf_op jit(solution)/shard_map/pack/pallas_call | solution.py:600
  1.9 15.3 %all_to_all.10 = f32[288,1,128]{2,1,0:T(1,128)S(1)} all-to-all(f32[288,1,128]{2,1,0:T(1,128)S(1)} %bitcast.45), channel_id=1, replica_groups={{31,27,23,19,15,11,7,3,30,26,22,18,14,10,6,2,29,25,21,17,13,9,5,1,28,24..., dimensions={0} | all-to-all | bytes 294912 | tf_op jit(solution)/shard_map/all_to_all | solution.py:596
  17.2 1.2 %solve.1 = f32[160,128]{1,0:T(8,128)S(1)} custom-call(f32[288,128]{1,0:T(8,128)S(1)} %bitcast.44), custom_call_target="tpu_custom_call" | custom-call | tf_op jit(solution)/shard_map/solve/pallas_call | solution.py:616
  18.3 0.0 copy-start
  18.3 9.5 %all_to_all.11 = f32[160,1,128]{2,1,0:T(1,128)S(1)} all-to-all(f32[160,1,128]{2,1,0:T(1,128)S(1)} %bitcast.46), channel_id=1, replica_groups={{31,27,23,19,15,11,7,3,30,26,22,18,14,10,6,2,29,25,21,17,13,9,5,1,28,24..., dimensions={0} | all-to-all | bytes 163840 | tf_op jit(solution)/shard_map/all_to_all | solution.py:596
  27.8 0.0 copy-done
  27.8 0.9 %unpack.1 = (f32[2,64,128]{2,1,0:T(8,128)}, f32[4,128]{1,0:T(4,128)}, f32[1,1]{1,0:T(1,128)}) custom-call(f32[160,128]{1,0:T(8,128)S(1)} %bitcast.47, f32[4,128]{1,0:T(4,128)S(1)} %bitcast.49), custom_call_target="tpu_custom_call" | custom-call | tf_op jit(solution)/shard_map/unpack/pallas_call | solution.py:639
Async XLA Ops:
  18.3 9.5 %copy-start = (f32[2,256]{1,0:T(2,128)S(1)}, f32[2,256]{1,0:T(2,128)}, u32[]{:S(2)}) copy-start(f32[2,256]{1,0:T(2,128)} %param.8) | copy-start | bytes 6148

commit v17 on v11

--- a/solution.py
+++ b/solution.py
@@ -205,7 +205,7 @@
             column_block(q)
 
 
-def solve_kernel(plan, in_ref, out_ref, field, eta_ref, side, rhs, faces, ratio, inverse):
+def solve_kernel(plan, in_ref, out_ref, field, eta_ref, side, rhs, faces, weight, gain):
     size, width, rows = plan.map_size, plan.width, plan.rows
     layers, here = plan.layers, plan.layers_here
     shape = (size, LANES)
@@ -307,53 +307,56 @@
     def coupling_of(k):
         return (2.0 * layers * layers) * (eta_ref[k] + eta_ref[k + 1])
 
+    def reciprocal(value):
+        guess = pl.reciprocal(value, approx=True)
+        return guess * (2.0 - value * guess)
+
     middle = layers // 2
     zero = jnp.zeros(shape, jnp.float32)
-
-    def eliminate(k, coupling, carry):
-        before, passed, value = carry
-        new_passed, new_value = [], []
+    one = jnp.ones(shape, jnp.float32)
+
+    def advance(k, coupling, carry):
+        flux, value, total = carry
+        across = reciprocal(coupling)
+        new_flux, new_value, new_total = [], [], []
         for c in range(2):
-            rest = side[c, k] + passed[c]
-            pivot = coupling + rest
-            guess = pl.reciprocal(pivot, approx=True)
-            correct = 2.0 - pivot * guess
-            new_passed.append((coupling * rest * guess) * correct)
-            inv = guess * correct
-            inverse[c, k] = inv
-            ratio[c, k] = coupling * inv
-            out = (rhs[c, k] + before * value[c]) * inv
-            rhs[c, k] = out
-            new_value.append(out)
-        return coupling, tuple(new_passed), tuple(new_value)
+            here_flux = flux[c] + side[c, k] * value[c]
+            after = value[c] + across * here_flux
+            here_total = total[c] + value[c] * rhs[c, k]
+            weight[c, k] = value[c]
+            gain[c, k] = reciprocal((coupling * value[c]) * after)
+            rhs[c, k] = here_total
+            new_flux.append(here_flux)
+            new_value.append(after)
+            new_total.append(here_total)
+        return tuple(new_flux), tuple(new_value), tuple(new_total)
 
     def lower_step(k, carry):
-        return eliminate(k, coupling_of(k), carry)
+        return advance(k, coupling_of(k), carry)
 
     def upper_step(k, carry):
-        return eliminate(k, coupling_of(k - 1), carry)
+        return advance(k, coupling_of(k - 1), carry)
 
     def fronts(step, carry):
         lower, upper = carry
         return lower_step(step, lower), upper_step(layers - 1 - step, upper)
 
-    def spread(first, body):
-        def outward(step, carry):
-            below, above = carry
-            return body(middle - 1 - step, below), body(middle + 1 + step, above)
-
-        below, above = repeat(plan, layers - 1 - middle, outward, (first, first))
+    def outward(body, carry):
+        def both(step, carry):
+            return body(middle - 1 - step, 0, body(middle + 1 + step, 1, carry))
+
+        carry = repeat(plan, layers - 1 - middle, both, carry)
         for k in range(2 * middle - layers, -1, -1):
-            below = body(k, below)
-        return below, above
+            carry = body(k, 0, carry)
+        return carry
 
     def sweep(keep):
         def stencil_body(k, carry):
             stencil(k, keep)
             return carry
 
-        bed = tuple(2.0 * friction for _ in range(2))
-        lower, upper = (zero, bed, (zero, zero)), (zero, (zero, zero), (zero, zero))
+        lower = ((2.0 * friction,) * 2, (one, one), (zero, zero))
+        upper = ((zero, zero), (one, one), (zero, zero))
         if plan.unrolled:
             stencil(0, keep)
             stencil(layers - 1, keep)
@@ -367,26 +370,36 @@
             lower, upper = repeat(plan, layers - 1 - middle, fronts, (lower, upper))
         for k in range(layers - 1 - middle, middle):
             lower = lower_step(k, lower)
-        centre_value = []
+        joints, start = [], []
         for c in range(2):
-            pivot = side[c, middle] + lower[1][c] + upper[1][c]
-            guess = pl.reciprocal(pivot, approx=True)
-            inv = guess * (2.0 - pivot * guess)
-            inverse[c, middle] = inv
-            total = rhs[c, middle] + (lower[0] * lower[2][c] + upper[0] * upper[2][c])
-            centre_value.append(jnp.where(ice, total * inv, 0.0))
-            field[c, middle] = centre_value[c]
-
-        def solved(k, nearer):
-            current = tuple(jnp.where(ice, rhs[c, k] + ratio[c, k] * nearer[c], 0.0) for c in range(2))
+            below, above = lower[1][c], upper[1][c]
+            product = below * above
+            inv = reciprocal(side[c, middle] * product + (lower[0][c] * above + upper[0][c] * below))
+            joint = (below, above, product, inv, reciprocal(below), reciprocal(above))
+            joints.append(joint)
+            solved = join(joint, rhs[c, middle], lower[2][c], upper[2][c])
+            field[c, middle] = jnp.where(ice, solved, 0.0)
+            start.append((solved * joint[4], solved * joint[5]))
+
+        def solved_layer(k, which, carry):
+            new = list(carry)
             for c in range(2):
-                field[c, k] = current[c]
-            return current
-
-        return spread(tuple(centre_value), solved)
+                scaled = carry[2 * which + c] + rhs[c, k] * gain[c, k]
+                field[c, k] = jnp.where(ice, weight[c, k] * scaled, 0.0)
+                new[2 * which + c] = scaled
+            return tuple(new)
+
+        outward(solved_layer, (start[0][0], start[1][0], start[0][1], start[1][1]))
+        return joints
+
+    def join(joint, right, lower_total, upper_total):
+        below, above, product, inv, _, _ = joint
+        return (right * product + (lower_total * above + upper_total * below)) * inv
 
     sweep(False)
-    base, top = sweep(True)
+    joints = sweep(True)
+    base = [field[c, 0] for c in range(2)]
+    top = [field[c, layers - 1] for c in range(2)]
 
     def send(k, carry):
         both = jnp.where(centre, field[0, k], lane_roll(field[1, k], plan.cols))
@@ -408,70 +421,46 @@
         second = (east * v_east + west * v_west) + 4.0 * (north * v_north + south * v_south)
         return first, second
 
-    carried = tuple(source[c] * inverse[c, layers - 1] for c in range(2))
-    for c in range(2):
-        rhs[c, layers - 1] = carried[c]
-
-    def first_inward(step, carried):
-        k = layers - 2 - step
-        out = tuple(coupling_of(k) * carried[c] * inverse[c, k] for c in range(2))
-        for c in range(2):
-            rhs[c, k] = out[c]
-        return out
-
-    carried = repeat(plan, layers - 2 - middle, first_inward, carried)
-    first_middle = tuple(coupling_of(middle) * carried[c] * inverse[c, middle] for c in range(2))
-
-    def first_outward(step, carry):
+    def side_sum(k, value):
+        east, west, north, south = (faces[n, k] for n in range(4))
+        u_east, u_west = x_pair(value[0], 0.0)
+        v_east, v_west = x_pair(value[1], 0.0)
+        u_north, u_south = y_pair(value[0])
+        v_north, v_south = y_pair(value[1])
+        first = 4.0 * (east * u_east + west * u_west) + (north * u_north + south * u_south)
+        second = (east * v_east + west * v_west) + 4.0 * (north * v_north + south * v_south)
+        return first, second
+
+    below_scaled = tuple(source[c] * joints[c][3] for c in range(2))
+    first_middle = tuple(below_scaled[c] * joints[c][0] for c in range(2))
+    above_scaled = tuple(first_middle[c] * joints[c][5] for c in range(2))
+    middle_sum = side_sum(middle, first_middle)
+
+    def below_layer(k, carry):
+        total, correction = carry
+        added = side_sum(k, tuple(weight[c, k] * below_scaled[c] for c in range(2)))
+        total = tuple(total[c] + weight[c, k] * added[c] for c in range(2))
+        return total, tuple(correction[c] + total[c] * gain[c, k] for c in range(2))
+
+    def above_layer(k, carry):
+        total, scaled = carry
+        scaled = tuple(scaled[c] + source[c] * gain[c, k] for c in range(2))
+        added = side_sum(k, tuple(weight[c, k] * scaled[c] for c in range(2)))
+        return tuple(total[c] + weight[c, k] * added[c] for c in range(2)), scaled
+
+    def adjoint_layers(step, carry):
         below, above = carry
-        low, high = middle - 1 - step, middle + 1 + step
-        below = tuple(ratio[c, low] * below[c] for c in range(2))
-        above = tuple(rhs[c, high] + ratio[c, high] * above[c] for c in range(2))
-        for k, value in ((low, below), (high, above)):
-            total = side_sum(k, value)
-            for c in range(2):
-                rhs[c, k] = total[c] * inverse[c, k]
-        return below, above
-
-    middle_sum = side_sum(middle, first_middle)
-    below, above = repeat(plan, layers - 1 - middle, first_outward, (first_middle, first_middle))
-    for k in range(2 * middle - layers, -1, -1):
-        below = tuple(ratio[c, k] * below[c] for c in range(2))
-        total = side_sum(k, below)
-        for c in range(2):
-            rhs[c, k] = total[c] * inverse[c, k]
-    for c in range(2):
-        rhs[c, layers - 1] = rhs[c, layers - 1] + source[c] * inverse[c, layers - 1]
-
-    def second_inward(step, carry):
-        below, above = carry
-        low, high = step + 1, layers - 2 - step
-        below = tuple(rhs[c, low] + (coupling_of(low - 1) * inverse[c, low]) * below[c] for c in range(2))
-        above = tuple(rhs[c, high] + (coupling_of(high) * inverse[c, high]) * above[c] for c in range(2))
-        for c in range(2):
-            rhs[c, low] = below[c]
-        return below, above
-
+        return below_layer(step, below), above_layer(middle + 1 + step, above)
+
+    nothing = (zero, zero)
     below, above = repeat(
-        plan,
-        layers - 2 - middle,
-        second_inward,
-        (tuple(rhs[c, 0] for c in range(2)), tuple(rhs[c, layers - 1] for c in range(2))),
+        plan, layers - 1 - middle, adjoint_layers, ((nothing, nothing), (tuple(source), above_scaled))
     )
     for k in range(layers - 1 - middle, middle):
-        below = tuple(rhs[c, k] + (coupling_of(k - 1) * inverse[c, k]) * below[c] for c in range(2))
-        for c in range(2):
-            rhs[c, k] = below[c]
+        below = below_layer(k, below)
     adjoint = tuple(
-        (middle_sum[c] + (coupling_of(middle - 1) * below[c] + coupling_of(middle) * above[c])) * inverse[c, middle]
-        for c in range(2)
+        join(joints[c], middle_sum[c], below[0][c], above[0][c]) * joints[c][4] + below[1][c] for c in range(2)
     )
-
-    def second_outward(step, nearer):
-        k = middle - 1 - step
-        return tuple(rhs[c, k] + ratio[c, k] * nearer[c] for c in range(2))
-
-    adjoint = repeat(plan, middle, second_outward, adjoint)
     adjoint = [jnp.where(ice, adjoint[c], 0.0) for c in range(2)]
     gradient = -friction * (base[0] * adjoint[0] + base[1] * adjoint[1])
 

time: 28.9 us -> 28.8 us (level)
  no operation moved by 1% of the time
where the time goes in v17:
time: 28.8 us; the launch traced here: 28.5 us
  blocking collectives  24.8 us (86%)
  Pallas kernels  3.11 us (11%)
  between operations  0.64 us (2%)
    all_to_all x2, blocking collectives, exchange(): lax.all_to_all(shaped, ('map', 'layer'), split_axis=0, concat_axis=0, til...  24.8 us
    pallas_call x1, Pallas kernels, on_device(): pl.pallas_call(functools.partial(pack_kernel, plan), out_shape=jax.ShapeD...  1.23 us
    pallas_call x1, Pallas kernels, on_device(): pl.pallas_call(functools.partial(solve_kernel, plan), out_shape=jax.Shape...  1.01 us
    pallas_call x1, Pallas kernels, on_device(): pl.pallas_call(functools.partial(unpack_kernel, plan), out_shape=(jax.Sha...  0.86 us

profile of v17, /device:TPU:0, one launch (start us, length us, event | category | flops | bytes accessed | tf_op | source)
XLA Modules:
  0.0 28.5 jit_solution(2080845373554152801)
XLA Ops:
  0.6 1.2 %pack.1 = f32[288,128]{1,0:T(8,128)S(1)} custom-call(f32[128,128]{1,0:T(8,128)} %bitcast.50, f32[8,128]{1,0:T(8,128)} %bitcast.51, f32[8,128]{1,0:T(8,128)} %bitcast.52, f32[4,128]{1,0:T(4,128)} %bitcast.48, s32[4,128]{1,0:T(4,128)} %bitcast.53), custom_call_target="tpu_custom_call" | custom-call | tf_op jit(solution)/shard_map/pack/pallas_call | solution.py:571
  1.9 15.3 %all_to_all.10 = f32[288,1,128]{2,1,0:T(1,128)S(1)} all-to-all(f32[288,1,128]{2,1,0:T(1,128)S(1)} %bitcast.45), channel_id=1, replica_groups={{31,27,23,19,15,11,7,3,30,26,22,18,14,10,6,2,29,25,21,17,13,9,5,1,28,24..., dimensions={0} | all-to-all | bytes 294912 | tf_op jit(solution)/shard_map/all_to_all | solution.py:567
  17.2 1.0 %solve.1 = f32[160,128]{1,0:T(8,128)S(1)} custom-call(f32[288,128]{1,0:T(8,128)S(1)} %bitcast.44), custom_call_target="tpu_custom_call" | custom-call | tf_op jit(solution)/shard_map/solve/pallas_call | solution.py:587
  18.2 0.0 copy-start
  18.2 9.5 %all_to_all.11 = f32[160,1,128]{2,1,0:T(1,128)S(1)} all-to-all(f32[160,1,128]{2,1,0:T(1,128)S(1)} %bitcast.46), channel_id=1, replica_groups={{31,27,23,19,15,11,7,3,30,26,22,18,14,10,6,2,29,25,21,17,13,9,5,1,28,24..., dimensions={0} | all-to-all | bytes 163840 | tf_op jit(solution)/shard_map/all_to_all | solution.py:567
  27.7 0.0 copy-done
  27.7 0.9 %unpack.1 = (f32[2,64,128]{2,1,0:T(8,128)}, f32[4,128]{1,0:T(4,128)}, f32[1,1]{1,0:T(1,128)}) custom-call(f32[160,128]{1,0:T(8,128)S(1)} %bitcast.47, f32[4,128]{1,0:T(4,128)S(1)} %bitcast.49), custom_call_target="tpu_custom_call" | custom-call | tf_op jit(solution)/shard_map/unpack/pallas_call | solution.py:608
Async XLA Ops:
  18.2 9.5 %copy-start = (f32[2,256]{1,0:T(2,128)S(1)}, f32[2,256]{1,0:T(2,128)}, u32[]{:S(2)}) copy-start(f32[2,256]{1,0:T(2,128)} %param.8) | copy-start | bytes 6148

commit v18 on v17

--- a/solution.py
+++ b/solution.py
@@ -223,12 +223,6 @@
     def arrived(part, row):
         return in_ref[block_row(part, plan.in_rows, row), :]
 
-    def over_parts(row):
-        total = arrived(0, row)
-        for part in range(1, plan.layer_size):
-            total = total + arrived(part, row)
-        return total
-
     def moved(value, source, target):
         return lane_roll(value, target - source)
 
@@ -261,12 +255,15 @@
     def viscosity(rate):
         return jnp.exp2(jnp.log(strain_floor + rate) * (-1.0 / (3.0 * math.log(2.0))))
 
+    sums = [None] * plan.in_rows
     for part in range(plan.layer_size):
-        for c in range(2):
-            for k in range(here):
-                field[c, part * here + k] = arrived(part, c * here + k)
-    line = over_parts(plan.vel_rows)
-    gaps = [[over_parts(2 * n), over_parts(2 * n + 1)] for n in range(4)]
+        for row in range(plan.in_rows):
+            value = arrived(part, row)
+            if row < plan.vel_rows:
+                field[row // here, part * here + row % here] = value
+            sums[row] = value if part == 0 else sums[row] + value
+    line = sums[plan.vel_rows]
+    gaps = [sums[2 * n : 2 * n + 2] for n in range(4)]
     reached = jnp.logical_and(lane % width >= plan.low, lane % width < plan.gap)
     centre = jnp.logical_and(lane % width >= plan.halo, lane % width < plan.halo + plan.cols)
     driving = [2.0 * driving_of(c, gaps[c]) for c in range(2)]

time: 28.8 us -> 28.8 us (level)
  no operation moved by 1% of the time
where the time goes in v18:
time: 28.8 us; the launch traced here: 28.5 us
  blocking collectives  24.8 us (86%)
  Pallas kernels  3.1 us (11%)
  between operations  0.64 us (2%)
    all_to_all x2, blocking collectives, exchange(): lax.all_to_all(shaped, ('map', 'layer'), split_axis=0, concat_axis=0, til...  24.8 us
    pallas_call x1, Pallas kernels, on_device(): pl.pallas_call(functools.partial(pack_kernel, plan), out_shape=jax.ShapeD...  1.23 us
    pallas_call x1, Pallas kernels, on_device(): pl.pallas_call(functools.partial(solve_kernel, plan), out_shape=jax.Shape...  1.01 us
    pallas_call x1, Pallas kernels, on_device(): pl.pallas_call(functools.partial(unpack_kernel, plan), out_shape=(jax.Sha...  0.86 us

profile of v18, /device:TPU:0, one launch (start us, length us, event | category | flops | bytes accessed | tf_op | source)
XLA Modules:
  0.0 28.5 jit_solution(9338688742761053844)
XLA Ops:
  0.6 1.2 %pack.1 = f32[288,128]{1,0:T(8,128)S(1)} custom-call(f32[128,128]{1,0:T(8,128)} %bitcast.50, f32[8,128]{1,0:T(8,128)} %bitcast.51, f32[8,128]{1,0:T(8,128)} %bitcast.52, f32[4,128]{1,0:T(4,128)} %bitcast.48, s32[4,128]{1,0:T(4,128)} %bitcast.53), custom_call_target="tpu_custom_call" | custom-call | tf_op jit(solution)/shard_map/pack/pallas_call | solution.py:568
  1.9 15.3 %all_to_all.10 = f32[288,1,128]{2,1,0:T(1,128)S(1)} all-to-all(f32[288,1,128]{2,1,0:T(1,128)S(1)} %bitcast.45), channel_id=1, replica_groups={{31,27,23,19,15,11,7,3,30,26,22,18,14,10,6,2,29,25,21,17,13,9,5,1,28,24..., dimensions={0} | all-to-all | bytes 294912 | tf_op jit(solution)/shard_map/all_to_all | solution.py:564
  17.2 1.0 %solve.1 = f32[160,128]{1,0:T(8,128)S(1)} custom-call(f32[288,128]{1,0:T(8,128)S(1)} %bitcast.44), custom_call_target="tpu_custom_call" | custom-call | tf_op jit(solution)/shard_map/solve/pallas_call | solution.py:584
  18.2 0.0 copy-start
  18.2 9.5 %all_to_all.11 = f32[160,1,128]{2,1,0:T(1,128)S(1)} all-to-all(f32[160,1,128]{2,1,0:T(1,128)S(1)} %bitcast.46), channel_id=1, replica_groups={{31,27,23,19,15,11,7,3,30,26,22,18,14,10,6,2,29,25,21,17,13,9,5,1,28,24..., dimensions={0} | all-to-all | bytes 163840 | tf_op jit(solution)/shard_map/all_to_all | solution.py:564
  27.7 0.0 copy-done
  27.7 0.9 %unpack.1 = (f32[2,64,128]{2,1,0:T(8,128)}, f32[4,128]{1,0:T(4,128)}, f32[1,1]{1,0:T(1,128)}) custom-call(f32[160,128]{1,0:T(8,128)S(1)} %bitcast.47, f32[4,128]{1,0:T(4,128)S(1)} %bitcast.49), custom_call_target="tpu_custom_call" | custom-call | tf_op jit(solution)/shard_map/unpack/pallas_call | solution.py:605
Async XLA Ops:
  18.2 9.5 %copy-start = (f32[2,256]{1,0:T(2,128)S(1)}, f32[2,256]{1,0:T(2,128)}, u32[]{:S(2)}) copy-start(f32[2,256]{1,0:T(2,128)} %param.8) | copy-start | bytes 6148

commit v19 on v18

--- a/solution.py
+++ b/solution.py
@@ -12,7 +12,7 @@
 step_size = 0.5
 LANES = 128
 REACH = 5
-BED_REACH = 3
+TOP_REACH = 1
 MIB = 1 << 20
 VELOCITY_COPIES = 4
 
@@ -38,15 +38,15 @@
         self.chunks = self.ny // LANES
         self.column_count = self.rows * self.map_size * self.ny
         self.vel_rows = 2 * self.layers_here
-        self.in_rows = self.vel_rows + 1
+        self.in_rows = self.vel_rows
         self.left_at = self.gap
-        self.right_at = self.gap + self.cols // 2 + 1
+        self.right_at = self.gap + self.cols // 2 + 3
         self.out_rows = self.layers_here + 1
         self.unrolled = self.map_size <= 8
         assert self.width * self.rows == LANES and self.cols * self.per_chunk == LANES
         assert self.low >= 0 and self.wide % 2 == 0 and self.width - self.wide >= self.half
         assert 2 * self.cols <= self.width and self.local_cols % LANES == 0
-        assert self.vel_rows == 8 and self.rows == 2 and 4 * self.cols <= LANES
+        assert self.vel_rows == 8 and self.rows == 2
 
 
 def repeat(plan, count, body, carry=0):
@@ -82,7 +82,6 @@
     lane = lax.broadcasted_iota(jnp.int32, shape, 1)
     sub = lax.broadcasted_iota(jnp.int32, shape, 0)
     in_gap = jnp.logical_not(jnp.logical_and(lane % width >= plan.low, lane % width < plan.gap))
-    no_line = jnp.zeros((1, LANES), jnp.float32)
 
     def slide(part, start, length, place):
         step, offset = start // LANES, start % LANES
@@ -119,7 +118,6 @@
                 at = pl.multiple_of(at, 8)
             at = at + (plan.per_chunk - 1 - t) * plan.in_rows
             out_ref[pl.ds(at, plan.vel_rows), :] = jnp.where(in_gap, 0.0, block)
-            out_ref[pl.ds(at + plan.vel_rows, 1), :] = no_line
         return carry
 
     repeat(plan, plan.chunks, chunk_windows)
@@ -137,19 +135,19 @@
 
     def gap_part(r, step):
         at = step * rows + r
-        observed = jnp.where(sub < 2, whole(observed_ref, at), whole(observed_ref, skip + at))
-        return jnp.where(sub < 4, observed, jnp.where(sub < 6, whole(mask_ref, at), whole(log_ref, at)))
-
-    def driving_part(r, step):
+        driving = jnp.where(sub < 2, whole(driving_ref, at), whole(driving_ref, skip + at))
+        return jnp.where(sub < 4, driving, jnp.where(sub < 6, whole(mask_ref, at), whole(log_ref, at)))
+
+    def observed_part(r, step):
         at = step * rows + r
-        return jnp.where(sub < 2, whole(driving_ref, at), whole(driving_ref, skip + at))
+        return jnp.where(sub < 2, whole(observed_ref, at), whole(observed_ref, skip + at))
 
     def sequence(make):
         return [
             [no_block] + [make(r, step) for step in range(local_chunks)] + [no_block] for r in range(rows)
         ]
 
-    gap_parts, driving_parts = sequence(gap_part), sequence(driving_part)
+    gap_parts, observed_parts = sequence(gap_part), sequence(observed_part)
     own = plan.local_cols // cols
     spill = -(-REACH // cols)
 
@@ -161,35 +159,24 @@
             def in_gaps(step):
                 return gap_parts[r][step + 1]
 
-            def of_driving(step):
-                return driving_parts[r][step + 1]
+            def of_observed(step):
+                return observed_parts[r][step + 1]
 
             at = r * width
             first = slide(in_gaps, start - REACH, half, (at + plan.gap) % LANES)
             second = slide(in_gaps, start - REACH + half, half, (at + plan.gap) % LANES)
-            before = slide(of_driving, start - BED_REACH, BED_REACH, (at + plan.left_at) % LANES)
-            after = slide(of_driving, start + cols, BED_REACH, (at + plan.right_at) % LANES)
+            before = slide(of_observed, start - TOP_REACH, TOP_REACH, (at + plan.left_at) % LANES)
+            after = slide(of_observed, start + cols, TOP_REACH, (at + plan.right_at) % LANES)
             ahead = (lane + (LANES - plan.gap - at)) % LANES
-            of_observed = sub < 4
-            first = jnp.where(jnp.logical_and(of_observed, ahead < BED_REACH), before, first)
-            second = jnp.where(jnp.logical_and(of_observed, ahead >= plan.right_at - plan.gap), after, second)
+            shared = sub < 4
+            first = jnp.where(jnp.logical_and(shared, ahead < TOP_REACH), before, first)
+            second = jnp.where(jnp.logical_and(shared, ahead >= plan.right_at - plan.gap), after, second)
             value = jnp.where(sub % 2 == 0, first, second)
             ahead = (lane + (LANES - plan.gap)) % LANES
             block = value if block is None else jnp.where(ahead >= r * width, value, block)
         at = pl.multiple_of((plan.layer_size - 1 - place) * (own * plan.in_rows), 8) + (own - 1 - q) * plan.in_rows
         here = pl.ds(at, plan.vel_rows)
         out_ref[here, :] = jnp.where(in_gap, block, out_ref[here, :])
-        if not 0 <= q < own:
-            return
-        line = None
-        step, offset = start // LANES, start % LANES
-        for r in range(rows):
-            for c in range(2):
-                row = c * skip + step * rows + r
-                put = (2 * r + c) * cols
-                value = lane_roll(driving_ref[row : row + 1, :], put - offset)
-                line = value if line is None else jnp.where(lane[:1] >= put, value, line)
-        out_ref[pl.ds(at + plan.vel_rows, 1), :] = line
 
     for q in range(own):
         column_block(q)
@@ -205,7 +192,9 @@
             column_block(q)
 
 
-def solve_kernel(plan, in_ref, out_ref, field, eta_ref, side, rhs, faces, weight, gain):
+def solve_kernel(plan, in_ref, observed_hbm, out_ref, observed_ref, arrival, field, eta_ref, side, rhs, faces, weight, gain):
+    copy = pltpu.make_async_copy(observed_hbm, observed_ref, arrival)
+    copy.start()
     size, width, rows = plan.map_size, plan.width, plan.rows
     layers, here = plan.layers, plan.layers_here
     shape = (size, LANES)
@@ -230,17 +219,21 @@
         left, right = (moved(value, plan.gap, plan.low + h * plan.half) for h, value in enumerate(halves))
         return jnp.where(lane % width < plan.low + plan.half, left, right)
 
-    def from_line(c):
+    def own_observed(c):
+        column = lax.axis_index("map") * plan.cols
+        local_chunks = plan.local_cols // LANES
         plane = None
         for r in range(rows):
-            value = moved(line, (2 * r + c) * plan.cols, r * width + plan.halo)
+            row = (c * local_chunks + column // LANES) * rows + r
+            value = observed_ref[pl.ds(row, size, stride=2 * local_chunks * rows), :]
+            value = pltpu.roll(value, (r * width + plan.halo + LANES - column % LANES) % LANES, 1)
             plane = value if plane is None else jnp.where(lane >= r * width, value, plane)
         return plane
 
-    def driving_of(c, halves):
-        left = moved(halves[0], plan.left_at, plan.halo - BED_REACH)
+    def observed_of(c, halves):
+        left = moved(halves[0], plan.left_at, plan.halo - TOP_REACH)
         right = moved(halves[1], plan.right_at, plan.halo + plan.cols)
-        return jnp.where(centre, from_line(c), jnp.where(lane % width < plan.halo, left, right))
+        return jnp.where(centre, own_observed(c), jnp.where(lane % width < plan.halo, left, right))
 
     def x_pair(value, edge):
         after = lane_roll(value, -width)
@@ -259,15 +252,12 @@
     for part in range(plan.layer_size):
         for row in range(plan.in_rows):
             value = arrived(part, row)
-            if row < plan.vel_rows:
-                field[row // here, part * here + row % here] = value
+            field[row // here, part * here + row % here] = value
             sums[row] = value if part == 0 else sums[row] + value
-    line = sums[plan.vel_rows]
     gaps = [sums[2 * n : 2 * n + 2] for n in range(4)]
     reached = jnp.logical_and(lane % width >= plan.low, lane % width < plan.gap)
     centre = jnp.logical_and(lane % width >= plan.halo, lane % width < plan.halo + plan.cols)
-    driving = [2.0 * driving_of(c, gaps[c]) for c in range(2)]
-    observed = [from_gap(gaps[c]) for c in range(2)]
+    driving = [2.0 * from_gap(gaps[c]) for c in range(2)]
     mask = jnp.where(reached, from_gap(gaps[2]), 0.0)
     ice = mask != 0.0
     friction = jnp.where(mask == 1.0, jnp.exp(from_gap(gaps[3])), 0.0)
@@ -405,7 +395,8 @@
 
     repeat(plan, layers, send)
 
-    mismatch = [jnp.where(ice, top[c] - observed[c], 0.0) for c in range(2)]
+    copy.wait()
+    mismatch = [jnp.where(ice, top[c] - observed_of(c, gaps[c]), 0.0) for c in range(2)]
     source = [(2.0 * layers) * mismatch[c] for c in range(2)]
 
     def side_sum(k, value):
@@ -580,13 +571,21 @@
 
     windows = exchange(packed)
 
+    columns = [
+        [m * plan.layer_size + part for m in reversed(range(plan.map_size))] for part in range(plan.layer_size)
+    ]
+    all_observed = lax.all_gather(inputs[2], ("map", "layer"), axis=0, tiled=True, axis_index_groups=columns)
+    all_observed = pltpu.with_memory_space_constraint(all_observed, pltpu.HBM)
+
     plane = (plan.layers, plan.map_size, LANES)
     solved = pl.pallas_call(
         functools.partial(solve_kernel, plan),
         out_shape=jax.ShapeDtypeStruct((plan.devices * plan.out_rows, LANES), f32),
-        in_specs=[vmem],
+        in_specs=[vmem, hbm],
         out_specs=vmem,
         scratch_shapes=[
+            pltpu.VMEM(all_observed.shape, f32),
+            pltpu.SemaphoreType.DMA,
             pltpu.VMEM((2,) + plane, f32),
             pltpu.VMEM(plane, f32),
             pltpu.VMEM((2,) + plane, f32),
@@ -597,7 +596,7 @@
         ],
         compiler_params=limit,
         name="solve",
-    )(windows)
+    )(windows, all_observed)
 
     back = exchange(solved)
 

time: 28.8 us -> 40.3 us (1.40)
  starting transfers between devices: 0 us -> 7.28 us
  blocking collectives: 24.8 us -> 28.1 us
  Pallas kernels: 3.1 us -> 3.91 us
    all_gather x0 -> x1, blocking collectives: none -> 15.7 us  [on_device(): lax.all_gather(inputs[2], ('map', 'layer'), axis=0, tiled=True, axis_inde...]
    all_to_all x2 -> x1, blocking collectives: 24.8 us -> 12.4 us  [exchange(): lax.all_to_all(shaped, ('map', 'layer'), split_axis=0, concat_axis=0, til...]
    all_to_all x0 -> x1, starting transfers between devices: none -> 7.28 us  [exchange(): lax.all_to_all(shaped, ('map', 'layer'), split_axis=0, concat_axis=0, til...]
    pallas_call x1, Pallas kernels: 1.23 us -> 1.85 us  [on_device(): pl.pallas_call(functools.partial(pack_kernel, plan), out_shape=jax.ShapeD...]
  transfers between devices with their start and end apart: 0 -> 1, of which waited for: 0 -> 0; matrix products, arithmetic and copies ran while one was open for 0% -> 0% of each run, Pallas kernels for 0% -> 0%
where the time goes in v19:
time: 40.3 us; the launch traced here: 40 us
  blocking collectives  28.1 us (70%)
  starting transfers between devices  7.28 us (18%)
  Pallas kernels  3.91 us (10%)
  between operations  0.68 us (2%)
    all_gather x1, blocking collectives, on_device(): lax.all_gather(inputs[2], ('map', 'layer'), axis=0, tiled=True, axis_inde...  15.7 us
    all_to_all x1, blocking collectives, exchange(): lax.all_to_all(shaped, ('map', 'layer'), split_axis=0, concat_axis=0, til...  12.4 us
    all_to_all x1, starting transfers between devices, exchange(): lax.all_to_all(shaped, ('map', 'layer'), split_axis=0, concat_axis=0, til...  7.28 us
    pallas_call x1, Pallas kernels, on_device(): pl.pallas_call(functools.partial(pack_kernel, plan), out_shape=jax.ShapeD...  1.85 us
    pallas_call x1, Pallas kernels, on_device(): pl.pallas_call(functools.partial(solve_kernel, plan), out_shape=jax.Shape...  1.19 us
    pallas_call x1, Pallas kernels, on_device(): pl.pallas_call(functools.partial(unpack_kernel, plan), out_shape=(jax.Sha...  0.86 us
  transfers between devices with their start and end apart: 1, of which 0 were waited for; matrix products, arithmetic and copies ran while one was open for 0% of the time, Pallas kernels for 0%

profile of v19, /device:TPU:0, one launch (start us, length us, event | category | flops | bytes accessed | tf_op | source)
XLA Modules:
  0.0 40.0 jit_solution(13906127040473392085)
XLA Ops:
  0.6 1.8 %pack.1 = f32[256,128]{1,0:T(8,128)} custom-call(f32[128,128]{1,0:T(8,128)} %bitcast.49, f32[8,128]{1,0:T(8,128)} %bitcast.52, f32[8,128]{1,0:T(8,128)} %bitcast.50, f32[4,128]{1,0:T(4,128)} %bitcast.47, s32[4,128]{1,0:T(4,128)} %bitcast.53), custom_call_target="tpu_custom_call" | custom-call | tf_op jit(solution)/shard_map/pack/pallas_call | solution.py:559
  2.5 0.0 copy-start.1
  2.5 7.3 %all-to-all-start = ((f32[256,1,128]{2,1,0:T(1,128)}), f32[256,1,128]{2,1,0:T(1,128)S(1)}, u32[]{:S(2)}, u32[]{:S(2)}) async-start(f32[256,1,128]{2,1,0:T(1,128)} %bitcast.16), calls=%async_computation | async-start | bytes 262144 | tf_op jit(solution)/shard_map/all_to_all | solution.py:555
  9.8 0.0 copy-done.1
  9.8 15.7 %all_gather.3.observed_hbm = f32[64,128]{1,0:T(8,128)} all-gather(f32[8,128]{1,0:T(8,128)S(1)} %bitcast.51), channel_id=1, replica_groups={{28,24,20,16,12,8,4,0},{29,25,21,17,13,9,5,1},{30,26,22,18,14,10,6,2},{..., dimensions={0}, use_global_device_ids=true | all-gather | bytes 36864 | tf_op jit(solution)/shard_map/all_gather | solution.py:577
  25.5 0.0 all-to-all-done
  25.5 1.2 %solve.1 = f32[160,128]{1,0:T(8,128)S(1)} custom-call(f32[256,128]{1,0:T(8,128)S(1)} %bitcast.44, f32[64,128]{1,0:T(8,128)} %all_gather.3.observed_hbm), custom_call_target="tpu_custom_call" | custom-call | tf_op jit(solution)/shard_map/solve/pallas_call | solution.py:581
  26.7 0.0 copy-start
  26.7 12.4 %all_to_all.10 = f32[160,1,128]{2,1,0:T(1,128)S(1)} all-to-all(f32[160,1,128]{2,1,0:T(1,128)S(1)} %bitcast.46), channel_id=1, replica_groups={{31,27,23,19,15,11,7,3,30,26,22,18,14,10,6,2,29,25,21,17,13,9,5,1,28,24..., dimensions={0} | all-to-all | bytes 163840 | tf_op jit(solution)/shard_map/all_to_all | solution.py:555
  39.1 0.0 copy-done
  39.1 0.9 %unpack.1 = (f32[2,64,128]{2,1,0:T(8,128)}, f32[4,128]{1,0:T(4,128)}, f32[1,1]{1,0:T(1,128)}) custom-call(f32[160,128]{1,0:T(8,128)S(1)} %bitcast.45, f32[4,128]{1,0:T(4,128)S(1)} %bitcast.48), custom_call_target="tpu_custom_call" | custom-call | tf_op jit(solution)/shard_map/unpack/pallas_call | solution.py:604
Async XLA Ops:
  2.5 7.3 %copy-start.1 = (f32[2,2,256]{2,1,0:T(2,128)S(1)}, f32[2,2,256]{2,1,0:T(2,128)}, u32[]{:S(2)}) copy-start(f32[2,2,256]{2,1,0:T(2,128)} %param.7) | copy-start | bytes 12292
  2.5 23.0 %all-to-all-start = ((f32[256,1,128]{2,1,0:T(1,128)}), f32[256,1,128]{2,1,0:T(1,128)S(1)}, u32[]{:S(2)}, u32[]{:S(2)}) async-start(f32[256,1,128]{2,1,0:T(1,128)} %bitcast.16), calls=%async_computation | async-start | bytes 262144 | tf_op jit(solution)/shard_map/all_to_all | solution.py:555
  26.7 12.5 %copy-start = (f32[2,256]{1,0:T(2,128)S(1)}, f32[2,256]{1,0:T(2,128)}, u32[]{:S(2)}) copy-start(f32[2,256]{1,0:T(2,128)} %param.8) | copy-start | bytes 6148

commit v20 on v18

--- a/solution.py
+++ b/solution.py
@@ -1,5 +1,4 @@
 import functools
-import math
 
 import jax
 import jax.numpy as jnp
@@ -252,8 +251,10 @@
     def y_pair(value):
         return lane_roll(value, -1), lane_roll(value, 1)
 
-    def viscosity(rate):
-        return jnp.exp2(jnp.log(strain_floor + rate) * (-1.0 / (3.0 * math.log(2.0))))
+    unit = 2.0 / 4.0 ** (1.0 / 3.0)
+
+    def viscosity(four_rates):
+        return jnp.exp2(jnp.log2(4.0 * strain_floor + four_rates) * (-1.0 / 3.0))
 
     sums = [None] * plan.in_rows
     for part in range(plan.layer_size):
@@ -266,7 +267,7 @@
     gaps = [sums[2 * n : 2 * n + 2] for n in range(4)]
     reached = jnp.logical_and(lane % width >= plan.low, lane % width < plan.gap)
     centre = jnp.logical_and(lane % width >= plan.halo, lane % width < plan.halo + plan.cols)
-    driving = [2.0 * driving_of(c, gaps[c]) for c in range(2)]
+    driving = [unit * driving_of(c, gaps[c]) for c in range(2)]
     observed = [from_gap(gaps[c]) for c in range(2)]
     mask = jnp.where(reached, from_gap(gaps[2]), 0.0)
     ice = mask != 0.0
@@ -281,10 +282,10 @@
         stretch_x = u_east - u_west
         stretch_y = v_north - v_south
         shear = 0.5 * ((u_north - u_south) + (v_east - v_west))
-        rate = 0.25 * (stretch_x * (stretch_x + stretch_y) + stretch_y * stretch_y + shear * shear)
+        four_rates = stretch_x * (stretch_x + stretch_y) + (stretch_y * stretch_y + shear * shear)
         half_v = 0.5 * v
-        eta = viscosity(rate)
-        eta_edge = viscosity(0.25 * (u * u + half_v * half_v))
+        eta = viscosity(four_rates)
+        eta_edge = viscosity(u * u + half_v * half_v)
         eta_east, eta_west = x_pair(eta, eta_edge)
         eta_north, eta_south = y_pair(eta)
         east, west = eta + eta_east, eta + eta_west
@@ -352,7 +353,7 @@
             stencil(k, keep)
             return carry
 
-        lower = ((2.0 * friction,) * 2, (one, one), (zero, zero))
+        lower = ((unit * friction,) * 2, (one, one), (zero, zero))
         upper = ((zero, zero), (one, one), (zero, zero))
         if plan.unrolled:
             stencil(0, keep)
@@ -406,7 +407,7 @@
     repeat(plan, layers, send)
 
     mismatch = [jnp.where(ice, top[c] - observed[c], 0.0) for c in range(2)]
-    source = [(2.0 * layers) * mismatch[c] for c in range(2)]
+    source = [(unit * layers) * mismatch[c] for c in range(2)]
 
     def side_sum(k, value):
         east, west, north, south = (faces[n, k] for n in range(4))

time: 28.8 us -> 28.8 us (level)
  no operation moved by 1% of the time
where the time goes in v20:
time: 28.8 us; the launch traced here: 28.5 us
  blocking collectives  24.8 us (86%)
  Pallas kernels  3.1 us (11%)
  between operations  0.64 us (2%)
    all_to_all x2, blocking collectives, exchange(): lax.all_to_all(shaped, ('map', 'layer'), split_axis=0, concat_axis=0, til...  24.8 us
    pallas_call x1, Pallas kernels, on_device(): pl.pallas_call(functools.partial(pack_kernel, plan), out_shape=jax.ShapeD...  1.23 us
    pallas_call x1, Pallas kernels, on_device(): pl.pallas_call(functools.partial(solve_kernel, plan), out_shape=jax.Shape...  1.01 us
    pallas_call x1, Pallas kernels, on_device(): pl.pallas_call(functools.partial(unpack_kernel, plan), out_shape=(jax.Sha...  0.86 us

profile of v20, /device:TPU:0, one launch (start us, length us, event | category | flops | bytes accessed | tf_op | source)
XLA Modules:
  0.0 28.5 jit_solution(17513124645890512153)
XLA Ops:
  0.6 1.2 %pack.1 = f32[288,128]{1,0:T(8,128)S(1)} custom-call(f32[128,128]{1,0:T(8,128)} %bitcast.50, f32[8,128]{1,0:T(8,128)} %bitcast.51, f32[8,128]{1,0:T(8,128)} %bitcast.52, f32[4,128]{1,0:T(4,128)} %bitcast.48, s32[4,128]{1,0:T(4,128)} %bitcast.53), custom_call_target="tpu_custom_call" | custom-call | tf_op jit(solution)/shard_map/pack/pallas_call | solution.py:569
  1.9 15.3 %all_to_all.10 = f32[288,1,128]{2,1,0:T(1,128)S(1)} all-to-all(f32[288,1,128]{2,1,0:T(1,128)S(1)} %bitcast.45), channel_id=1, replica_groups={{31,27,23,19,15,11,7,3,30,26,22,18,14,10,6,2,29,25,21,17,13,9,5,1,28,24..., dimensions={0} | all-to-all | bytes 294912 | tf_op jit(solution)/shard_map/all_to_all | solution.py:565
  17.2 1.0 %solve.1 = f32[160,128]{1,0:T(8,128)S(1)} custom-call(f32[288,128]{1,0:T(8,128)S(1)} %bitcast.44), custom_call_target="tpu_custom_call" | custom-call | tf_op jit(solution)/shard_map/solve/pallas_call | solution.py:585
  18.2 0.0 copy-start
  18.2 9.5 %all_to_all.11 = f32[160,1,128]{2,1,0:T(1,128)S(1)} all-to-all(f32[160,1,128]{2,1,0:T(1,128)S(1)} %bitcast.46), channel_id=1, replica_groups={{31,27,23,19,15,11,7,3,30,26,22,18,14,10,6,2,29,25,21,17,13,9,5,1,28,24..., dimensions={0} | all-to-all | bytes 163840 | tf_op jit(solution)/shard_map/all_to_all | solution.py:565
  27.7 0.0 copy-done
  27.7 0.9 %unpack.1 = (f32[2,64,128]{2,1,0:T(8,128)}, f32[4,128]{1,0:T(4,128)}, f32[1,1]{1,0:T(1,128)}) custom-call(f32[160,128]{1,0:T(8,128)S(1)} %bitcast.47, f32[4,128]{1,0:T(4,128)S(1)} %bitcast.49), custom_call_target="tpu_custom_call" | custom-call | tf_op jit(solution)/shard_map/unpack/pallas_call | solution.py:606
Async XLA Ops:
  18.2 9.5 %copy-start = (f32[2,256]{1,0:T(2,128)S(1)}, f32[2,256]{1,0:T(2,128)}, u32[]{:S(2)}) copy-start(f32[2,256]{1,0:T(2,128)} %param.8) | copy-start | bytes 6148

commit v21 on v20

--- a/solution.py
+++ b/solution.py
@@ -98,12 +98,8 @@
         def velocity(r):
             def part(step):
                 chunk = i + step
-                if isinstance(chunk, int) and not 0 <= chunk < plan.chunks:
-                    return jnp.zeros(shape, jnp.float32)
-                at = chunk if isinstance(chunk, int) else jnp.clip(chunk, 0, plan.chunks - 1)
+                at = jnp.clip(chunk, 0, plan.chunks - 1)
                 value = vel_ref[pl.ds(at * rows + r, plan.vel_rows, stride=plan.chunks * rows), :]
-                if isinstance(chunk, int):
-                    return value
                 return jnp.where(jnp.logical_and(chunk >= 0, chunk < plan.chunks), value, 0.0)
 
             return part
@@ -114,14 +110,12 @@
                 value = slide(velocity(r), plan.cols * t - plan.halo, width, r * width)
                 block = value if block is None else jnp.where(lane >= r * width, value, block)
             at = (plan.chunks - 1 - i) * plan.per_chunk * plan.in_rows
-            if not isinstance(at, int):
-                at = pl.multiple_of(at, 8)
-            at = at + (plan.per_chunk - 1 - t) * plan.in_rows
+            at = pl.multiple_of(at, 4) + (plan.per_chunk - 1 - t) * plan.in_rows
             out_ref[pl.ds(at, plan.vel_rows), :] = jnp.where(in_gap, 0.0, block)
             out_ref[pl.ds(at + plan.vel_rows, 1), :] = no_line
         return carry
 
-    repeat(plan, plan.chunks, chunk_windows)
+    lax.fori_loop(0, plan.chunks, chunk_windows, 0, unroll=2)
     for copy in copies[VELOCITY_COPIES:]:
         copy.wait()
 

time: 28.8 us -> 29 us (level)
  no operation moved by 1% of the time
where the time goes in v21:
time: 29 us; the launch traced here: 28.8 us
  blocking collectives  24.8 us (86%)
  Pallas kernels  3.33 us (11%)
  between operations  0.64 us (2%)
    all_to_all x2, blocking collectives, exchange(): lax.all_to_all(shaped, ('map', 'layer'), split_axis=0, concat_axis=0, til...  24.8 us
    pallas_call x1, Pallas kernels, on_device(): pl.pallas_call(functools.partial(pack_kernel, plan), out_shape=jax.ShapeD...  1.46 us
    pallas_call x1, Pallas kernels, on_device(): pl.pallas_call(functools.partial(solve_kernel, plan), out_shape=jax.Shape...  1.01 us
    pallas_call x1, Pallas kernels, on_device(): pl.pallas_call(functools.partial(unpack_kernel, plan), out_shape=(jax.Sha...  0.86 us

profile of v21, /device:TPU:0, one launch (start us, length us, event | category | flops | bytes accessed | tf_op | source)
XLA Modules:
  0.0 28.8 jit_solution(17967865571790787742)
XLA Ops:
  0.6 1.5 %pack.1 = f32[288,128]{1,0:T(8,128)S(1)} custom-call(f32[128,128]{1,0:T(8,128)} %bitcast.50, f32[8,128]{1,0:T(8,128)} %bitcast.51, f32[8,128]{1,0:T(8,128)} %bitcast.52, f32[4,128]{1,0:T(4,128)} %bitcast.48, s32[4,128]{1,0:T(4,128)} %bitcast.53), custom_call_target="tpu_custom_call" | custom-call | tf_op jit(solution)/shard_map/pack/pallas_call | solution.py:563
  2.1 15.3 %all_to_all.10 = f32[288,1,128]{2,1,0:T(1,128)S(1)} all-to-all(f32[288,1,128]{2,1,0:T(1,128)S(1)} %bitcast.45), channel_id=1, replica_groups={{31,27,23,19,15,11,7,3,30,26,22,18,14,10,6,2,29,25,21,17,13,9,5,1,28,24..., dimensions={0} | all-to-all | bytes 294912 | tf_op jit(solution)/shard_map/all_to_all | solution.py:559
  17.4 1.0 %solve.1 = f32[160,128]{1,0:T(8,128)S(1)} custom-call(f32[288,128]{1,0:T(8,128)S(1)} %bitcast.44), custom_call_target="tpu_custom_call" | custom-call | tf_op jit(solution)/shard_map/solve/pallas_call | solution.py:579
  18.4 0.0 copy-start
  18.4 9.5 %all_to_all.11 = f32[160,1,128]{2,1,0:T(1,128)S(1)} all-to-all(f32[160,1,128]{2,1,0:T(1,128)S(1)} %bitcast.46), channel_id=1, replica_groups={{31,27,23,19,15,11,7,3,30,26,22,18,14,10,6,2,29,25,21,17,13,9,5,1,28,24..., dimensions={0} | all-to-all | bytes 163840 | tf_op jit(solution)/shard_map/all_to_all | solution.py:559
  27.9 0.0 copy-done
  27.9 0.9 %unpack.1 = (f32[2,64,128]{2,1,0:T(8,128)}, f32[4,128]{1,0:T(4,128)}, f32[1,1]{1,0:T(1,128)}) custom-call(f32[160,128]{1,0:T(8,128)S(1)} %bitcast.47, f32[4,128]{1,0:T(4,128)S(1)} %bitcast.49), custom_call_target="tpu_custom_call" | custom-call | tf_op jit(solution)/shard_map/unpack/pallas_call | solution.py:600
Async XLA Ops:
  18.4 9.5 %copy-start = (f32[2,256]{1,0:T(2,128)S(1)}, f32[2,256]{1,0:T(2,128)}, u32[]{:S(2)}) copy-start(f32[2,256]{1,0:T(2,128)} %param.8) | copy-start | bytes 6148

commit v22 on v20

--- a/solution.py
+++ b/solution.py
@@ -75,8 +75,8 @@
         (mask_hbm, mask_ref),
     ]
     copies = [pltpu.make_async_copy(pair[0], pair[1], arrival.at[n]) for n, pair in enumerate(pairs)]
-    for copy in copies:
-        copy.start()
+    for n, copy in enumerate(copies):
+        copy.start(priority=1 if n >= VELOCITY_COPIES else n % 2)
     shape = (plan.vel_rows, LANES)
     lane = lax.broadcasted_iota(jnp.int32, shape, 1)
     sub = lax.broadcasted_iota(jnp.int32, shape, 0)
@@ -528,11 +528,11 @@
             return carry
 
         repeat(plan, plan.chunks, chunk_body)
-        out[c].start()
+        out[c].start(priority=c)
     friction_ref[...] = log_ref[...] - grad_ref[lax.axis_index("layer")] * scale
-    out[2].start()
+    out[2].start(priority=1)
     misfit_ref[...] = 0.5 * misfit_sum / plan.column_count
-    out[3].start()
+    out[3].start(priority=1)
     for copy in out:
         copy.wait()
 

time: 28.8 us -> 28.8 us (level)
  no operation moved by 1% of the time
where the time goes in v22:
time: 28.8 us; the launch traced here: 28.5 us
  blocking collectives  24.8 us (86%)
  Pallas kernels  3.1 us (11%)
  between operations  0.64 us (2%)
    all_to_all x2, blocking collectives, exchange(): lax.all_to_all(shaped, ('map', 'layer'), split_axis=0, concat_axis=0, til...  24.8 us
    pallas_call x1, Pallas kernels, on_device(): pl.pallas_call(functools.partial(pack_kernel, plan), out_shape=jax.ShapeD...  1.23 us
    pallas_call x1, Pallas kernels, on_device(): pl.pallas_call(functools.partial(solve_kernel, plan), out_shape=jax.Shape...  1.01 us
    pallas_call x1, Pallas kernels, on_device(): pl.pallas_call(functools.partial(unpack_kernel, plan), out_shape=(jax.Sha...  0.86 us

profile of v22, /device:TPU:0, one launch (start us, length us, event | category | flops | bytes accessed | tf_op | source)
XLA Modules:
  0.0 28.5 jit_solution(16304785050225432972)
XLA Ops:
  0.6 1.2 %pack.1 = f32[288,128]{1,0:T(8,128)S(1)} custom-call(f32[128,128]{1,0:T(8,128)} %bitcast.50, f32[8,128]{1,0:T(8,128)} %bitcast.51, f32[8,128]{1,0:T(8,128)} %bitcast.52, f32[4,128]{1,0:T(4,128)} %bitcast.48, s32[4,128]{1,0:T(4,128)} %bitcast.53), custom_call_target="tpu_custom_call" | custom-call | tf_op jit(solution)/shard_map/pack/pallas_call | solution.py:569
  1.9 15.3 %all_to_all.10 = f32[288,1,128]{2,1,0:T(1,128)S(1)} all-to-all(f32[288,1,128]{2,1,0:T(1,128)S(1)} %bitcast.45), channel_id=1, replica_groups={{31,27,23,19,15,11,7,3,30,26,22,18,14,10,6,2,29,25,21,17,13,9,5,1,28,24..., dimensions={0} | all-to-all | bytes 294912 | tf_op jit(solution)/shard_map/all_to_all | solution.py:565
  17.2 1.0 %solve.1 = f32[160,128]{1,0:T(8,128)S(1)} custom-call(f32[288,128]{1,0:T(8,128)S(1)} %bitcast.44), custom_call_target="tpu_custom_call" | custom-call | tf_op jit(solution)/shard_map/solve/pallas_call | solution.py:585
  18.2 0.0 copy-start
  18.2 9.5 %all_to_all.11 = f32[160,1,128]{2,1,0:T(1,128)S(1)} all-to-all(f32[160,1,128]{2,1,0:T(1,128)S(1)} %bitcast.46), channel_id=1, replica_groups={{31,27,23,19,15,11,7,3,30,26,22,18,14,10,6,2,29,25,21,17,13,9,5,1,28,24..., dimensions={0} | all-to-all | bytes 163840 | tf_op jit(solution)/shard_map/all_to_all | solution.py:565
  27.7 0.0 copy-done
  27.7 0.9 %unpack.1 = (f32[2,64,128]{2,1,0:T(8,128)}, f32[4,128]{1,0:T(4,128)}, f32[1,1]{1,0:T(1,128)}) custom-call(f32[160,128]{1,0:T(8,128)S(1)} %bitcast.47, f32[4,128]{1,0:T(4,128)S(1)} %bitcast.49), custom_call_target="tpu_custom_call" | custom-call | tf_op jit(solution)/shard_map/unpack/pallas_call | solution.py:606
Async XLA Ops:
  18.2 9.5 %copy-start = (f32[2,256]{1,0:T(2,128)S(1)}, f32[2,256]{1,0:T(2,128)}, u32[]{:S(2)}) copy-start(f32[2,256]{1,0:T(2,128)} %param.8) | copy-start | bytes 6148

commit v23 on v21

--- a/solution.py
+++ b/solution.py
@@ -68,12 +68,12 @@
     width, rows, cols, half = plan.width, plan.rows, plan.cols, plan.half
     piece = vel_ref.shape[0] // VELOCITY_COPIES
     spans = [pl.ds(n * piece, piece) for n in range(VELOCITY_COPIES)]
-    pairs = [(vel_hbm.at[span, :], vel_ref.at[span, :]) for span in spans] + [
+    pairs = [
         (driving_hbm, driving_ref),
         (observed_hbm, observed_ref),
         (log_hbm, log_ref),
         (mask_hbm, mask_ref),
-    ]
+    ] + [(vel_hbm.at[span, :], vel_ref.at[span, :]) for span in spans]
     copies = [pltpu.make_async_copy(pair[0], pair[1], arrival.at[n]) for n, pair in enumerate(pairs)]
     for copy in copies:
         copy.start()
@@ -81,7 +81,6 @@
     lane = lax.broadcasted_iota(jnp.int32, shape, 1)
     sub = lax.broadcasted_iota(jnp.int32, shape, 0)
     in_gap = jnp.logical_not(jnp.logical_and(lane % width >= plan.low, lane % width < plan.gap))
-    no_line = jnp.zeros((1, LANES), jnp.float32)
 
     def slide(part, start, length, place):
         step, offset = start // LANES, start % LANES
@@ -91,32 +90,8 @@
             value = jnp.where(lax.broadcasted_iota(jnp.int32, value.shape, 1) >= offset, value, after)
         return lane_roll(value, place - offset)
 
-    for copy in copies[:VELOCITY_COPIES]:
-        copy.wait()
-
-    def chunk_windows(i, carry):
-        def velocity(r):
-            def part(step):
-                chunk = i + step
-                at = jnp.clip(chunk, 0, plan.chunks - 1)
-                value = vel_ref[pl.ds(at * rows + r, plan.vel_rows, stride=plan.chunks * rows), :]
-                return jnp.where(jnp.logical_and(chunk >= 0, chunk < plan.chunks), value, 0.0)
-
-            return part
-
-        for t in range(plan.per_chunk):
-            block = None
-            for r in range(rows):
-                value = slide(velocity(r), plan.cols * t - plan.halo, width, r * width)
-                block = value if block is None else jnp.where(lane >= r * width, value, block)
-            at = (plan.chunks - 1 - i) * plan.per_chunk * plan.in_rows
-            at = pl.multiple_of(at, 4) + (plan.per_chunk - 1 - t) * plan.in_rows
-            out_ref[pl.ds(at, plan.vel_rows), :] = jnp.where(in_gap, 0.0, block)
-            out_ref[pl.ds(at + plan.vel_rows, 1), :] = no_line
-        return carry
-
-    lax.fori_loop(0, plan.chunks, chunk_windows, 0, unroll=2)
-    for copy in copies[VELOCITY_COPIES:]:
+    out_ref[...] = jnp.zeros_like(out_ref)
+    for copy in copies[:-VELOCITY_COPIES]:
         copy.wait()
 
     place = lax.axis_index("layer")
@@ -171,7 +146,7 @@
             block = value if block is None else jnp.where(ahead >= r * width, value, block)
         at = pl.multiple_of((plan.layer_size - 1 - place) * (own * plan.in_rows), 8) + (own - 1 - q) * plan.in_rows
         here = pl.ds(at, plan.vel_rows)
-        out_ref[here, :] = jnp.where(in_gap, block, out_ref[here, :])
+        out_ref[here, :] = block
         if not 0 <= q < own:
             return
         line = None
@@ -196,6 +171,38 @@
     def _():
         for q in range(own, own + spill):
             column_block(q)
+
+    for copy in copies[-VELOCITY_COPIES:]:
+        copy.wait()
+
+    def chunk_windows(i, carry):
+        def velocity(r):
+            def part(step):
+                chunk = i + step
+                if isinstance(chunk, int) and not 0 <= chunk < plan.chunks:
+                    return jnp.zeros(shape, jnp.float32)
+                at = chunk if isinstance(chunk, int) else jnp.clip(chunk, 0, plan.chunks - 1)
+                value = vel_ref[pl.ds(at * rows + r, plan.vel_rows, stride=plan.chunks * rows), :]
+                if isinstance(chunk, int):
+                    return value
+                return jnp.where(jnp.logical_and(chunk >= 0, chunk < plan.chunks), value, 0.0)
+
+            return part
+
+        for t in range(plan.per_chunk):
+            block = None
+            for r in range(rows):
+                value = slide(velocity(r), plan.cols * t - plan.halo, width, r * width)
+                block = value if block is None else jnp.where(lane >= r * width, value, block)
+            at = (plan.chunks - 1 - i) * plan.per_chunk * plan.in_rows
+            if not isinstance(at, int):
+                at = pl.multiple_of(at, 8)
+            at = at + (plan.per_chunk - 1 - t) * plan.in_rows
+            here = pl.ds(at, plan.vel_rows)
+            out_ref[here, :] = jnp.where(in_gap, out_ref[here, :], block)
+        return carry
+
+    repeat(plan, plan.chunks, chunk_windows)
 
 
 def solve_kernel(plan, in_ref, out_ref, field, eta_ref, side, rhs, faces, weight, gain):

time: 29 us -> 28.7 us (0.990)
  no operation moved by 1% of the time
where the time goes in v23:
time: 28.7 us; the launch traced here: 28.5 us
  blocking collectives  24.8 us (86%)
  Pallas kernels  3.05 us (11%)
  between operations  0.64 us (2%)
    all_to_all x2, blocking collectives, exchange(): lax.all_to_all(shaped, ('map', 'layer'), split_axis=0, concat_axis=0, til...  24.8 us
    pallas_call x1, Pallas kernels, on_device(): pl.pallas_call(functools.partial(pack_kernel, plan), out_shape=jax.ShapeD...  1.18 us
    pallas_call x1, Pallas kernels, on_device(): pl.pallas_call(functools.partial(solve_kernel, plan), out_shape=jax.Shape...  1.01 us
    pallas_call x1, Pallas kernels, on_device(): pl.pallas_call(functools.partial(unpack_kernel, plan), out_shape=(jax.Sha...  0.86 us

profile of v23, /device:TPU:0, one launch (start us, length us, event | category | flops | bytes accessed | tf_op | source)
XLA Modules:
  0.0 28.5 jit_solution(8354157911616338022)
XLA Ops:
  0.6 1.2 %pack.1 = f32[288,128]{1,0:T(8,128)S(1)} custom-call(f32[128,128]{1,0:T(8,128)} %bitcast.50, f32[8,128]{1,0:T(8,128)} %bitcast.51, f32[8,128]{1,0:T(8,128)} %bitcast.52, f32[4,128]{1,0:T(4,128)} %bitcast.48, s32[4,128]{1,0:T(4,128)} %bitcast.53), custom_call_target="tpu_custom_call" | custom-call | tf_op jit(solution)/shard_map/pack/pallas_call | solution.py:570
  1.8 15.3 %all_to_all.10 = f32[288,1,128]{2,1,0:T(1,128)S(1)} all-to-all(f32[288,1,128]{2,1,0:T(1,128)S(1)} %bitcast.45), channel_id=1, replica_groups={{31,27,23,19,15,11,7,3,30,26,22,18,14,10,6,2,29,25,21,17,13,9,5,1,28,24..., dimensions={0} | all-to-all | bytes 294912 | tf_op jit(solution)/shard_map/all_to_all | solution.py:566
  17.1 1.0 %solve.1 = f32[160,128]{1,0:T(8,128)S(1)} custom-call(f32[288,128]{1,0:T(8,128)S(1)} %bitcast.44), custom_call_target="tpu_custom_call" | custom-call | tf_op jit(solution)/shard_map/solve/pallas_call | solution.py:586
  18.1 0.0 copy-start
  18.1 9.5 %all_to_all.11 = f32[160,1,128]{2,1,0:T(1,128)S(1)} all-to-all(f32[160,1,128]{2,1,0:T(1,128)S(1)} %bitcast.46), channel_id=1, replica_groups={{31,27,23,19,15,11,7,3,30,26,22,18,14,10,6,2,29,25,21,17,13,9,5,1,28,24..., dimensions={0} | all-to-all | bytes 163840 | tf_op jit(solution)/shard_map/all_to_all | solution.py:566
  27.6 0.0 copy-done
  27.6 0.9 %unpack.1 = (f32[2,64,128]{2,1,0:T(8,128)}, f32[4,128]{1,0:T(4,128)}, f32[1,1]{1,0:T(1,128)}) custom-call(f32[160,128]{1,0:T(8,128)S(1)} %bitcast.47, f32[4,128]{1,0:T(4,128)S(1)} %bitcast.49), custom_call_target="tpu_custom_call" | custom-call | tf_op jit(solution)/shard_map/unpack/pallas_call | solution.py:607
Async XLA Ops:
  18.1 9.5 %copy-start = (f32[2,256]{1,0:T(2,128)S(1)}, f32[2,256]{1,0:T(2,128)}, u32[]{:S(2)}) copy-start(f32[2,256]{1,0:T(2,128)} %param.8) | copy-start | bytes 6148

commit v24 on v23

--- a/solution.py
+++ b/solution.py
@@ -175,25 +175,51 @@
     for copy in copies[-VELOCITY_COPIES:]:
         copy.wait()
 
+    kept = {}
+
     def chunk_windows(i, carry):
-        def velocity(r):
-            def part(step):
-                chunk = i + step
-                if isinstance(chunk, int) and not 0 <= chunk < plan.chunks:
-                    return jnp.zeros(shape, jnp.float32)
-                at = chunk if isinstance(chunk, int) else jnp.clip(chunk, 0, plan.chunks - 1)
-                value = vel_ref[pl.ds(at * rows + r, plan.vel_rows, stride=plan.chunks * rows), :]
-                if isinstance(chunk, int):
-                    return value
-                return jnp.where(jnp.logical_and(chunk >= 0, chunk < plan.chunks), value, 0.0)
-
-            return part
+        seen = kept if plan.unrolled else {}
+
+        def once(key, make):
+            if key not in seen:
+                seen[key] = make()
+            return seen[key]
+
+        def read(step, r):
+            chunk = i + step
+            if isinstance(chunk, int) and not 0 <= chunk < plan.chunks:
+                return jnp.zeros(shape, jnp.float32)
+            at = chunk if isinstance(chunk, int) else jnp.clip(chunk, 0, plan.chunks - 1)
+            value = vel_ref[pl.ds(at * rows + r, plan.vel_rows, stride=plan.chunks * rows), :]
+            if isinstance(chunk, int):
+                return value
+            return jnp.where(jnp.logical_and(chunk >= 0, chunk < plan.chunks), value, 0.0)
+
+        def turned(step, r):
+            name = i + step if plan.unrolled else step
+            return once(("turned", name, r), lambda: lane_roll(read(step, r), r * width))
+
+        def moved(step, r):
+            if r == 0:
+                return turned(step, 0)
+            name = i + step if plan.unrolled else step
+            return once(("moved", name, r), lambda: jnp.where(lane >= r * width, turned(step, r), turned(step - 1, r)))
 
         for t in range(plan.per_chunk):
+            start = plan.cols * t - plan.halo
+            step, offset = start // LANES, start % LANES
             block = None
             for r in range(rows):
-                value = slide(velocity(r), plan.cols * t - plan.halo, width, r * width)
-                block = value if block is None else jnp.where(lane >= r * width, value, block)
+                low, high = offset + r * width, offset + (r + 1) * width
+                if high <= LANES:
+                    value = moved(step, r)
+                elif low >= LANES:
+                    value = moved(step + 1, r)
+                else:
+                    value = jnp.where(lane >= offset, moved(step, r), moved(step + 1, r))
+                ahead = (lane + (LANES - offset)) % LANES
+                block = value if block is None else jnp.where(ahead >= r * width, value, block)
+            block = lane_roll(block, -offset)
             at = (plan.chunks - 1 - i) * plan.per_chunk * plan.in_rows
             if not isinstance(at, int):
                 at = pl.multiple_of(at, 8)

time: 28.7 us -> 28.8 us (level)
  no operation moved by 1% of the time
where the time goes in v24:
time: 28.8 us; the launch traced here: 28.5 us
  blocking collectives  24.8 us (86%)
  Pallas kernels  3.09 us (11%)
  between operations  0.64 us (2%)
    all_to_all x2, blocking collectives, exchange(): lax.all_to_all(shaped, ('map', 'layer'), split_axis=0, concat_axis=0, til...  24.8 us
    pallas_call x1, Pallas kernels, on_device(): pl.pallas_call(functools.partial(pack_kernel, plan), out_shape=jax.ShapeD...  1.22 us
    pallas_call x1, Pallas kernels, on_device(): pl.pallas_call(functools.partial(solve_kernel, plan), out_shape=jax.Shape...  1.01 us
    pallas_call x1, Pallas kernels, on_device(): pl.pallas_call(functools.partial(unpack_kernel, plan), out_shape=(jax.Sha...  0.86 us

profile of v24, /device:TPU:0, one launch (start us, length us, event | category | flops | bytes accessed | tf_op | source)
XLA Modules:
  0.0 28.5 jit_solution(643317244027911454)
XLA Ops:
  0.6 1.2 %pack.1 = f32[288,128]{1,0:T(8,128)S(1)} custom-call(f32[128,128]{1,0:T(8,128)} %bitcast.50, f32[8,128]{1,0:T(8,128)} %bitcast.51, f32[8,128]{1,0:T(8,128)} %bitcast.52, f32[4,128]{1,0:T(4,128)} %bitcast.48, s32[4,128]{1,0:T(4,128)} %bitcast.53), custom_call_target="tpu_custom_call" | custom-call | tf_op jit(solution)/shard_map/pack/pallas_call | solution.py:596
  1.9 15.3 %all_to_all.10 = f32[288,1,128]{2,1,0:T(1,128)S(1)} all-to-all(f32[288,1,128]{2,1,0:T(1,128)S(1)} %bitcast.45), channel_id=1, replica_groups={{31,27,23,19,15,11,7,3,30,26,22,18,14,10,6,2,29,25,21,17,13,9,5,1,28,24..., dimensions={0} | all-to-all | bytes 294912 | tf_op jit(solution)/shard_map/all_to_all | solution.py:592
  17.2 1.0 %solve.1 = f32[160,128]{1,0:T(8,128)S(1)} custom-call(f32[288,128]{1,0:T(8,128)S(1)} %bitcast.44), custom_call_target="tpu_custom_call" | custom-call | tf_op jit(solution)/shard_map/solve/pallas_call | solution.py:612
  18.2 0.0 copy-start
  18.2 9.5 %all_to_all.11 = f32[160,1,128]{2,1,0:T(1,128)S(1)} all-to-all(f32[160,1,128]{2,1,0:T(1,128)S(1)} %bitcast.46), channel_id=1, replica_groups={{31,27,23,19,15,11,7,3,30,26,22,18,14,10,6,2,29,25,21,17,13,9,5,1,28,24..., dimensions={0} | all-to-all | bytes 163840 | tf_op jit(solution)/shard_map/all_to_all | solution.py:592
  27.7 0.0 copy-done
  27.7 0.9 %unpack.1 = (f32[2,64,128]{2,1,0:T(8,128)}, f32[4,128]{1,0:T(4,128)}, f32[1,1]{1,0:T(1,128)}) custom-call(f32[160,128]{1,0:T(8,128)S(1)} %bitcast.47, f32[4,128]{1,0:T(4,128)S(1)} %bitcast.49), custom_call_target="tpu_custom_call" | custom-call | tf_op jit(solution)/shard_map/unpack/pallas_call | solution.py:633
Async XLA Ops:
  18.2 9.5 %copy-start = (f32[2,256]{1,0:T(2,128)S(1)}, f32[2,256]{1,0:T(2,128)}, u32[]{:S(2)}) copy-start(f32[2,256]{1,0:T(2,128)} %param.8) | copy-start | bytes 6148

commit v25 on v23

--- a/solution.py
+++ b/solution.py
@@ -317,17 +317,20 @@
     def advance(k, coupling, carry):
         flux, value, total = carry
         across = reciprocal(coupling)
-        new_flux, new_value, new_total = [], [], []
+        new_flux, new_value, new_total, product = [], [], [], []
         for c in range(2):
             here_flux = flux[c] + side[c, k] * value[c]
             after = value[c] + across * here_flux
             here_total = total[c] + value[c] * rhs[c, k]
             weight[c, k] = value[c]
-            gain[c, k] = reciprocal((coupling * value[c]) * after)
+            product.append((coupling * value[c]) * after)
             rhs[c, k] = here_total
             new_flux.append(here_flux)
             new_value.append(after)
             new_total.append(here_total)
+        both = reciprocal(product[0] * product[1])
+        gain[0, k] = both * product[1]
+        gain[1, k] = both * product[0]
         return tuple(new_flux), tuple(new_value), tuple(new_total)
 
     def lower_step(k, carry):

time: 28.7 us -> 28.7 us (level)
  no operation moved by 1% of the time
where the time goes in v25:
time: 28.7 us; the launch traced here: 28.5 us
  blocking collectives  24.8 us (86%)
  Pallas kernels  3.05 us (11%)
  between operations  0.64 us (2%)
    all_to_all x2, blocking collectives, exchange(): lax.all_to_all(shaped, ('map', 'layer'), split_axis=0, concat_axis=0, til...  24.8 us
    pallas_call x1, Pallas kernels, on_device(): pl.pallas_call(functools.partial(pack_kernel, plan), out_shape=jax.ShapeD...  1.18 us
    pallas_call x1, Pallas kernels, on_device(): pl.pallas_call(functools.partial(solve_kernel, plan), out_shape=jax.Shape...  1 us
    pallas_call x1, Pallas kernels, on_device(): pl.pallas_call(functools.partial(unpack_kernel, plan), out_shape=(jax.Sha...  0.86 us

profile of v25, /device:TPU:0, one launch (start us, length us, event | category | flops | bytes accessed | tf_op | source)
XLA Modules:
  0.0 28.5 jit_solution(8616029066022146232)
XLA Ops:
  0.6 1.2 %pack.1 = f32[288,128]{1,0:T(8,128)S(1)} custom-call(f32[128,128]{1,0:T(8,128)} %bitcast.50, f32[8,128]{1,0:T(8,128)} %bitcast.51, f32[8,128]{1,0:T(8,128)} %bitcast.52, f32[4,128]{1,0:T(4,128)} %bitcast.48, s32[4,128]{1,0:T(4,128)} %bitcast.53), custom_call_target="tpu_custom_call" | custom-call | tf_op jit(solution)/shard_map/pack/pallas_call | solution.py:573
  1.8 15.3 %all_to_all.10 = f32[288,1,128]{2,1,0:T(1,128)S(1)} all-to-all(f32[288,1,128]{2,1,0:T(1,128)S(1)} %bitcast.45), channel_id=1, replica_groups={{31,27,23,19,15,11,7,3,30,26,22,18,14,10,6,2,29,25,21,17,13,9,5,1,28,24..., dimensions={0} | all-to-all | bytes 294912 | tf_op jit(solution)/shard_map/all_to_all | solution.py:569
  17.1 1.0 %solve.1 = f32[160,128]{1,0:T(8,128)S(1)} custom-call(f32[288,128]{1,0:T(8,128)S(1)} %bitcast.44), custom_call_target="tpu_custom_call" | custom-call | tf_op jit(solution)/shard_map/solve/pallas_call | solution.py:589
  18.1 0.0 copy-start
  18.1 9.5 %all_to_all.11 = f32[160,1,128]{2,1,0:T(1,128)S(1)} all-to-all(f32[160,1,128]{2,1,0:T(1,128)S(1)} %bitcast.46), channel_id=1, replica_groups={{31,27,23,19,15,11,7,3,30,26,22,18,14,10,6,2,29,25,21,17,13,9,5,1,28,24..., dimensions={0} | all-to-all | bytes 163840 | tf_op jit(solution)/shard_map/all_to_all | solution.py:569
  27.6 0.0 copy-done
  27.6 0.9 %unpack.1 = (f32[2,64,128]{2,1,0:T(8,128)}, f32[4,128]{1,0:T(4,128)}, f32[1,1]{1,0:T(1,128)}) custom-call(f32[160,128]{1,0:T(8,128)S(1)} %bitcast.47, f32[4,128]{1,0:T(4,128)S(1)} %bitcast.49), custom_call_target="tpu_custom_call" | custom-call | tf_op jit(solution)/shard_map/unpack/pallas_call | solution.py:610
Async XLA Ops:
  18.1 9.5 %copy-start = (f32[2,256]{1,0:T(2,128)S(1)}, f32[2,256]{1,0:T(2,128)}, u32[]{:S(2)}) copy-start(f32[2,256]{1,0:T(2,128)} %param.8) | copy-start | bytes 6148

commit v26 on v25

--- a/solution.py
+++ b/solution.py
@@ -314,9 +314,8 @@
     zero = jnp.zeros(shape, jnp.float32)
     one = jnp.ones(shape, jnp.float32)
 
-    def advance(k, coupling, carry):
+    def advance(k, coupling, across, carry):
         flux, value, total = carry
-        across = reciprocal(coupling)
         new_flux, new_value, new_total, product = [], [], [], []
         for c in range(2):
             here_flux = flux[c] + side[c, k] * value[c]
@@ -334,14 +333,14 @@
         return tuple(new_flux), tuple(new_value), tuple(new_total)
 
     def lower_step(k, carry):
-        return advance(k, coupling_of(k), carry)
-
-    def upper_step(k, carry):
-        return advance(k, coupling_of(k - 1), carry)
+        coupling = coupling_of(k)
+        return advance(k, coupling, reciprocal(coupling), carry)
 
     def fronts(step, carry):
-        lower, upper = carry
-        return lower_step(step, lower), upper_step(layers - 1 - step, upper)
+        low, high = step, layers - 1 - step
+        under, over = coupling_of(low), coupling_of(high - 1)
+        both = reciprocal(under * over)
+        return advance(low, under, both * over, carry[0]), advance(high, over, both * under, carry[1])
 
     def outward(body, carry):
         def both(step, carry):
@@ -377,7 +376,8 @@
             below, above = lower[1][c], upper[1][c]
             product = below * above
             inv = reciprocal(side[c, middle] * product + (lower[0][c] * above + upper[0][c] * below))
-            joint = (below, above, product, inv, reciprocal(below), reciprocal(above))
+            both = reciprocal(product)
+            joint = (below, above, product, inv, both * above, both * below)
             joints.append(joint)
             solved = join(joint, rhs[c, middle], lower[2][c], upper[2][c])
             field[c, middle] = jnp.where(ice, solved, 0.0)

time: 28.7 us -> 28.7 us (level)
  no operation moved by 1% of the time
where the time goes in v26:
time: 28.7 us; the launch traced here: 28.5 us
  blocking collectives  24.8 us (86%)
  Pallas kernels  3.06 us (11%)
  between operations  0.64 us (2%)
    all_to_all x2, blocking collectives, exchange(): lax.all_to_all(shaped, ('map', 'layer'), split_axis=0, concat_axis=0, til...  24.8 us
    pallas_call x1, Pallas kernels, on_device(): pl.pallas_call(functools.partial(pack_kernel, plan), out_shape=jax.ShapeD...  1.18 us
    pallas_call x1, Pallas kernels, on_device(): pl.pallas_call(functools.partial(solve_kernel, plan), out_shape=jax.Shape...  1.01 us
    pallas_call x1, Pallas kernels, on_device(): pl.pallas_call(functools.partial(unpack_kernel, plan), out_shape=(jax.Sha...  0.86 us

profile of v26, /device:TPU:0, one launch (start us, length us, event | category | flops | bytes accessed | tf_op | source)
XLA Modules:
  0.0 28.5 jit_solution(3629142393630254296)
XLA Ops:
  0.6 1.2 %pack.1 = f32[288,128]{1,0:T(8,128)S(1)} custom-call(f32[128,128]{1,0:T(8,128)} %bitcast.50, f32[8,128]{1,0:T(8,128)} %bitcast.51, f32[8,128]{1,0:T(8,128)} %bitcast.52, f32[4,128]{1,0:T(4,128)} %bitcast.48, s32[4,128]{1,0:T(4,128)} %bitcast.53), custom_call_target="tpu_custom_call" | custom-call | tf_op jit(solution)/shard_map/pack/pallas_call | solution.py:573
  1.8 15.3 %all_to_all.10 = f32[288,1,128]{2,1,0:T(1,128)S(1)} all-to-all(f32[288,1,128]{2,1,0:T(1,128)S(1)} %bitcast.45), channel_id=1, replica_groups={{31,27,23,19,15,11,7,3,30,26,22,18,14,10,6,2,29,25,21,17,13,9,5,1,28,24..., dimensions={0} | all-to-all | bytes 294912 | tf_op jit(solution)/shard_map/all_to_all | solution.py:569
  17.1 1.0 %solve.1 = f32[160,128]{1,0:T(8,128)S(1)} custom-call(f32[288,128]{1,0:T(8,128)S(1)} %bitcast.44), custom_call_target="tpu_custom_call" | custom-call | tf_op jit(solution)/shard_map/solve/pallas_call | solution.py:589
  18.2 0.0 copy-start
  18.2 9.5 %all_to_all.11 = f32[160,1,128]{2,1,0:T(1,128)S(1)} all-to-all(f32[160,1,128]{2,1,0:T(1,128)S(1)} %bitcast.46), channel_id=1, replica_groups={{31,27,23,19,15,11,7,3,30,26,22,18,14,10,6,2,29,25,21,17,13,9,5,1,28,24..., dimensions={0} | all-to-all | bytes 163840 | tf_op jit(solution)/shard_map/all_to_all | solution.py:569
  27.6 0.0 copy-done
  27.6 0.9 %unpack.1 = (f32[2,64,128]{2,1,0:T(8,128)}, f32[4,128]{1,0:T(4,128)}, f32[1,1]{1,0:T(1,128)}) custom-call(f32[160,128]{1,0:T(8,128)S(1)} %bitcast.47, f32[4,128]{1,0:T(4,128)S(1)} %bitcast.49), custom_call_target="tpu_custom_call" | custom-call | tf_op jit(solution)/shard_map/unpack/pallas_call | solution.py:610
Async XLA Ops:
  18.2 9.5 %copy-start = (f32[2,256]{1,0:T(2,128)S(1)}, f32[2,256]{1,0:T(2,128)}, u32[]{:S(2)}) copy-start(f32[2,256]{1,0:T(2,128)} %param.8) | copy-start | bytes 6148

commit v27 on v25

--- a/solution.py
+++ b/solution.py
@@ -13,7 +13,7 @@
 REACH = 5
 BED_REACH = 3
 MIB = 1 << 20
-VELOCITY_COPIES = 4
+VELOCITY_COPIES = 2
 
 
 class Plan:

time: 28.7 us -> 28.7 us (level)
  no operation moved by 1% of the time
where the time goes in v27:
time: 28.7 us; the launch traced here: 28.5 us
  blocking collectives  24.8 us (86%)
  Pallas kernels  3.03 us (11%)
  between operations  0.64 us (2%)
    all_to_all x2, blocking collectives, exchange(): lax.all_to_all(shaped, ('map', 'layer'), split_axis=0, concat_axis=0, til...  24.8 us
    pallas_call x1, Pallas kernels, on_device(): pl.pallas_call(functools.partial(pack_kernel, plan), out_shape=jax.ShapeD...  1.16 us
    pallas_call x1, Pallas kernels, on_device(): pl.pallas_call(functools.partial(solve_kernel, plan), out_shape=jax.Shape...  1 us
    pallas_call x1, Pallas kernels, on_device(): pl.pallas_call(functools.partial(unpack_kernel, plan), out_shape=(jax.Sha...  0.86 us

profile of v27, /device:TPU:0, one launch (start us, length us, event | category | flops | bytes accessed | tf_op | source)
XLA Modules:
  0.0 28.5 jit_solution(5736217728996451223)
XLA Ops:
  0.6 1.2 %pack.1 = f32[288,128]{1,0:T(8,128)S(1)} custom-call(f32[128,128]{1,0:T(8,128)} %bitcast.50, f32[8,128]{1,0:T(8,128)} %bitcast.51, f32[8,128]{1,0:T(8,128)} %bitcast.52, f32[4,128]{1,0:T(4,128)} %bitcast.48, s32[4,128]{1,0:T(4,128)} %bitcast.53), custom_call_target="tpu_custom_call" | custom-call | tf_op jit(solution)/shard_map/pack/pallas_call | solution.py:573
  1.8 15.3 %all_to_all.10 = f32[288,1,128]{2,1,0:T(1,128)S(1)} all-to-all(f32[288,1,128]{2,1,0:T(1,128)S(1)} %bitcast.45), channel_id=1, replica_groups={{31,27,23,19,15,11,7,3,30,26,22,18,14,10,6,2,29,25,21,17,13,9,5,1,28,24..., dimensions={0} | all-to-all | bytes 294912 | tf_op jit(solution)/shard_map/all_to_all | solution.py:569
  17.1 1.0 %solve.1 = f32[160,128]{1,0:T(8,128)S(1)} custom-call(f32[288,128]{1,0:T(8,128)S(1)} %bitcast.44), custom_call_target="tpu_custom_call" | custom-call | tf_op jit(solution)/shard_map/solve/pallas_call | solution.py:589
  18.1 0.0 copy-start
  18.1 9.5 %all_to_all.11 = f32[160,1,128]{2,1,0:T(1,128)S(1)} all-to-all(f32[160,1,128]{2,1,0:T(1,128)S(1)} %bitcast.46), channel_id=1, replica_groups={{31,27,23,19,15,11,7,3,30,26,22,18,14,10,6,2,29,25,21,17,13,9,5,1,28,24..., dimensions={0} | all-to-all | bytes 163840 | tf_op jit(solution)/shard_map/all_to_all | solution.py:569
  27.6 0.0 copy-done
  27.6 0.9 %unpack.1 = (f32[2,64,128]{2,1,0:T(8,128)}, f32[4,128]{1,0:T(4,128)}, f32[1,1]{1,0:T(1,128)}) custom-call(f32[160,128]{1,0:T(8,128)S(1)} %bitcast.47, f32[4,128]{1,0:T(4,128)S(1)} %bitcast.49), custom_call_target="tpu_custom_call" | custom-call | tf_op jit(solution)/shard_map/unpack/pallas_call | solution.py:610
Async XLA Ops:
  18.1 9.5 %copy-start = (f32[2,256]{1,0:T(2,128)S(1)}, f32[2,256]{1,0:T(2,128)}, u32[]{:S(2)}) copy-start(f32[2,256]{1,0:T(2,128)} %param.8) | copy-start | bytes 6148
